TPU v7x, 32 devices: a whole 2x2x4 slice. The times are simulated.
32 devices in a mesh: groups: 2 (over x), attn: 16 (over z, y, core).
Axes of the slice: x: 2, y: 2, z: 4, core: 2. Of those that a mesh axis runs over, the one named last changes fastest.
Arguments:
- queries: bfloat16 [512, 3072], P(('groups', 'attn')), parts along dimension 0, may hold values from -6 to 6
- residual: bfloat16 [512, 3072], P(('groups', 'attn')), parts along dimension 0, may hold values from -36 to 36
- key_cache: bfloat16 [512, 96, 512], P(('groups', 'attn')), parts along dimension 0, may hold values from -6 to 6
- value_cache: bfloat16 [512, 96, 512], P(('groups', 'attn')), parts along dimension 0, may hold values from -6 to 6
- new_keys: bfloat16 [512, 512], P(('groups', 'attn')), parts along dimension 0, may hold values from -6 to 6
- new_values: bfloat16 [512, 512], P(('groups', 'attn')), parts along dimension 0, may hold values from -6 to 6
- cache_len: int32 [512], P(('groups', 'attn')), parts along dimension 0, may hold values from 1 to 96, 12288 in all
- norm_gain: float32 [3072], replicated, may hold values from 0.5 to 1.5
- expert_ids: int32 [512, 2], P(('groups', 'attn')), parts along dimension 0, may hold values from 0 to 3, all different within a row; in each aligned block of 8 rows (0 to 7, 8 to 15, ...) at most 6 rows name the same one
- gate_fixed: int32 [512, 2], P(('groups', 'attn')), parts along dimension 0, may hold values from 1 to 4096
- gate_weight: bfloat16 [3072, 32768], P(None, 'attn'), may hold values from -0.109375 to 0.109375
- up_weight: bfloat16 [3072, 32768], P(None, 'attn'), may hold values from -0.109375 to 0.109375
- down_weight: bfloat16 [32768, 3072], P('attn'), may hold values from -0.0625 to 0.0625
Outputs:
- mixed: bfloat16 [512, 3072], P(('groups', 'attn')), parts along dimension 0
There are 2 independent parts, one for each index of `groups`. A program takes and returns all parts, laid end to end along the dimension named above; an argument that names none is the same for every part. Nothing has to cross between parts.
Inputs may be any that keep to these rules, and one draw needn't show every extreme that they name: `cache_len`: slots in use of each sequence. Within each part (each replica's 256 sequences) the lengths sum to 12288, and some sequence of the part uses all 96; the whole array over all parts sums to that total times the number of parts. `expert_ids`: the 2 experts of a token differ. In each aligned block of 8 rows (one device's micro-batch) no expert is named by more than 6 rows, and in every draw some block has an expert named by exactly 6 rows. `gate_fixed`: A routing weight is the value divided by 4096.
All inputs are finite; a program needn't handle non-finite values. No bound on the sum of `cache_len` on one device may be relied on, other than what follows from the above.
Results may differ from a plain program's by a relative error of at most 0.0057.
Values may be sent and summed in bfloat16 or wider, within the bound.
No kernel may reach another device: no remote copies, remote signals or barrier semaphores. Data moves between devices by JAX's collectives and lax.ppermute only.
A program may use at most 128 MiB of HBM per device.

v0:
```python
import math

import jax
import jax.numpy as jnp
from jax import lax
from jax.sharding import PartitionSpec as P

HEAD = 128
Q_HEADS = 24
KV_HEADS = 4
EXPERTS = 4
TOP = 2
MICRO = 2
MB_ROWS = 8
CACHE = 96
CAP = 6


EPS = 1e-05
FIXED_ONE = 4096.0


def attend(queries, residual, key_cache, value_cache, new_keys, new_values, cache_len):
    rows_here = queries.shape[0]
    grouped = Q_HEADS // KV_HEADS
    query_heads = queries.reshape(rows_here, KV_HEADS, grouped, HEAD)
    key_heads = key_cache.reshape(rows_here, CACHE, KV_HEADS, HEAD)
    value_heads = value_cache.reshape(rows_here, CACHE, KV_HEADS, HEAD)
    own_key = new_keys.reshape(rows_here, KV_HEADS, HEAD)
    own_value = new_values.astype(jnp.float32).reshape(rows_here, KV_HEADS, HEAD)
    scaling = 1.0 / math.sqrt(HEAD)
    scores = (
        jnp.einsum("tkgh,tpkh->tkgp", query_heads, key_heads, preferred_element_type=jnp.float32)
        * scaling
    )
    live_mask = jnp.arange(CACHE)[None, :] < cache_len[:, None]
    scores = jnp.where(live_mask[:, None, None, :], scores, -jnp.inf)
    own_score = (
        jnp.einsum("tkgh,tkh->tkg", query_heads, own_key, preferred_element_type=jnp.float32)
        * scaling
    )
    highest = jnp.maximum(jnp.max(scores, axis=-1), own_score)
    exponent = jnp.exp(scores - highest[..., None])
    own_weight = jnp.exp(own_score - highest)
    totals = jnp.sum(exponent, axis=-1) + own_weight
    probabilities = (exponent / totals[..., None]).astype(jnp.bfloat16)
    own_prob = lax.optimization_barrier((own_weight / totals).astype(jnp.bfloat16)).astype(
        jnp.float32
    )
    attended = jnp.einsum(
        "tkgp,tpkh->tkgh", probabilities, value_heads, preferred_element_type=jnp.float32
    )
    attended = attended + own_prob[..., None] * own_value[:, :, None, :]
    attended = attended.reshape(rows_here, Q_HEADS * HEAD)
    return (residual.astype(jnp.float32) + attended).astype(jnp.bfloat16)


def routing(chosen, weights):
    rows_here = chosen.shape[0]
    flattened = chosen.reshape(-1)
    onehot = (flattened[:, None] == jnp.arange(EXPERTS)[None, :]).astype(jnp.int32)
    ranking = jnp.sum((jnp.cumsum(onehot, axis=0) - onehot) * onehot, axis=1)
    slot_index = flattened * CAP + ranking
    matches = (slot_index[:, None] == jnp.arange(EXPERTS * CAP)[None, :]).reshape(
        rows_here, TOP, EXPERTS * CAP
    )
    picker = jnp.transpose(jnp.any(matches, axis=1)).astype(jnp.bfloat16)
    blender = jnp.sum(jnp.where(matches, weights[:, :, None], 0.0), axis=1)
    return (picker, blender)


def run_experts(incoming_rows, gate_weight, up_weight, down_weight):
    layout = incoming_rows.shape
    gathered = incoming_rows.reshape(-1, layout[-1])
    gate_act = jnp.dot(gathered, gate_weight, preferred_element_type=jnp.float32)
    up_act = jnp.dot(gathered, up_weight, preferred_element_type=jnp.float32)
    activated = (jax.nn.silu(gate_act) * up_act).astype(jnp.bfloat16)
    produced = jnp.dot(activated, down_weight, preferred_element_type=jnp.float32).astype(
        jnp.bfloat16
    )
    produced = lax.optimization_barrier(produced)
    return produced.reshape(layout[:-1] + (down_weight.shape[1],))


def local(
    queries,
    residual,
    key_cache,
    value_cache,
    new_keys,
    new_values,
    cache_len,
    norm_gain,
    expert_ids,
    gate_fixed,
    gate_weight,
    up_weight,
    down_weight,
):
    device_count = lax.axis_size("attn")
    splits = device_count // EXPERTS
    width = queries.shape[1]
    results = []
    for batch_index in range(MICRO):
        window = slice(batch_index * MB_ROWS, (batch_index + 1) * MB_ROWS)
        hidden = attend(
            queries[window],
            residual[window],
            key_cache[window],
            value_cache[window],
            new_keys[window],
            new_values[window],
            cache_len[window],
        )
        hidden_f = lax.optimization_barrier(hidden).astype(jnp.float32)
        mean_square = jnp.mean(hidden_f * hidden_f, axis=-1, keepdims=True)
        normed = (hidden_f * lax.rsqrt(mean_square + EPS) * norm_gain[None, :]).astype(jnp.bfloat16)
        weights = gate_fixed[window].astype(jnp.float32) / FIXED_ONE
        picker, blender = routing(expert_ids[window], weights)
        blocks = jnp.dot(picker, normed, preferred_element_type=jnp.float32).astype(jnp.bfloat16)
        blocks = blocks.reshape(EXPERTS, CAP, width)
        outgoing = jnp.repeat(blocks, splits, axis=0)
        partial_value = run_experts(
            lax.all_to_all(outgoing, "attn", split_axis=0, concat_axis=0, tiled=True),
            gate_weight,
            up_weight,
            down_weight,
        )
        returned = lax.all_to_all(partial_value, "attn", split_axis=0, concat_axis=0, tiled=True)
        summed = jnp.sum(returned.reshape(EXPERTS, splits, CAP, width).astype(jnp.float32), axis=1)
        mixture = jnp.dot(
            blender,
            summed.reshape(EXPERTS * CAP, width),
            precision=lax.Precision.HIGHEST,
            preferred_element_type=jnp.float32,
        )
        results.append((hidden_f + mixture).astype(jnp.bfloat16))
    return jnp.concatenate(results, axis=0)


def solution(mesh):
    in_specs = (
        P(("groups", "attn"), None),
        P(("groups", "attn"), None),
        P(("groups", "attn"), None, None),
        P(("groups", "attn"), None, None),
        P(("groups", "attn"), None),
        P(("groups", "attn"), None),
        P(("groups", "attn")),
        P(),
        P(("groups", "attn"), None),
        P(("groups", "attn"), None),
        P(None, "attn"),
        P(None, "attn"),
        P("attn", None),
    )
    out_specs = P(("groups", "attn"), None)
    return jax.shard_map(local, mesh=mesh, in_specs=in_specs, out_specs=out_specs, check_vma=False)
```

profile of v0, /device:TPU:0, one launch (start us, length us, event | category | flops | bytes accessed | tf_op | source)
XLA Modules:
  0.0 117.7 jit_solution(14686752304107345523)
XLA Ops:
  0.0 0.8 fusion.52
  0.8 0.8 fusion.51
  2.3 0.7 slice_bitcast_fusion.5
  3.1 0.7 bitcast_convert_fusion.1
  3.8 0.8 fusion.50
  4.6 1.6 %slice_bitcast_fusion.3 = (bf16[8,12,4,8,128]{4,3,2,1,0:T(8,128)(2,1)S(1)}, bf16[8,12,4,8,128]{4,3,2,1,0:T(8,128)(2,1)S(1)}) fusion(bf16[16,96,512]{2,1,0:T(8,128)(2,1)} %param.15), kind=kLoop, calls=%fused_computation.31 | loop fusion | bytes 3145728
  6.5 0.6 fusion.53
  7.1 0.2 fusion.16
  7.6 0.6 fusion.54
  8.2 0.2 fusion.17
  8.5 1.6 %slice_bitcast_fusion.2 = (bf16[8,12,4,8,128]{4,3,2,1,0:T(8,128)(2,1)S(1)}, bf16[8,12,4,8,128]{4,3,2,1,0:T(8,128)(2,1)S(1)}) fusion(bf16[16,96,512]{2,1,0:T(8,128)(2,1)} %param.16), kind=kLoop, calls=%fused_computation.30 | loop fusion | bytes 3145728
  10.1 0.4 convolution_add_fusion.2
  10.5 0.4 convolution_add_fusion.3
  11.1 0.3 convolution_convert_fusion.3
  11.5 1.0 broadcast_in_dim.70
  12.4 7.4 %all-to-all-start = ((bf16[16,6,3072]{2,1,0:T(8,128)(2,1)}), bf16[16,6,3072]{2,1,0:T(8,128)(2,1)S(1)}, u32[]{:S(2)}, u32[]{:S(2)}) async-start(bf16[16,6,3072]{2,1,0:T(8,128)(2,1)} %bitcast.6), calls=%async_computation | async-start | bytes 1572864 | tf_op jit(solution)/shard_map/all_to_all | solution.py:124
  20.7 0.3 convolution_convert_fusion.2
  21.0 17.5 %all-to-all-done = bf16[16,6,3072]{2,1,0:T(8,128)(2,1)S(1)} async-done(((bf16[16,6,3072]{2,1,0:T(8,128)(2,1)}), bf16[16,6,3072]{2,1,0:T(8,128)(2,1)S(1)}, u32[]{:S(2)}, u32[]{:S(2)}) %all-to-all-start) | async-done | bytes 589856 | tf_op jit(solution)/shard_map/all_to_all | solution.py:124
  38.5 1.0 broadcast_in_dim.73
  39.5 5.5 %all-to-all-start.2 = ((bf16[16,6,3072]{2,1,0:T(8,128)(2,1)}), bf16[16,6,3072]{2,1,0:T(8,128)(2,1)S(1)}, u32[]{:S(2)}, u32[]{:S(2)}) async-start(bf16[16,6,3072]{2,1,0:T(8,128)(2,1)} %bitcast.14), calls=%async_computation.2 | async-start | bytes 1572864 | tf_op jit(solution)/shard_map/all_to_all | solution.py:124
  45.2 6.7 %fusion.55 = f32[96,2048]{1,0:T(8,128)S(1)} fusion(bf16[96,3072]{1,0:T(8,128)(2,1)S(1)} %reshape.172, bf16[3072,2048]{1,0:T(8,128)(2,1)} %param.23), kind=kOutput, calls=%fused_computation.108 | convolution fusion | flops 1207959552 | bytes 13959168 | tf_op jit(solution)/shard_map/dot_general | solution.py:75
  51.9 12.3 %convolution_convert_fusion.1 = bf16[96,3072]{1,0:T(8,128)(2,1)S(1)} fusion(bf16[2048,3072]{1,0:T(8,128)(2,1)} %param.25, bf16[96,3072]{1,0:T(8,128)(2,1)S(1)} %reshape.172, bf16[3072,2048]{1,0:T(8,128)(2,1)} %param.24, f32[96,2048]{1,0:T(8,128)S(1)} %fusion.55), kind=kOutput, calls=%fused_computation.1 | convolution fusion | flops 2417393664 | bytes 27131904 | tf_op jit(solution)/shard_map/dot_general | solution.py:78
  64.2 1.1 reshape.173
  65.3 6.0 %all-to-all-start.1 = ((bf16[16,6,3072]{2,1,0:T(8,128)(2,1)}), bf16[16,6,3072]{2,1,0:T(8,128)(2,1)S(1)}, u32[]{:S(2)}, u32[]{:S(2)}) async-start(bf16[16,6,3072]{2,1,0:T(8,128)(2,1)} %reshape.173), calls=%async_computation.1 | async-start | bytes 1572864 | tf_op jit(solution)/shard_map/all_to_all | solution.py:129
  71.5 6.7 %fusion.56 = f32[96,2048]{1,0:T(8,128)S(1)} fusion(bf16[96,3072]{1,0:T(8,128)(2,1)S(1)} %reshape.182, bf16[3072,2048]{1,0:T(8,128)(2,1)} %param.23), kind=kOutput, calls=%fused_computation.109 | convolution fusion | flops 1207959552 | bytes 13959168 | tf_op jit(solution)/shard_map/dot_general | solution.py:75
  78.2 12.3 %convolution_convert_fusion = bf16[96,3072]{1,0:T(8,128)(2,1)S(1)} fusion(bf16[2048,3072]{1,0:T(8,128)(2,1)} %param.25, bf16[96,3072]{1,0:T(8,128)(2,1)S(1)} %reshape.182, bf16[3072,2048]{1,0:T(8,128)(2,1)} %param.24, f32[96,2048]{1,0:T(8,128)S(1)} %fusion.56), kind=kOutput, calls=%fused_computation | convolution fusion | flops 2417393664 | bytes 27131904 | tf_op jit(solution)/shard_map/dot_general | solution.py:78
  90.5 1.1 reshape.183
  91.6 6.0 %all-to-all-start.3 = ((bf16[16,6,3072]{2,1,0:T(8,128)(2,1)}), bf16[16,6,3072]{2,1,0:T(8,128)(2,1)S(1)}, u32[]{:S(2)}, u32[]{:S(2)}) async-start(bf16[16,6,3072]{2,1,0:T(8,128)(2,1)} %reshape.183), calls=%async_computation.3 | async-start | bytes 1572864 | tf_op jit(solution)/shard_map/all_to_all | solution.py:129
  98.0 18.3 %all-to-all-done.3 = bf16[16,6,3072]{2,1,0:T(8,128)(2,1)S(1)} async-done(((bf16[16,6,3072]{2,1,0:T(8,128)(2,1)}), bf16[16,6,3072]{2,1,0:T(8,128)(2,1)S(1)}, u32[]{:S(2)}, u32[]{:S(2)}) %all-to-all-start.3) | async-done | bytes 589856 | tf_op jit(solution)/shard_map/all_to_all | solution.py:129
  116.5 0.3 fusion
  116.8 0.3 fusion.1
  117.1 0.6 pad_maximum_fusion
  (54 shorter events, 3.4 us)
Async XLA Ops:
  0.0 11.0 %copy-start = (bf16[16,3072]{1,0:T(8,128)(2,1)S(1)}, bf16[16,3072]{1,0:T(8,128)(2,1)}, u32[]{:S(2)}) copy-start(bf16[16,3072]{1,0:T(8,128)(2,1)} %param.14) | copy-start | bytes 294916
  0.0 11.1 %copy-start.1 = (f32[3072]{0:T(1024)S(1)}, f32[3072]{0:T(1024)}, u32[]{:S(2)}) copy-start(f32[3072]{0:T(1024)} %param.20) | copy-start | bytes 36868
  12.4 26.1 %all-to-all-start = ((bf16[16,6,3072]{2,1,0:T(8,128)(2,1)}), bf16[16,6,3072]{2,1,0:T(8,128)(2,1)S(1)}, u32[]{:S(2)}, u32[]{:S(2)}) async-start(bf16[16,6,3072]{2,1,0:T(8,128)(2,1)} %bitcast.6), calls=%async_computation | async-start | bytes 1572864 | tf_op jit(solution)/shard_map/all_to_all | solution.py:124
  39.5 25.7 %all-to-all-start.2 = ((bf16[16,6,3072]{2,1,0:T(8,128)(2,1)}), bf16[16,6,3072]{2,1,0:T(8,128)(2,1)S(1)}, u32[]{:S(2)}, u32[]{:S(2)}) async-start(bf16[16,6,3072]{2,1,0:T(8,128)(2,1)} %bitcast.14), calls=%async_computation.2 | async-start | bytes 1572864 | tf_op jit(solution)/shard_map/all_to_all | solution.py:124
  65.3 26.3 %all-to-all-start.1 = ((bf16[16,6,3072]{2,1,0:T(8,128)(2,1)}), bf16[16,6,3072]{2,1,0:T(8,128)(2,1)S(1)}, u32[]{:S(2)}, u32[]{:S(2)}) async-start(bf16[16,6,3072]{2,1,0:T(8,128)(2,1)} %reshape.173), calls=%async_computation.1 | async-start | bytes 1572864 | tf_op jit(solution)/shard_map/all_to_all | solution.py:129
  78.2 19.4 %copy-start.2 = (s32[16,2]{0,1:T(2,128)S(1)}, s32[16,2]{0,1:T(2,128)}, u32[]{:S(2)}) copy-start(s32[16,2]{0,1:T(2,128)} %param.22) | copy-start | bytes 388
  91.6 24.7 %all-to-all-start.3 = ((bf16[16,6,3072]{2,1,0:T(8,128)(2,1)}), bf16[16,6,3072]{2,1,0:T(8,128)(2,1)S(1)}, u32[]{:S(2)}, u32[]{:S(2)}) async-start(bf16[16,6,3072]{2,1,0:T(8,128)(2,1)} %reshape.183), calls=%async_computation.3 | async-start | bytes 1572864 | tf_op jit(solution)/shard_map/all_to_all | solution.py:129
where the time goes:
time: 119 us; the launch traced here: 118 us
  matrix products  41.3 us (35%)
  waiting for transfers between devices  35.8 us (30%)
  starting transfers between devices  24.9 us (21%)
  local copies, waits for them, and re-layouts  11.9 us (10%)
  other arithmetic  3.56 us (3%)
    dot_general x2, matrix products, run_experts(): jnp.dot(activated, down_weight, preferred_element_type=jnp.float32)  24.6 us
    all_to_all x2, waiting for transfers between devices, local(): lax.all_to_all(partial_value, 'attn', split_axis=0, concat_axis=0, tiled=...  18.3 us
    all_to_all x2, waiting for transfers between devices, local(): lax.all_to_all(outgoing, 'attn', split_axis=0, concat_axis=0, tiled=True)  17.5 us
    dot_general x2, matrix products, run_experts(): jnp.dot(gathered, gate_weight, preferred_element_type=jnp.float32)  13.4 us
    all_to_all x2, starting transfers between devices, local(): lax.all_to_all(outgoing, 'attn', split_axis=0, concat_axis=0, tiled=True)  12.9 us
    all_to_all x2, starting transfers between devices, local(): lax.all_to_all(partial_value, 'attn', split_axis=0, concat_axis=0, tiled=...  12 us
    unnamed x10, local copies, waits for them, and re-layouts  3.46 us
  transfers between devices with their start and end apart: 4, of which 2 were waited for; matrix products, arithmetic and copies ran while one was open for 36% of the time, Pallas kernels for 0%

commit v1 on v0

v1 whole, which is shorter than its diff:
```python
import functools
import math

import jax
import jax.numpy as jnp
import numpy as np
from jax import lax
from jax.experimental import pallas as pl
from jax.experimental.pallas import tpu as pltpu
from jax.sharding import PartitionSpec as P

HEAD = 128
Q_HEADS = 24
KV_HEADS = 4
EXPERTS = 4
TOP = 2
MB_ROWS = 8
CACHE = 96
CAP = 6
EPS = 1e-05
FEAT = 4
ROWS = 16
SLOTS = CAP * ROWS // MB_ROWS
PACK = FEAT * SLOTS
GROUP = Q_HEADS // KV_HEADS
LANES = FEAT * ROWS
MIB = 2**20
BF16, F32, I32 = jnp.bfloat16, jnp.float32, jnp.int32


def iota(shape, dim):
    return lax.broadcasted_iota(I32, shape, dim)


def slots_of(plane, ids_ref):
    expert = (plane + iota((8, ROWS), 0)) & (EXPERTS - 1)
    first = ids_ref[0:1, :] == expert
    second = ids_ref[1:2, :] == expert
    named = jnp.where(first | second, 1.0, 0.0).astype(BF16)
    token, lane_token = iota((ROWS, LANES), 0), iota((ROWS, LANES), 1) & (ROWS - 1)
    spread = jnp.where(token == lane_token, 1.0, 0.0).astype(BF16)
    earlier = (token < lane_token) & ((token >> 3) == (lane_token >> 3))
    earlier = jnp.where(earlier, 1.0, 0.0).astype(BF16)
    named_wide = jnp.dot(named, spread, preferred_element_type=F32)
    rank = jnp.dot(named, earlier, preferred_element_type=F32).astype(I32)
    batch = (iota((8, LANES), 1) & (ROWS - 1)) >> 3
    slot = jnp.where(named_wide > 0.5, batch * CAP + rank, -1)
    return slot, spread, first, second


def matching(slot, s):
    row, lane = iota((PACK, LANES), 0), iota((PACK, LANES), 1)
    chunk = sum((row >= SLOTS * f).astype(I32) for f in range(1, FEAT))
    return (chunk == (lane >> 4)) & (slot[s : s + 1, :] == row - SLOTS * chunk)


def attention_kernel(
    plane_ref, len_ref, q_ref, res_ref, k_hbm, v_hbm, nk_ref, nv_ref, gain_ref, ids_ref,
    hid_ref, b0_ref, b1_ref, b2_ref, b3_ref,
    k_ref, v_ref, q_scr, o_scr, sems,
):
    parts = sems.shape[1]
    step = ROWS // parts
    copies = []
    for c in range(parts):
        own = pl.ds(c * step, step)
        pair = (
            pltpu.make_async_copy(k_hbm.at[own], k_ref.at[own], sems.at[0, c]),
            pltpu.make_async_copy(v_hbm.at[own], v_ref.at[own], sems.at[1, c]),
        )
        for copy in pair:
            copy.start()
        copies.append(pair)
    for h in range(Q_HEADS):
        q_scr[pl.ds(h, ROWS, stride=Q_HEADS), :] = q_ref[:, h * HEAD : (h + 1) * HEAD].astype(F32)
    row, col = iota((Q_HEADS, KV_HEADS * HEAD), 0), iota((Q_HEADS, KV_HEADS * HEAD), 1)
    reads = sum((row >= GROUP * k).astype(I32) for k in range(1, KV_HEADS)) == (col >> 7)
    head_row = iota((Q_HEADS, HEAD), 0)
    position, own_col = iota((Q_HEADS, CACHE), 1), iota((Q_HEADS, ROWS), 1)
    scaling = 1.0 / math.sqrt(HEAD)
    contract = (((1,), (1,)), ((), ()))
    nk, nv = nk_ref[...], nv_ref[...]
    low = -1e30
    for t in range(ROWS):
        if t % step == 0:
            for copy in copies[t // step]:
                copy.wait()
        q = q_scr[t * Q_HEADS : (t + 1) * Q_HEADS, :]
        q = jnp.where(reads, jnp.concatenate([q] * KV_HEADS, axis=1), 0.0).astype(BF16)
        s1 = lax.dot_general(q, k_ref[t], contract, preferred_element_type=F32) * scaling
        s2 = lax.dot_general(q, nk, contract, preferred_element_type=F32) * scaling
        s1 = jnp.where(position < len_ref[t], s1, low)
        s2 = jnp.where(own_col == t, s2, low)
        top = jnp.maximum(jnp.max(s1, axis=1, keepdims=True), jnp.max(s2, axis=1, keepdims=True))
        e1, e2 = jnp.exp(s1 - top), jnp.exp(s2 - top)
        total = jnp.sum(e1, axis=1, keepdims=True) + jnp.sum(e2, axis=1, keepdims=True)
        p1, p2 = (e1 / total).astype(BF16), (e2 / total).astype(BF16)
        o = jnp.dot(p1, v_ref[t], preferred_element_type=F32)
        o = o + jnp.dot(p2, nv, preferred_element_type=F32)
        picked = o[:, 0:HEAD]
        for k in range(1, KV_HEADS):
            picked = jnp.where(head_row >= GROUP * k, o[:, k * HEAD : (k + 1) * HEAD], picked)
        o_scr[t * Q_HEADS : (t + 1) * Q_HEADS, :] = picked
    squares = jnp.zeros((ROWS, HEAD), F32)
    hidden = []
    for h in range(Q_HEADS):
        span = slice(h * HEAD, (h + 1) * HEAD)
        part = (res_ref[:, span].astype(F32) + o_scr[pl.ds(h, ROWS, stride=Q_HEADS), :]).astype(BF16)
        hid_ref[:, span] = part
        part = part.astype(F32)
        squares = squares + part * part
        hidden.append(part)
    width = Q_HEADS * HEAD
    scale = lax.rsqrt(jnp.sum(squares, axis=1, keepdims=True) * (1.0 / width) + EPS)
    per = Q_HEADS // FEAT
    chunks = []
    for f in range(FEAT):
        heads = [
            (hidden[h] * scale * gain_ref[:, h * HEAD : (h + 1) * HEAD]).astype(BF16)
            for h in range(f * per, (f + 1) * per)
        ]
        chunks.append(jnp.concatenate(heads, axis=1))
    stacked = jnp.concatenate(chunks, axis=0)
    slot, _, _, _ = slots_of(plane_ref[0], ids_ref)
    for s, out in enumerate((b0_ref, b1_ref, b2_ref, b3_ref)):
        picker = jnp.where(matching(slot, s), 1.0, 0.0).astype(BF16)
        out[...] = jnp.dot(picker, stacked, preferred_element_type=F32).astype(BF16)


def blend_kernel(plane_ref, ids_ref, gate_ref, out_ref):
    slot, spread, first, second = slots_of(plane_ref[0], ids_ref)
    gate = jnp.where(first, gate_ref[0:1, :], 0) + jnp.where(second, gate_ref[1:2, :], 0)
    high = jnp.dot((gate >> 6).astype(F32).astype(BF16), spread, preferred_element_type=F32)
    rest = jnp.dot((gate & 63).astype(F32).astype(BF16), spread, preferred_element_type=F32)
    for s in range(EXPERTS):
        match = matching(slot, s)
        rows = slice(s * PACK, (s + 1) * PACK)
        out_ref[rows, 0:LANES] = jnp.where(match, high[s : s + 1, :], 0.0).astype(BF16)
        out_ref[rows, LANES : 2 * LANES] = jnp.where(match, rest[s : s + 1, :], 0.0).astype(BF16)


def experts_kernel(slabs, *refs):
    blocks = refs[: slabs * EXPERTS]
    order_ref, back_ref, gate_ref, up_ref, down_ref = refs[slabs * EXPERTS : slabs * EXPERTS + 5]
    outs = refs[slabs * EXPERTS + 5 : -3]
    x_ref, a_ref, y_ref = refs[-3:]
    rows = EXPERTS * SLOTS
    part = y_ref.shape[2]
    order = order_ref[...]
    for q in range(slabs):
        packed = jnp.concatenate([b[...] for b in blocks[q * EXPERTS : (q + 1) * EXPERTS]], axis=0)
        x = jnp.dot(order, packed, preferred_element_type=F32).astype(BF16)
        for f in range(FEAT):
            x_ref[q * rows : (q + 1) * rows, f * part : (f + 1) * part] = x[f * rows : (f + 1) * rows]
    x = x_ref[...]
    units = gate_ref.shape[1]
    tile = min(512, units)
    for j in range(units // tile):
        span = slice(j * tile, (j + 1) * tile)
        g = jnp.dot(x, gate_ref[:, span], preferred_element_type=F32)
        u = jnp.dot(x, up_ref[:, span], preferred_element_type=F32)
        a_ref[:, span] = (g / (1.0 + jnp.exp(-g)) * u).astype(BF16)
    a = a_ref[...]
    for f in range(FEAT):
        span = slice(f * part, (f + 1) * part)
        y_ref[f] = jnp.dot(a, down_ref[:, span], preferred_element_type=F32).astype(BF16)
    back = back_ref[...]
    for q in range(slabs):
        stacked = jnp.concatenate([y_ref[f, q * rows : (q + 1) * rows, :] for f in range(FEAT)], axis=0)
        packed = jnp.dot(back, stacked, preferred_element_type=F32).astype(BF16)
        half = q // (slabs // 2)
        at = (q % (slabs // 2)) * EXPERTS * PACK
        outs[half][at : at + EXPERTS * PACK, :] = packed


def mix_kernel(hid_ref, blend_ref, m0_ref, m1_ref, m2_ref, m3_ref, out_ref):
    part = m0_ref.shape[1]
    packed = jnp.concatenate([m0_ref[...], m1_ref[...], m2_ref[...], m3_ref[...]], axis=0)
    mixed = lax.dot_general(blend_ref[...], packed, (((0,), (0,)), ((), ())), preferred_element_type=F32)
    mixed = mixed[:LANES] * (1.0 / 64.0) + mixed[LANES:] * (1.0 / 4096.0)
    for f in range(FEAT):
        span = slice(f * part, (f + 1) * part)
        own = hid_ref[:, span].astype(F32) + mixed[f * ROWS : (f + 1) * ROWS]
        out_ref[:, span] = own.astype(BF16)


VMEM = pl.BlockSpec(memory_space=pltpu.VMEM)
SMEM = pl.BlockSpec(memory_space=pltpu.SMEM)
HBM = pl.BlockSpec(memory_space=pl.ANY)


def params(mib):
    return pltpu.CompilerParams(vmem_limit_bytes=mib * MIB)


def local(
    queries, residual, key_cache, value_cache, new_keys, new_values, cache_len, norm_gain,
    expert_ids, gate_fixed, gate_weight, up_weight, down_weight,
):
    devices = lax.axis_size("attn")
    splits = devices // EXPERTS
    width = queries.shape[1]
    part = width // FEAT
    kv_width = key_cache.shape[2]
    plane = (lax.axis_index("attn") // splits).astype(I32).reshape(1)
    ids, gates = expert_ids.T, gate_fixed.T
    block = jax.ShapeDtypeStruct((PACK, part), BF16)

    hidden, *blocks = pl.pallas_call(
        attention_kernel,
        out_shape=[jax.ShapeDtypeStruct((ROWS, width), BF16)] + [block] * EXPERTS,
        in_specs=[SMEM, SMEM, VMEM, VMEM, HBM, HBM, VMEM, VMEM, VMEM, VMEM],
        out_specs=[VMEM] * (1 + EXPERTS),
        scratch_shapes=[
            pltpu.VMEM((ROWS, CACHE, kv_width), BF16),
            pltpu.VMEM((ROWS, CACHE, kv_width), BF16),
            pltpu.VMEM((ROWS * Q_HEADS, HEAD), F32),
            pltpu.VMEM((ROWS * Q_HEADS, HEAD), F32),
            pltpu.SemaphoreType.DMA((2, 4)),
        ],
        compiler_params=params(14),
        cost_estimate=pl.CostEstimate(flops=10**9, bytes_accessed=20 * 10**6, transcendentals=0),
        name="attention",
    )(
        plane, cache_len, queries, residual, key_cache, value_cache, new_keys, new_values,
        norm_gain.reshape(1, width), ids,
    )
    blend = pl.pallas_call(
        blend_kernel,
        out_shape=jax.ShapeDtypeStruct((EXPERTS * PACK, 2 * LANES), BF16),
        in_specs=[SMEM, VMEM, VMEM],
        out_specs=VMEM,
        compiler_params=params(4),
        name="blend",
    )(plane, ids, gates)

    def shifted(x, s):
        return lax.ppermute(x, "attn", [(i, (i + s * splits) % devices) for i in range(devices)])

    def swapped(x, bit):
        return lax.ppermute(x, "attn", [(i, i ^ bit) for i in range(devices)])

    got = [blocks[0]] + [shifted(blocks[s], s) for s in range(1, EXPERTS)]
    bit = splits // 2
    while bit >= 1:
        got = got + [swapped(b, bit) for b in got]
        bit //= 2
    total = splits * EXPERTS * SLOTS
    to = np.arange(EXPERTS * PACK)
    f, s, j = to // (EXPERTS * SLOTS), to // SLOTS % EXPERTS, to % SLOTS
    order = np.zeros((EXPERTS * PACK, EXPERTS * PACK), np.float32)
    order[to, s * PACK + f * SLOTS + j] = 1.0
    weights = [pltpu.with_memory_space_constraint(w, pltpu.VMEM) for w in (gate_weight, up_weight, down_weight)]
    units = gate_weight.shape[1]
    keep, send = pl.pallas_call(
        functools.partial(experts_kernel, splits),
        out_shape=[jax.ShapeDtypeStruct((splits // 2 * EXPERTS * PACK, part), BF16)] * 2,
        in_specs=[VMEM] * (splits * EXPERTS + 5),
        out_specs=[VMEM] * 2,
        scratch_shapes=[
            pltpu.VMEM((total, width), BF16),
            pltpu.VMEM((total, units), BF16),
            pltpu.VMEM((FEAT, total, part), BF16),
        ],
        compiler_params=params(16 if total <= 192 else 36),
        cost_estimate=pl.CostEstimate(
            flops=6 * total * width * units, bytes_accessed=6 * width * units, transcendentals=0
        ),
        name="experts",
    )(*got, jnp.asarray(order, BF16), jnp.asarray(order.T, BF16), *weights)

    def plus(a, b):
        return (a.astype(F32) + b.astype(F32)).astype(BF16)

    keep = plus(keep, swapped(send, 1))
    rows, bit = keep.shape[0], 2
    while rows > EXPERTS * PACK * 2:
        keep = plus(keep[: rows // 2], swapped(keep[rows // 2 :], bit))
        rows, bit = rows // 2, bit * 2
    summed = [
        plus(keep[s * PACK : (s + 1) * PACK], swapped(keep[rows // 2 + s * PACK : rows // 2 + (s + 1) * PACK], bit))
        for s in range(EXPERTS)
    ]
    mine = [summed[0]] + [shifted(summed[s], -s) for s in range(1, EXPERTS)]
    return pl.pallas_call(
        mix_kernel,
        out_shape=jax.ShapeDtypeStruct((ROWS, width), BF16),
        in_specs=[VMEM] * (2 + EXPERTS),
        out_specs=VMEM,
        compiler_params=params(8),
        name="mix",
    )(hidden, blend, *mine)


def solution(mesh):
    rows = P(("groups", "attn"), None)
    cached = P(("groups", "attn"), None, None)
    in_specs = (
        rows, rows, cached, cached, rows, rows, P(("groups", "attn")), P(), rows, rows,
        P(None, "attn"), P(None, "attn"), P("attn", None),
    )
    return jax.shard_map(local, mesh=mesh, in_specs=in_specs, out_specs=rows, check_vma=False)
```

time: 119 us -> 80.7 us (0.68)
  matrix products: 41.3 us -> 0 us
  Pallas kernels: 0 us -> 18.8 us
  waiting for transfers between devices: 35.8 us -> 17.8 us
  local copies, waits for them, and re-layouts: 11.9 us -> 21.8 us
  starting transfers between devices: 24.9 us -> 21.5 us
  other arithmetic: 3.56 us -> 0.22 us
    dot_general x14 -> x0, matrix products: 41.3 us -> none  [the longest x2 24.6 us: run_experts(): jnp.dot(activated, down_weight, preferred_element_type=jnp.float32)]
    all_to_all x4 -> x0, waiting for transfers between devices: 35.8 us -> none  [the longest x2 18.3 us: local(): lax.all_to_all(partial_value, 'attn', split_axis=0, concat_axis=0, tiled=...]
    all_to_all x4 -> x0, starting transfers between devices: 24.9 us -> none  [the longest x2 12.9 us: local(): lax.all_to_all(outgoing, 'attn', split_axis=0, concat_axis=0, tiled=True)]
    ppermute x0 -> x23, starting transfers between devices: none -> 21.5 us  [the longest x6 11.4 us: shifted(): lax.ppermute(x, 'attn', [(i, (i + s * splits) % devices) for i in range(d...]
    pallas_call x0 -> x4, Pallas kernels: none -> 18.8 us  [the longest x1 8.99 us: local(): pl.pallas_call(functools.partial(experts_kernel, splits), out_shape=[jax....]
    unnamed x10 -> x30, local copies, waits for them, and re-layouts: 3.46 us -> 21.8 us
    ppermute x0 -> x23, waiting for transfers between devices: none -> 17.8 us  [the longest x17 11.8 us: swapped(): return lax.ppermute(x, 'attn', [(i, i ^ bit) for i in range(devices)])]
    reshape x11 -> x0, local copies, waits for them, and re-layouts: 3.57 us -> none  [the longest x2 2.19 us: run_experts(): return produced.reshape(layout[:-1] + (down_weight.shape[1],))]
  transfers between devices with their start and end apart: 4 -> 23, of which waited for: 2 -> 14; matrix products, arithmetic and copies ran while one was open for 36% -> 0% of each run, Pallas kernels for 0% -> 0%
where the time goes in v1:
time: 80.7 us; the launch traced here: 80.2 us
  local copies, waits for them, and re-layouts  21.8 us (27%)
  starting transfers between devices  21.5 us (27%)
  Pallas kernels  18.8 us (23%)
  waiting for transfers between devices  17.8 us (22%)
    unnamed x30, local copies, waits for them, and re-layouts  21.8 us
    ppermute x17, waiting for transfers between devices, swapped(): return lax.ppermute(x, 'attn', [(i, i ^ bit) for i in range(devices)])  11.8 us
    ppermute x6, starting transfers between devices, shifted(): lax.ppermute(x, 'attn', [(i, (i + s * splits) % devices) for i in range(d...  11.4 us
    ppermute x17, starting transfers between devices, swapped(): return lax.ppermute(x, 'attn', [(i, i ^ bit) for i in range(devices)])  10.1 us
    pallas_call x1, Pallas kernels, local(): pl.pallas_call(functools.partial(experts_kernel, splits), out_shape=[jax....  8.99 us
    pallas_call x1, Pallas kernels, local(): pl.pallas_call(attention_kernel, out_shape=[jax.ShapeDtypeStruct((ROWS, w...  8.67 us
    ppermute x6, waiting for transfers between devices, shifted(): lax.ppermute(x, 'attn', [(i, (i + s * splits) % devices) for i in range(d...  6.03 us
  transfers between devices with their start and end apart: 23, of which 14 were waited for; matrix products, arithmetic and copies ran while one was open for 0% of the time, Pallas kernels for 0%

profile of v1, /device:TPU:0, one launch (start us, length us, event | category | flops | bytes accessed | tf_op | source)
XLA Modules:
  0.0 80.2 jit_solution(9334614450036522985)
XLA Ops:
  0.7 1.4 %copy-done.7 = bf16[16,96,512]{2,1,0:T(8,128)(2,1)S(1)} copy-done((bf16[16,96,512]{2,1,0:T(8,128)(2,1)S(1)}, bf16[16,96,512]{2,1,0:T(8,128)(2,1)}, u32[]{:S(2)}) %copy-start.7) | copy-done | bytes 1572888
  2.1 1.4 %copy-done.8 = bf16[16,96,512]{2,1,0:T(8,128)(2,1)S(1)} copy-done((bf16[16,96,512]{2,1,0:T(8,128)(2,1)S(1)}, bf16[16,96,512]{2,1,0:T(8,128)(2,1)}, u32[]{:S(2)}) %copy-start.8) | copy-done | bytes 1572888
  3.5 0.9 %copy-done.9 = bf16[16,3072]{1,0:T(8,128)(2,1)S(1)} copy-done((bf16[16,3072]{1,0:T(8,128)(2,1)S(1)}, bf16[16,3072]{1,0:T(8,128)(2,1)}, u32[]{:S(2)}) %copy-start.9) | copy-done | bytes 98328
  4.4 0.9 %copy-done.10 = bf16[16,3072]{1,0:T(8,128)(2,1)S(1)} copy-done((bf16[16,3072]{1,0:T(8,128)(2,1)S(1)}, bf16[16,3072]{1,0:T(8,128)(2,1)}, u32[]{:S(2)}) %copy-start.10) | copy-done | bytes 98328
  8.1 8.7 %attention.1 = (bf16[16,3072]{1,0:T(8,128)(2,1)S(1)}, bf16[48,768]{1,0:T(8,128)(2,1)S(1)}, bf16[48,768]{1,0:T(8,128)(2,1)S(1)}, bf16[48,768]{1,0:T(8,128)(2,1)S(1)}, bf16[48,768]{1,0:T(8,128)(2,1)S(1)}) custom-call(s32[1]{0:T(128)} %bitcast.plane_ref, s32[16]{0:T(128)S(1)} %copy-done.14, bf16[16,3072]{1,0:T(8,128)(2,1)S(1)} %copy-done.9, ...), custom_call_target="tpu_custom_call" | custom-call | flops 1000000000 | bytes 20000000 | tf_op jit(solution)/shard_map/attention/pallas_call | solution.py:209
  16.8 3.1 %collective-permute-start = (bf16[48,768]{1,0:T(8,128)(2,1)S(1)}, bf16[48,768]{1,0:T(8,128)(2,1)S(1)}, u32[]{:S(2)}, u32[]{:S(2)}) collective-permute-start(bf16[48,768]{1,0:T(8,128)(2,1)S(1)} %get-tuple-element.14), channel_id=1, source_target_pairs={{0,4},{1,5},{2,6},{3,7},{4,8},{5,9},{6,10},{7,11},{8,12},{9,13},{1... | collective-permute-start | bytes 221192 | tf_op jit(solution)/shard_map/ppermute | solution.py:238
  19.8 2.6 %collective-permute-start.1 = (bf16[48,768]{1,0:T(8,128)(2,1)S(1)}, bf16[48,768]{1,0:T(8,128)(2,1)S(1)}, u32[]{:S(2)}, u32[]{:S(2)}) collective-permute-start(bf16[48,768]{1,0:T(8,128)(2,1)S(1)} %get-tuple-element.15), channel_id=1, source_target_pairs={{0,8},{1,9},{2,10},{3,11},{4,12},{5,13},{6,14},{7,15},{8,0},{9,1},... | collective-permute-start | bytes 221192 | tf_op jit(solution)/shard_map/ppermute | solution.py:238
  22.4 1.4 %collective-permute-start.2 = (bf16[48,768]{1,0:T(8,128)(2,1)S(1)}, bf16[48,768]{1,0:T(8,128)(2,1)S(1)}, u32[]{:S(2)}, u32[]{:S(2)}) collective-permute-start(bf16[48,768]{1,0:T(8,128)(2,1)S(1)} %get-tuple-element.16), channel_id=1, source_target_pairs={{0,12},{1,13},{2,14},{3,15},{4,0},{5,1},{6,2},{7,3},{8,4},{9,5},{1... | collective-permute-start | bytes 221192 | tf_op jit(solution)/shard_map/ppermute | solution.py:238
  23.8 1.5 %collective-permute-start.3 = (bf16[48,768]{1,0:T(8,128)(2,1)S(1)}, bf16[48,768]{1,0:T(8,128)(2,1)S(1)}, u32[]{:S(2)}, u32[]{:S(2)}) collective-permute-start(bf16[48,768]{1,0:T(8,128)(2,1)S(1)} %get-tuple-element.13.refs_0_), channel_id=1, source_target_pairs={{0,2},{1,3},{2,0},{3,1},{4,6},{5,7},{6,4},{7,5},{8,10},{9,11},{10,... | collective-permute-start | bytes 221192 | tf_op jit(solution)/shard_map/ppermute | solution.py:241
  25.3 1.2 %collective-permute-start.4 = (bf16[48,768]{1,0:T(8,128)(2,1)S(1)}, bf16[48,768]{1,0:T(8,128)(2,1)S(1)}, u32[]{:S(2)}, u32[]{:S(2)}) collective-permute-start(bf16[48,768]{1,0:T(8,128)(2,1)S(1)} %collective-permute-done.refs_1_), channel_id=1, source_target_pairs={{0,2},{1,3},{2,0},{3,1},{4,6},{5,7},{6,4},{7,5},{8,10},{9,11},{10,... | collective-permute-start | bytes 221192 | tf_op jit(solution)/shard_map/ppermute | solution.py:241
  26.5 0.9 %collective-permute-done.1.refs_2_ = bf16[48,768]{1,0:T(8,128)(2,1)S(1)} collective-permute-done((bf16[48,768]{1,0:T(8,128)(2,1)S(1)}, bf16[48,768]{1,0:T(8,128)(2,1)S(1)}, u32[]{:S(2)}, u32[]{:S(2)}) %collective-permute-start.1) | collective-permute-done | bytes 73760 | tf_op jit(solution)/shard_map/ppermute | solution.py:238
  27.4 1.7 %collective-permute-start.5 = (bf16[48,768]{1,0:T(8,128)(2,1)S(1)}, bf16[48,768]{1,0:T(8,128)(2,1)S(1)}, u32[]{:S(2)}, u32[]{:S(2)}) collective-permute-start(bf16[48,768]{1,0:T(8,128)(2,1)S(1)} %collective-permute-done.1.refs_2_), channel_id=1, source_target_pairs={{0,2},{1,3},{2,0},{3,1},{4,6},{5,7},{6,4},{7,5},{8,10},{9,11},{10,... | collective-permute-start | bytes 221192 | tf_op jit(solution)/shard_map/ppermute | solution.py:241
  30.1 2.4 %collective-permute-done.5.refs_6_ = bf16[48,768]{1,0:T(8,128)(2,1)S(1)} collective-permute-done((bf16[48,768]{1,0:T(8,128)(2,1)S(1)}, bf16[48,768]{1,0:T(8,128)(2,1)S(1)}, u32[]{:S(2)}, u32[]{:S(2)}) %collective-permute-start.5) | collective-permute-done | bytes 73760 | tf_op jit(solution)/shard_map/ppermute | solution.py:241
  32.5 0.9 %collective-permute-done.6.refs_7_ = bf16[48,768]{1,0:T(8,128)(2,1)S(1)} collective-permute-done((bf16[48,768]{1,0:T(8,128)(2,1)S(1)}, bf16[48,768]{1,0:T(8,128)(2,1)S(1)}, u32[]{:S(2)}, u32[]{:S(2)}) %collective-permute-start.6) | collective-permute-done | bytes 73760 | tf_op jit(solution)/shard_map/ppermute | solution.py:241
  35.2 4.6 %copy-done = bf16[3072,2048]{1,0:T(8,128)(2,1)S(1)} copy-done((bf16[3072,2048]{1,0:T(8,128)(2,1)S(1)}, bf16[3072,2048]{1,0:T(8,128)(2,1)}, u32[]{:S(2)}) %copy-start) | copy-done | bytes 12582936
  39.8 4.6 %copy-done.1 = bf16[3072,2048]{1,0:T(8,128)(2,1)S(1)} copy-done((bf16[3072,2048]{1,0:T(8,128)(2,1)S(1)}, bf16[3072,2048]{1,0:T(8,128)(2,1)}, u32[]{:S(2)}) %copy-start.1) | copy-done | bytes 12582936
  44.4 4.6 %copy-done.2 = bf16[2048,3072]{1,0:T(8,128)(2,1)S(1)} copy-done((bf16[2048,3072]{1,0:T(8,128)(2,1)S(1)}, bf16[2048,3072]{1,0:T(8,128)(2,1)}, u32[]{:S(2)}) %copy-start.2) | copy-done | bytes 12582936
  49.0 9.0 %experts.1 = (bf16[384,768]{1,0:T(8,128)(2,1)S(1)}, bf16[384,768]{1,0:T(8,128)(2,1)}) custom-call(bf16[48,768]{1,0:T(8,128)(2,1)S(1)} %get-tuple-element.13.refs_0_, bf16[48,768]{1,0:T(8,128)(2,1)S(1)} %collective-permute-done.refs_1_, bf16[48,768]{1,0:T(8,128)(2,1)S(1)} %collective-permute-done.1.refs_2_, ...), custom_call_target="tpu_custom_call" | custom-call | flops 7247757312 | bytes 37748736 | tf_op jit(solution)/shard_map/experts/pallas_call | solution.py:255
  58.1 2.1 %collective-permute-done.15 = bf16[384,768]{1,0:T(8,128)(2,1)S(1)} collective-permute-done((bf16[384,768]{1,0:T(8,128)(2,1)}, bf16[384,768]{1,0:T(8,128)(2,1)S(1)}, u32[]{:S(2)}, u32[]{:S(2)}) %collective-permute-start.15) | collective-permute-done | bytes 589856 | tf_op jit(solution)/shard_map/ppermute | solution.py:241
  60.4 1.0 %collective-permute-start.16 = (bf16[48,768]{1,0:T(8,128)(2,1)S(1)}, bf16[48,768]{1,0:T(8,128)(2,1)S(1)}, u32[]{:S(2)}, u32[]{:S(2)}) collective-permute-start(bf16[48,768]{1,0:T(8,128)(2,1)S(1)} %get-tuple-element.26), channel_id=1, source_target_pairs={{0,2},{1,3},{2,0},{3,1},{4,6},{5,7},{6,4},{7,5},{8,10},{9,11},{10,... | collective-permute-start | bytes 221192 | tf_op jit(solution)/shard_map/ppermute | solution.py:241
  61.4 1.1 %collective-permute-start.17 = (bf16[48,768]{1,0:T(8,128)(2,1)S(1)}, bf16[48,768]{1,0:T(8,128)(2,1)S(1)}, u32[]{:S(2)}, u32[]{:S(2)}) collective-permute-start(bf16[48,768]{1,0:T(8,128)(2,1)S(1)} %get-tuple-element.25), channel_id=1, source_target_pairs={{0,2},{1,3},{2,0},{3,1},{4,6},{5,7},{6,4},{7,5},{8,10},{9,11},{10,... | collective-permute-start | bytes 221192 | tf_op jit(solution)/shard_map/ppermute | solution.py:241
  62.4 1.0 %collective-permute-start.19 = (bf16[48,768]{1,0:T(8,128)(2,1)S(1)}, bf16[48,768]{1,0:T(8,128)(2,1)S(1)}, u32[]{:S(2)}, u32[]{:S(2)}) collective-permute-start(bf16[48,768]{1,0:T(8,128)(2,1)S(1)} %get-tuple-element.24), channel_id=1, source_target_pairs={{0,2},{1,3},{2,0},{3,1},{4,6},{5,7},{6,4},{7,5},{8,10},{9,11},{10,... | collective-permute-start | bytes 221192 | tf_op jit(solution)/shard_map/ppermute | solution.py:241
  63.4 1.0 %collective-permute-start.21 = (bf16[48,768]{1,0:T(8,128)(2,1)S(1)}, bf16[48,768]{1,0:T(8,128)(2,1)S(1)}, u32[]{:S(2)}, u32[]{:S(2)}) collective-permute-start(bf16[48,768]{1,0:T(8,128)(2,1)S(1)} %get-tuple-element.23), channel_id=1, source_target_pairs={{0,2},{1,3},{2,0},{3,1},{4,6},{5,7},{6,4},{7,5},{8,10},{9,11},{10,... | collective-permute-start | bytes 221192 | tf_op jit(solution)/shard_map/ppermute | solution.py:241
  64.5 1.1 %collective-permute-done.16 = bf16[48,768]{1,0:T(8,128)(2,1)S(1)} collective-permute-done((bf16[48,768]{1,0:T(8,128)(2,1)S(1)}, bf16[48,768]{1,0:T(8,128)(2,1)S(1)}, u32[]{:S(2)}, u32[]{:S(2)}) %collective-permute-start.16) | collective-permute-done | bytes 73760 | tf_op jit(solution)/shard_map/ppermute | solution.py:241
  65.5 1.6 %collective-permute-done.17 = bf16[48,768]{1,0:T(8,128)(2,1)S(1)} collective-permute-done((bf16[48,768]{1,0:T(8,128)(2,1)S(1)}, bf16[48,768]{1,0:T(8,128)(2,1)S(1)}, u32[]{:S(2)}, u32[]{:S(2)}) %collective-permute-start.17) | collective-permute-done | bytes 73760 | tf_op jit(solution)/shard_map/ppermute | solution.py:241
  67.1 1.6 %collective-permute-done.19 = bf16[48,768]{1,0:T(8,128)(2,1)S(1)} collective-permute-done((bf16[48,768]{1,0:T(8,128)(2,1)S(1)}, bf16[48,768]{1,0:T(8,128)(2,1)S(1)}, u32[]{:S(2)}, u32[]{:S(2)}) %collective-permute-start.19) | collective-permute-done | bytes 73760 | tf_op jit(solution)/shard_map/ppermute | solution.py:241
  68.7 0.8 collective-permute-done.21
  69.6 3.3 %collective-permute-start.18 = (bf16[48,768]{1,0:T(8,128)(2,1)S(1)}, bf16[48,768]{1,0:T(8,128)(2,1)S(1)}, u32[]{:S(2)}, u32[]{:S(2)}) collective-permute-start(bf16[48,768]{1,0:T(8,128)(2,1)S(1)} %get-tuple-element.21), channel_id=1, source_target_pairs={{0,12},{1,13},{2,14},{3,15},{4,0},{5,1},{6,2},{7,3},{8,4},{9,5},{1... | collective-permute-start | bytes 221192 | tf_op jit(solution)/shard_map/ppermute | solution.py:238
  72.8 1.2 %collective-permute-start.22 = (bf16[48,768]{1,0:T(8,128)(2,1)S(1)}, bf16[48,768]{1,0:T(8,128)(2,1)S(1)}, u32[]{:S(2)}, u32[]{:S(2)}) collective-permute-start(bf16[48,768]{1,0:T(8,128)(2,1)S(1)} %get-tuple-element.19), channel_id=1, source_target_pairs={{0,4},{1,5},{2,6},{3,7},{4,8},{5,9},{6,10},{7,11},{8,12},{9,13},{1... | collective-permute-start | bytes 221192 | tf_op jit(solution)/shard_map/ppermute | solution.py:238
  74.2 1.3 %collective-permute-done.18.m1_ref = bf16[48,768]{1,0:T(8,128)(2,1)S(1)} collective-permute-done((bf16[48,768]{1,0:T(8,128)(2,1)S(1)}, bf16[48,768]{1,0:T(8,128)(2,1)S(1)}, u32[]{:S(2)}, u32[]{:S(2)}) %collective-permute-start.18) | collective-permute-done | bytes 73760 | tf_op jit(solution)/shard_map/ppermute | solution.py:238
  75.5 3.8 %collective-permute-done.20.m2_ref = bf16[48,768]{1,0:T(8,128)(2,1)S(1)} collective-permute-done((bf16[48,768]{1,0:T(8,128)(2,1)S(1)}, bf16[48,768]{1,0:T(8,128)(2,1)S(1)}, u32[]{:S(2)}, u32[]{:S(2)}) %collective-permute-start.20) | collective-permute-done | bytes 73760 | tf_op jit(solution)/shard_map/ppermute | solution.py:238
  79.3 0.9 %mix.1 = bf16[16,3072]{1,0:T(8,128)(2,1)} custom-call(bf16[16,3072]{1,0:T(8,128)(2,1)S(1)} %get-tuple-element.12.hid_ref, bf16[192,128]{1,0:T(8,128)(2,1)S(1)} %blend.1.blend_ref, bf16[48,768]{1,0:T(8,128)(2,1)S(1)} %get-tuple-element.22.m0_ref, bf16[48,768]{1,0:T(8,128)(2,1)S(1)} %collective-permute-done.18.m1_ref, ...), custom_call_target="tpu_custom_call" | custom-call | tf_op jit(solution)/shard_map/mix/pallas_call | solution.py:285
  (51 shorter events, 6.9 us)
Async XLA Ops:
  0.7 1.4 %copy-start.7 = (bf16[16,96,512]{2,1,0:T(8,128)(2,1)S(1)}, bf16[16,96,512]{2,1,0:T(8,128)(2,1)}, u32[]{:S(2)}) copy-start(bf16[16,96,512]{2,1,0:T(8,128)(2,1)} %k_hbm.1) | copy-start | bytes 4718596
  2.1 1.4 %copy-start.8 = (bf16[16,96,512]{2,1,0:T(8,128)(2,1)S(1)}, bf16[16,96,512]{2,1,0:T(8,128)(2,1)}, u32[]{:S(2)}) copy-start(bf16[16,96,512]{2,1,0:T(8,128)(2,1)} %v_hbm.1) | copy-start | bytes 4718596
  3.5 0.9 %copy-start.9 = (bf16[16,3072]{1,0:T(8,128)(2,1)S(1)}, bf16[16,3072]{1,0:T(8,128)(2,1)}, u32[]{:S(2)}) copy-start(bf16[16,3072]{1,0:T(8,128)(2,1)} %q_ref.1) | copy-start | bytes 294916
  8.1 27.2 %copy-start.3 = (bf16[192,192]{1,0:T(8,128)(2,1)S(1)}, bf16[192,192]{1,0:T(8,128)(2,1)}, u32[]{:S(2)}) copy-start(bf16[192,192]{1,0:T(8,128)(2,1)} %constant.22.clone.refs_16_.refs_17_) | copy-start | bytes 221188
  16.8 8.5 %collective-permute-start = (bf16[48,768]{1,0:T(8,128)(2,1)S(1)}, bf16[48,768]{1,0:T(8,128)(2,1)S(1)}, u32[]{:S(2)}, u32[]{:S(2)}) collective-permute-start(bf16[48,768]{1,0:T(8,128)(2,1)S(1)} %get-tuple-element.14), channel_id=1, source_target_pairs={{0,4},{1,5},{2,6},{3,7},{4,8},{5,9},{6,10},{7,11},{8,12},{9,13},{1... | collective-permute-start | bytes 221192 | tf_op jit(solution)/shard_map/ppermute | solution.py:238
  19.8 7.5 %collective-permute-start.1 = (bf16[48,768]{1,0:T(8,128)(2,1)S(1)}, bf16[48,768]{1,0:T(8,128)(2,1)S(1)}, u32[]{:S(2)}, u32[]{:S(2)}) collective-permute-start(bf16[48,768]{1,0:T(8,128)(2,1)S(1)} %get-tuple-element.15), channel_id=1, source_target_pairs={{0,8},{1,9},{2,10},{3,11},{4,12},{5,13},{6,14},{7,15},{8,0},{9,1},... | collective-permute-start | bytes 221192 | tf_op jit(solution)/shard_map/ppermute | solution.py:238
  22.4 6.7 %collective-permute-start.2 = (bf16[48,768]{1,0:T(8,128)(2,1)S(1)}, bf16[48,768]{1,0:T(8,128)(2,1)S(1)}, u32[]{:S(2)}, u32[]{:S(2)}) collective-permute-start(bf16[48,768]{1,0:T(8,128)(2,1)S(1)} %get-tuple-element.16), channel_id=1, source_target_pairs={{0,12},{1,13},{2,14},{3,15},{4,0},{5,1},{6,2},{7,3},{8,4},{9,5},{1... | collective-permute-start | bytes 221192 | tf_op jit(solution)/shard_map/ppermute | solution.py:238
  23.8 5.6 %collective-permute-start.3 = (bf16[48,768]{1,0:T(8,128)(2,1)S(1)}, bf16[48,768]{1,0:T(8,128)(2,1)S(1)}, u32[]{:S(2)}, u32[]{:S(2)}) collective-permute-start(bf16[48,768]{1,0:T(8,128)(2,1)S(1)} %get-tuple-element.13.refs_0_), channel_id=1, source_target_pairs={{0,2},{1,3},{2,0},{3,1},{4,6},{5,7},{6,4},{7,5},{8,10},{9,11},{10,... | collective-permute-start | bytes 221192 | tf_op jit(solution)/shard_map/ppermute | solution.py:241
  25.3 4.1 %collective-permute-start.7 = (bf16[48,768]{1,0:T(8,128)(2,1)S(1)}, bf16[48,768]{1,0:T(8,128)(2,1)S(1)}, u32[]{:S(2)}, u32[]{:S(2)}) collective-permute-start(bf16[48,768]{1,0:T(8,128)(2,1)S(1)} %get-tuple-element.13.refs_0_), channel_id=1, source_target_pairs={{0,1},{1,0},{2,3},{3,2},{4,5},{5,4},{6,7},{7,6},{8,9},{9,8},{10,11... | collective-permute-start | bytes 221192 | tf_op jit(solution)/shard_map/ppermute | solution.py:241
  25.3 4.8 %collective-permute-start.4 = (bf16[48,768]{1,0:T(8,128)(2,1)S(1)}, bf16[48,768]{1,0:T(8,128)(2,1)S(1)}, u32[]{:S(2)}, u32[]{:S(2)}) collective-permute-start(bf16[48,768]{1,0:T(8,128)(2,1)S(1)} %collective-permute-done.refs_1_), channel_id=1, source_target_pairs={{0,2},{1,3},{2,0},{3,1},{4,6},{5,7},{6,4},{7,5},{8,10},{9,11},{10,... | collective-permute-start | bytes 221192 | tf_op jit(solution)/shard_map/ppermute | solution.py:241
  27.4 5.1 %collective-permute-start.5 = (bf16[48,768]{1,0:T(8,128)(2,1)S(1)}, bf16[48,768]{1,0:T(8,128)(2,1)S(1)}, u32[]{:S(2)}, u32[]{:S(2)}) collective-permute-start(bf16[48,768]{1,0:T(8,128)(2,1)S(1)} %collective-permute-done.1.refs_2_), channel_id=1, source_target_pairs={{0,2},{1,3},{2,0},{3,1},{4,6},{5,7},{6,4},{7,5},{8,10},{9,11},{10,... | collective-permute-start | bytes 221192 | tf_op jit(solution)/shard_map/ppermute | solution.py:241
  29.1 4.4 %collective-permute-start.6 = (bf16[48,768]{1,0:T(8,128)(2,1)S(1)}, bf16[48,768]{1,0:T(8,128)(2,1)S(1)}, u32[]{:S(2)}, u32[]{:S(2)}) collective-permute-start(bf16[48,768]{1,0:T(8,128)(2,1)S(1)} %collective-permute-done.2.refs_3_), channel_id=1, source_target_pairs={{0,2},{1,3},{2,0},{3,1},{4,6},{5,7},{6,4},{7,5},{8,10},{9,11},{10,... | collective-permute-start | bytes 221192 | tf_op jit(solution)/shard_map/ppermute | solution.py:241
  29.4 4.0 %collective-permute-start.11 = (bf16[48,768]{1,0:T(8,128)(2,1)S(1)}, bf16[48,768]{1,0:T(8,128)(2,1)S(1)}, u32[]{:S(2)}, u32[]{:S(2)}) collective-permute-start(bf16[48,768]{1,0:T(8,128)(2,1)S(1)} %collective-permute-done.3.refs_4_), channel_id=1, source_target_pairs={{0,1},{1,0},{2,3},{3,2},{4,5},{5,4},{6,7},{7,6},{8,9},{9,8},{10,11... | collective-permute-start | bytes 221192 | tf_op jit(solution)/shard_map/ppermute | solution.py:241
  29.4 4.5 %collective-permute-start.10 = (bf16[48,768]{1,0:T(8,128)(2,1)S(1)}, bf16[48,768]{1,0:T(8,128)(2,1)S(1)}, u32[]{:S(2)}, u32[]{:S(2)}) collective-permute-start(bf16[48,768]{1,0:T(8,128)(2,1)S(1)} %collective-permute-done.2.refs_3_), channel_id=1, source_target_pairs={{0,1},{1,0},{2,3},{3,2},{4,5},{5,4},{6,7},{7,6},{8,9},{9,8},{10,11... | collective-permute-start | bytes 221192 | tf_op jit(solution)/shard_map/ppermute | solution.py:241
  30.1 4.0 %collective-permute-start.8 = (bf16[48,768]{1,0:T(8,128)(2,1)S(1)}, bf16[48,768]{1,0:T(8,128)(2,1)S(1)}, u32[]{:S(2)}, u32[]{:S(2)}) collective-permute-start(bf16[48,768]{1,0:T(8,128)(2,1)S(1)} %collective-permute-done.refs_1_), channel_id=1, source_target_pairs={{0,1},{1,0},{2,3},{3,2},{4,5},{5,4},{6,7},{7,6},{8,9},{9,8},{10,11... | collective-permute-start | bytes 221192 | tf_op jit(solution)/shard_map/ppermute | solution.py:241
  32.5 1.5 %collective-permute-start.9 = (bf16[48,768]{1,0:T(8,128)(2,1)S(1)}, bf16[48,768]{1,0:T(8,128)(2,1)S(1)}, u32[]{:S(2)}, u32[]{:S(2)}) collective-permute-start(bf16[48,768]{1,0:T(8,128)(2,1)S(1)} %collective-permute-done.1.refs_2_), channel_id=1, source_target_pairs={{0,1},{1,0},{2,3},{3,2},{4,5},{5,4},{6,7},{7,6},{8,9},{9,8},{10,11... | collective-permute-start | bytes 221192 | tf_op jit(solution)/shard_map/ppermute | solution.py:241
  33.5 1.3 %collective-permute-start.12 = (bf16[48,768]{1,0:T(8,128)(2,1)S(1)}, bf16[48,768]{1,0:T(8,128)(2,1)S(1)}, u32[]{:S(2)}, u32[]{:S(2)}) collective-permute-start(bf16[48,768]{1,0:T(8,128)(2,1)S(1)} %collective-permute-done.4.refs_5_), channel_id=1, source_target_pairs={{0,1},{1,0},{2,3},{3,2},{4,5},{5,4},{6,7},{7,6},{8,9},{9,8},{10,11... | collective-permute-start | bytes 221192 | tf_op jit(solution)/shard_map/ppermute | solution.py:241
  33.5 1.4 %collective-permute-start.13 = (bf16[48,768]{1,0:T(8,128)(2,1)S(1)}, bf16[48,768]{1,0:T(8,128)(2,1)S(1)}, u32[]{:S(2)}, u32[]{:S(2)}) collective-permute-start(bf16[48,768]{1,0:T(8,128)(2,1)S(1)} %collective-permute-done.5.refs_6_), channel_id=1, source_target_pairs={{0,1},{1,0},{2,3},{3,2},{4,5},{5,4},{6,7},{7,6},{8,9},{9,8},{10,11... | collective-permute-start | bytes 221192 | tf_op jit(solution)/shard_map/ppermute | solution.py:241
  34.0 1.3 %collective-permute-start.14 = (bf16[48,768]{1,0:T(8,128)(2,1)S(1)}, bf16[48,768]{1,0:T(8,128)(2,1)S(1)}, u32[]{:S(2)}, u32[]{:S(2)}) collective-permute-start(bf16[48,768]{1,0:T(8,128)(2,1)S(1)} %collective-permute-done.6.refs_7_), channel_id=1, source_target_pairs={{0,1},{1,0},{2,3},{3,2},{4,5},{5,4},{6,7},{7,6},{8,9},{9,8},{10,11... | collective-permute-start | bytes 221192 | tf_op jit(solution)/shard_map/ppermute | solution.py:241
  35.2 4.6 %copy-start = (bf16[3072,2048]{1,0:T(8,128)(2,1)S(1)}, bf16[3072,2048]{1,0:T(8,128)(2,1)}, u32[]{:S(2)}) copy-start(bf16[3072,2048]{1,0:T(8,128)(2,1)} %refs_18_.1) | copy-start | bytes 37748740
  39.8 4.6 %copy-start.1 = (bf16[3072,2048]{1,0:T(8,128)(2,1)S(1)}, bf16[3072,2048]{1,0:T(8,128)(2,1)}, u32[]{:S(2)}) copy-start(bf16[3072,2048]{1,0:T(8,128)(2,1)} %refs_19_.1) | copy-start | bytes 37748740
  44.4 4.6 %copy-start.2 = (bf16[2048,3072]{1,0:T(8,128)(2,1)S(1)}, bf16[2048,3072]{1,0:T(8,128)(2,1)}, u32[]{:S(2)}) copy-start(bf16[2048,3072]{1,0:T(8,128)(2,1)} %refs_20_.1) | copy-start | bytes 37748740
  58.0 2.2 %collective-permute-start.15 = (bf16[384,768]{1,0:T(8,128)(2,1)}, bf16[384,768]{1,0:T(8,128)(2,1)S(1)}, u32[]{:S(2)}, u32[]{:S(2)}) collective-permute-start(bf16[384,768]{1,0:T(8,128)(2,1)} %get-tuple-element.18), channel_id=1, source_target_pairs={{0,1},{1,0},{2,3},{3,2},{4,5},{5,4},{6,7},{7,6},{8,9},{9,8},{10,11... | collective-permute-start | bytes 1769480 | tf_op jit(solution)/shard_map/ppermute | solution.py:241
  60.2 13.8 %copy-start.5 = (s32[16,2]{0,1:T(2,128)S(1)}, s32[16,2]{0,1:T(2,128)}, u32[]{:S(2)}) copy-start(s32[16,2]{0,1:T(2,128)} %param.23) | copy-start | bytes 388
  60.2 13.8 %copy-start.6 = (s32[16,2]{0,1:T(2,128)S(1)}, s32[16,2]{0,1:T(2,128)}, u32[]{:S(2)}) copy-start(s32[16,2]{0,1:T(2,128)} %param.24) | copy-start | bytes 388
  60.4 5.2 %collective-permute-start.16 = (bf16[48,768]{1,0:T(8,128)(2,1)S(1)}, bf16[48,768]{1,0:T(8,128)(2,1)S(1)}, u32[]{:S(2)}, u32[]{:S(2)}) collective-permute-start(bf16[48,768]{1,0:T(8,128)(2,1)S(1)} %get-tuple-element.26), channel_id=1, source_target_pairs={{0,2},{1,3},{2,0},{3,1},{4,6},{5,7},{6,4},{7,5},{8,10},{9,11},{10,... | collective-permute-start | bytes 221192 | tf_op jit(solution)/shard_map/ppermute | solution.py:241
  61.4 5.7 %collective-permute-start.17 = (bf16[48,768]{1,0:T(8,128)(2,1)S(1)}, bf16[48,768]{1,0:T(8,128)(2,1)S(1)}, u32[]{:S(2)}, u32[]{:S(2)}) collective-permute-start(bf16[48,768]{1,0:T(8,128)(2,1)S(1)} %get-tuple-element.25), channel_id=1, source_target_pairs={{0,2},{1,3},{2,0},{3,1},{4,6},{5,7},{6,4},{7,5},{8,10},{9,11},{10,... | collective-permute-start | bytes 221192 | tf_op jit(solution)/shard_map/ppermute | solution.py:241
  62.4 6.2 %collective-permute-start.19 = (bf16[48,768]{1,0:T(8,128)(2,1)S(1)}, bf16[48,768]{1,0:T(8,128)(2,1)S(1)}, u32[]{:S(2)}, u32[]{:S(2)}) collective-permute-start(bf16[48,768]{1,0:T(8,128)(2,1)S(1)} %get-tuple-element.24), channel_id=1, source_target_pairs={{0,2},{1,3},{2,0},{3,1},{4,6},{5,7},{6,4},{7,5},{8,10},{9,11},{10,... | collective-permute-start | bytes 221192 | tf_op jit(solution)/shard_map/ppermute | solution.py:241
  63.4 6.1 %collective-permute-start.21 = (bf16[48,768]{1,0:T(8,128)(2,1)S(1)}, bf16[48,768]{1,0:T(8,128)(2,1)S(1)}, u32[]{:S(2)}, u32[]{:S(2)}) collective-permute-start(bf16[48,768]{1,0:T(8,128)(2,1)S(1)} %get-tuple-element.23), channel_id=1, source_target_pairs={{0,2},{1,3},{2,0},{3,1},{4,6},{5,7},{6,4},{7,5},{8,10},{9,11},{10,... | collective-permute-start | bytes 221192 | tf_op jit(solution)/shard_map/ppermute | solution.py:241
  69.6 5.9 %collective-permute-start.18 = (bf16[48,768]{1,0:T(8,128)(2,1)S(1)}, bf16[48,768]{1,0:T(8,128)(2,1)S(1)}, u32[]{:S(2)}, u32[]{:S(2)}) collective-permute-start(bf16[48,768]{1,0:T(8,128)(2,1)S(1)} %get-tuple-element.21), channel_id=1, source_target_pairs={{0,12},{1,13},{2,14},{3,15},{4,0},{5,1},{6,2},{7,3},{8,4},{9,5},{1... | collective-permute-start | bytes 221192 | tf_op jit(solution)/shard_map/ppermute | solution.py:238
  72.8 6.5 %collective-permute-start.20 = (bf16[48,768]{1,0:T(8,128)(2,1)S(1)}, bf16[48,768]{1,0:T(8,128)(2,1)S(1)}, u32[]{:S(2)}, u32[]{:S(2)}) collective-permute-start(bf16[48,768]{1,0:T(8,128)(2,1)S(1)} %get-tuple-element.20), channel_id=1, source_target_pairs={{0,8},{1,9},{2,10},{3,11},{4,12},{5,13},{6,14},{7,15},{8,0},{9,1},... | collective-permute-start | bytes 221192 | tf_op jit(solution)/shard_map/ppermute | solution.py:238
  72.8 6.5 %collective-permute-start.22 = (bf16[48,768]{1,0:T(8,128)(2,1)S(1)}, bf16[48,768]{1,0:T(8,128)(2,1)S(1)}, u32[]{:S(2)}, u32[]{:S(2)}) collective-permute-start(bf16[48,768]{1,0:T(8,128)(2,1)S(1)} %get-tuple-element.19), channel_id=1, source_target_pairs={{0,4},{1,5},{2,6},{3,7},{4,8},{5,9},{6,10},{7,11},{8,12},{9,13},{1... | collective-permute-start | bytes 221192 | tf_op jit(solution)/shard_map/ppermute | solution.py:238
  (6 other events, 4.4 us)

commit v2 on v1

--- a/solution.py
+++ b/solution.py
@@ -55,22 +55,40 @@
 
 
 def attention_kernel(
-    plane_ref, len_ref, q_ref, res_ref, k_hbm, v_hbm, nk_ref, nv_ref, gain_ref, ids_ref,
-    hid_ref, b0_ref, b1_ref, b2_ref, b3_ref,
-    k_ref, v_ref, q_scr, o_scr, sems,
+    plane_ref, *refs
 ):
+    operands, outs, scratch = refs[:9], refs[9:14], refs[14:]
+    len_hbm, q_hbm, res_hbm, k_hbm, v_hbm, nk_hbm, nv_hbm, gain_hbm, ids_hbm = operands
+    hid_ref, *block_refs = outs
+    len_ref, q_ref, res_ref, k_ref, v_ref, nk_ref, nv_ref, gain_ref, ids_ref, q_scr, o_scr, sems, small = scratch
     parts = sems.shape[1]
     step = ROWS // parts
+
+    def fetch(source, target, sem):
+        copy = pltpu.make_async_copy(source, target, sem)
+        copy.start()
+        return copy
+
+    early = [
+        fetch(q_hbm, q_ref, small.at[0]),
+        fetch(nk_hbm, nk_ref, small.at[1]),
+        fetch(nv_hbm, nv_ref, small.at[2]),
+        fetch(len_hbm, len_ref, small.at[3]),
+    ]
     copies = []
     for c in range(parts):
         own = pl.ds(c * step, step)
-        pair = (
-            pltpu.make_async_copy(k_hbm.at[own], k_ref.at[own], sems.at[0, c]),
-            pltpu.make_async_copy(v_hbm.at[own], v_ref.at[own], sems.at[1, c]),
-        )
-        for copy in pair:
-            copy.start()
-        copies.append(pair)
+        copies.append((
+            fetch(k_hbm.at[own], k_ref.at[own], sems.at[0, c]),
+            fetch(v_hbm.at[own], v_ref.at[own], sems.at[1, c]),
+        ))
+    late = [
+        fetch(res_hbm, res_ref, small.at[4]),
+        fetch(gain_hbm, gain_ref, small.at[5]),
+        fetch(ids_hbm, ids_ref, small.at[6]),
+    ]
+    for copy in early:
+        copy.wait()
     for h in range(Q_HEADS):
         q_scr[pl.ds(h, ROWS, stride=Q_HEADS), :] = q_ref[:, h * HEAD : (h + 1) * HEAD].astype(F32)
     row, col = iota((Q_HEADS, KV_HEADS * HEAD), 0), iota((Q_HEADS, KV_HEADS * HEAD), 1)
@@ -101,6 +119,8 @@
         for k in range(1, KV_HEADS):
             picked = jnp.where(head_row >= GROUP * k, o[:, k * HEAD : (k + 1) * HEAD], picked)
         o_scr[t * Q_HEADS : (t + 1) * Q_HEADS, :] = picked
+    for copy in late:
+        copy.wait()
     squares = jnp.zeros((ROWS, HEAD), F32)
     hidden = []
     for h in range(Q_HEADS):
@@ -122,7 +142,7 @@
         chunks.append(jnp.concatenate(heads, axis=1))
     stacked = jnp.concatenate(chunks, axis=0)
     slot, _, _, _ = slots_of(plane_ref[0], ids_ref)
-    for s, out in enumerate((b0_ref, b1_ref, b2_ref, b3_ref)):
+    for s, out in enumerate(block_refs):
         picker = jnp.where(matching(slot, s), 1.0, 0.0).astype(BF16)
         out[...] = jnp.dot(picker, stacked, preferred_element_type=F32).astype(BF16)
 
@@ -186,11 +206,50 @@
 
 VMEM = pl.BlockSpec(memory_space=pltpu.VMEM)
 SMEM = pl.BlockSpec(memory_space=pltpu.SMEM)
-HBM = pl.BlockSpec(memory_space=pl.ANY)
+HBM = pl.BlockSpec(memory_space=pltpu.HBM)
 
 
 def params(mib):
     return pltpu.CompilerParams(vmem_limit_bytes=mib * MIB)
+
+
+def attention(plane, *operands):
+    width, kv_width = operands[1].shape[1], operands[3].shape[2]
+    block = jax.ShapeDtypeStruct((PACK, width // FEAT), BF16)
+    pinned = [pltpu.with_memory_space_constraint(x, pltpu.HBM) for x in operands]
+    return pl.pallas_call(
+        attention_kernel,
+        out_shape=[jax.ShapeDtypeStruct((ROWS, width), BF16)] + [block] * EXPERTS,
+        in_specs=[SMEM] + [HBM] * len(operands),
+        out_specs=[VMEM] * (1 + EXPERTS),
+        scratch_shapes=[pltpu.SMEM(operands[0].shape, I32)]
+        + [pltpu.VMEM(x.shape, x.dtype) for x in operands[1:]]
+        + [
+            pltpu.VMEM((ROWS * Q_HEADS, HEAD), F32),
+            pltpu.VMEM((ROWS * Q_HEADS, HEAD), F32),
+            pltpu.SemaphoreType.DMA((2, 4)),
+            pltpu.SemaphoreType.DMA((7,)),
+        ],
+        compiler_params=params(6),
+        cost_estimate=pl.CostEstimate(flops=40 * 10**9, bytes_accessed=4 * 10**6, transcendentals=0),
+        name="attention",
+    )(plane, *pinned)
+
+
+def add_kernel(at, keep_ref, came_ref, out_ref):
+    rows = out_ref.shape[0]
+    out_ref[...] = (keep_ref[at : at + rows, :].astype(F32) + came_ref[...].astype(F32)).astype(BF16)
+
+
+def add_block(keep, came, at):
+    return pl.pallas_call(
+        functools.partial(add_kernel, at),
+        out_shape=jax.ShapeDtypeStruct(came.shape, BF16),
+        in_specs=[VMEM] * 2,
+        out_specs=VMEM,
+        compiler_params=params(4),
+        name="add_block",
+    )(keep, came)
 
 
 def local(
@@ -201,27 +260,9 @@
     splits = devices // EXPERTS
     width = queries.shape[1]
     part = width // FEAT
-    kv_width = key_cache.shape[2]
     plane = (lax.axis_index("attn") // splits).astype(I32).reshape(1)
     ids, gates = expert_ids.T, gate_fixed.T
-    block = jax.ShapeDtypeStruct((PACK, part), BF16)
-
-    hidden, *blocks = pl.pallas_call(
-        attention_kernel,
-        out_shape=[jax.ShapeDtypeStruct((ROWS, width), BF16)] + [block] * EXPERTS,
-        in_specs=[SMEM, SMEM, VMEM, VMEM, HBM, HBM, VMEM, VMEM, VMEM, VMEM],
-        out_specs=[VMEM] * (1 + EXPERTS),
-        scratch_shapes=[
-            pltpu.VMEM((ROWS, CACHE, kv_width), BF16),
-            pltpu.VMEM((ROWS, CACHE, kv_width), BF16),
-            pltpu.VMEM((ROWS * Q_HEADS, HEAD), F32),
-            pltpu.VMEM((ROWS * Q_HEADS, HEAD), F32),
-            pltpu.SemaphoreType.DMA((2, 4)),
-        ],
-        compiler_params=params(14),
-        cost_estimate=pl.CostEstimate(flops=10**9, bytes_accessed=20 * 10**6, transcendentals=0),
-        name="attention",
-    )(
+    hidden, *blocks = attention(
         plane, cache_len, queries, residual, key_cache, value_cache, new_keys, new_values,
         norm_gain.reshape(1, width), ids,
     )
@@ -277,10 +318,12 @@
     while rows > EXPERTS * PACK * 2:
         keep = plus(keep[: rows // 2], swapped(keep[rows // 2 :], bit))
         rows, bit = rows // 2, bit * 2
-    summed = [
-        plus(keep[s * PACK : (s + 1) * PACK], swapped(keep[rows // 2 + s * PACK : rows // 2 + (s + 1) * PACK], bit))
-        for s in range(EXPERTS)
-    ]
+    summed = [None] * EXPERTS
+    came = {}
+    for s in (2, 1, 3, 0):
+        came[s] = swapped(keep[rows // 2 + s * PACK : rows // 2 + (s + 1) * PACK], bit)
+    for s in (2, 1, 3, 0):
+        summed[s] = add_block(keep, came[s], s * PACK)
     mine = [summed[0]] + [shifted(summed[s], -s) for s in range(1, EXPERTS)]
     return pl.pallas_call(
         mix_kernel,

time: 80.7 us -> 53.1 us (0.66)
  local copies, waits for them, and re-layouts: 21.8 us -> 0.08 us
  waiting for transfers between devices: 17.8 us -> 12.1 us
    unnamed x30 -> x24, local copies, waits for them, and re-layouts: 21.8 us -> 0.06 us
    ppermute x6, waiting for transfers between devices: 6.03 us -> 2.98 us  [shifted(): lax.ppermute(x, 'attn', [(i, (i + s * splits) % devices) for i in range(d...]
    ppermute x17, waiting for transfers between devices: 11.8 us -> 9.17 us  [swapped(): return lax.ppermute(x, 'attn', [(i, i ^ bit) for i in range(devices)])]
    pallas_call x1 -> x5, Pallas kernels: 8.67 us -> 8.1 us  [the longest x1 8.02 us: attention(): pl.pallas_call(attention_kernel, out_shape=[jax.ShapeDtypeStruct((ROWS, w...]
  transfers between devices with their start and end apart: 23 -> 23, of which waited for: 14 -> 12; matrix products, arithmetic and copies ran while one was open for 0% -> 0% of each run, Pallas kernels for 0% -> 1%
where the time goes in v2:
time: 53.1 us; the launch traced here: 53 us
  starting transfers between devices  22.1 us (42%)
  Pallas kernels  18.2 us (34%)
  waiting for transfers between devices  12.1 us (23%)
    ppermute x6, starting transfers between devices, shifted(): lax.ppermute(x, 'attn', [(i, (i + s * splits) % devices) for i in range(d...  12.1 us
    ppermute x17, starting transfers between devices, swapped(): return lax.ppermute(x, 'attn', [(i, i ^ bit) for i in range(devices)])  10.1 us
    ppermute x17, waiting for transfers between devices, swapped(): return lax.ppermute(x, 'attn', [(i, i ^ bit) for i in range(devices)])  9.17 us
    pallas_call x1, Pallas kernels, local(): pl.pallas_call(functools.partial(experts_kernel, splits), out_shape=[jax....  9.02 us
    pallas_call x1, Pallas kernels, attention(): pl.pallas_call(attention_kernel, out_shape=[jax.ShapeDtypeStruct((ROWS, w...  8.02 us
    ppermute x6, waiting for transfers between devices, shifted(): lax.ppermute(x, 'attn', [(i, (i + s * splits) % devices) for i in range(d...  2.98 us
  transfers between devices with their start and end apart: 23, of which 12 were waited for; matrix products, arithmetic and copies ran while one was open for 0% of the time, Pallas kernels for 1%

profile of v2, /device:TPU:0, one launch (start us, length us, event | category | flops | bytes accessed | tf_op | source)
XLA Modules:
  0.0 53.0 jit_solution(10961755152839123797)
XLA Ops:
  0.1 8.0 %attention.1 = (bf16[16,3072]{1,0:T(8,128)(2,1)S(1)}, bf16[48,768]{1,0:T(8,128)(2,1)S(1)}, bf16[48,768]{1,0:T(8,128)(2,1)S(1)}, bf16[48,768]{1,0:T(8,128)(2,1)S(1)}, bf16[48,768]{1,0:T(8,128)(2,1)S(1)}) custom-call(s32[1]{0:T(128)} %bitcast.plane_ref, s32[16]{0:T(128)} %refs_0_.1, bf16[16,3072]{1,0:T(8,128)(2,1)} %refs_1_.1, bf16[16,3072]{1,0:T(8,128)(2,1)} %refs_2_.1, ...), custom_call_target="tpu_custom_call" | custom-call | flops 40000000000 | bytes 4000000 | tf_op jit(solution)/shard_map/attention/pallas_call | solution.py:220
  8.1 3.1 %collective-permute-start = (bf16[48,768]{1,0:T(8,128)(2,1)S(1)}, bf16[48,768]{1,0:T(8,128)(2,1)S(1)}, u32[]{:S(2)}, u32[]{:S(2)}) collective-permute-start(bf16[48,768]{1,0:T(8,128)(2,1)S(1)} %get-tuple-element.14), channel_id=1, source_target_pairs={{0,4},{1,5},{2,6},{3,7},{4,8},{5,9},{6,10},{7,11},{8,12},{9,13},{1... | collective-permute-start | bytes 221192 | tf_op jit(solution)/shard_map/ppermute | solution.py:279
  11.2 2.6 %collective-permute-start.1 = (bf16[48,768]{1,0:T(8,128)(2,1)S(1)}, bf16[48,768]{1,0:T(8,128)(2,1)S(1)}, u32[]{:S(2)}, u32[]{:S(2)}) collective-permute-start(bf16[48,768]{1,0:T(8,128)(2,1)S(1)} %get-tuple-element.15), channel_id=1, source_target_pairs={{0,8},{1,9},{2,10},{3,11},{4,12},{5,13},{6,14},{7,15},{8,0},{9,1},... | collective-permute-start | bytes 221192 | tf_op jit(solution)/shard_map/ppermute | solution.py:279
  13.8 1.4 %collective-permute-start.2 = (bf16[48,768]{1,0:T(8,128)(2,1)S(1)}, bf16[48,768]{1,0:T(8,128)(2,1)S(1)}, u32[]{:S(2)}, u32[]{:S(2)}) collective-permute-start(bf16[48,768]{1,0:T(8,128)(2,1)S(1)} %get-tuple-element.16), channel_id=1, source_target_pairs={{0,12},{1,13},{2,14},{3,15},{4,0},{5,1},{6,2},{7,3},{8,4},{9,5},{1... | collective-permute-start | bytes 221192 | tf_op jit(solution)/shard_map/ppermute | solution.py:279
  15.1 1.5 %collective-permute-start.3 = (bf16[48,768]{1,0:T(8,128)(2,1)S(1)}, bf16[48,768]{1,0:T(8,128)(2,1)S(1)}, u32[]{:S(2)}, u32[]{:S(2)}) collective-permute-start(bf16[48,768]{1,0:T(8,128)(2,1)S(1)} %get-tuple-element.13.refs_0_), channel_id=1, source_target_pairs={{0,2},{1,3},{2,0},{3,1},{4,6},{5,7},{6,4},{7,5},{8,10},{9,11},{10,... | collective-permute-start | bytes 221192 | tf_op jit(solution)/shard_map/ppermute | solution.py:282
  16.7 1.1 %collective-permute-start.4 = (bf16[48,768]{1,0:T(8,128)(2,1)S(1)}, bf16[48,768]{1,0:T(8,128)(2,1)S(1)}, u32[]{:S(2)}, u32[]{:S(2)}) collective-permute-start(bf16[48,768]{1,0:T(8,128)(2,1)S(1)} %collective-permute-done.refs_1_), channel_id=1, source_target_pairs={{0,2},{1,3},{2,0},{3,1},{4,6},{5,7},{6,4},{7,5},{8,10},{9,11},{10,... | collective-permute-start | bytes 221192 | tf_op jit(solution)/shard_map/ppermute | solution.py:282
  17.8 0.9 %collective-permute-done.1.refs_2_ = bf16[48,768]{1,0:T(8,128)(2,1)S(1)} collective-permute-done((bf16[48,768]{1,0:T(8,128)(2,1)S(1)}, bf16[48,768]{1,0:T(8,128)(2,1)S(1)}, u32[]{:S(2)}, u32[]{:S(2)}) %collective-permute-start.1) | collective-permute-done | bytes 73760 | tf_op jit(solution)/shard_map/ppermute | solution.py:279
  18.7 1.7 %collective-permute-start.5 = (bf16[48,768]{1,0:T(8,128)(2,1)S(1)}, bf16[48,768]{1,0:T(8,128)(2,1)S(1)}, u32[]{:S(2)}, u32[]{:S(2)}) collective-permute-start(bf16[48,768]{1,0:T(8,128)(2,1)S(1)} %collective-permute-done.1.refs_2_), channel_id=1, source_target_pairs={{0,2},{1,3},{2,0},{3,1},{4,6},{5,7},{6,4},{7,5},{8,10},{9,11},{10,... | collective-permute-start | bytes 221192 | tf_op jit(solution)/shard_map/ppermute | solution.py:282
  20.4 0.3 collective-permute-start.6
  20.8 0.5 collective-permute-start.10
  21.4 2.5 %collective-permute-done.5.refs_6_ = bf16[48,768]{1,0:T(8,128)(2,1)S(1)} collective-permute-done((bf16[48,768]{1,0:T(8,128)(2,1)S(1)}, bf16[48,768]{1,0:T(8,128)(2,1)S(1)}, u32[]{:S(2)}, u32[]{:S(2)}) %collective-permute-start.5) | collective-permute-done | bytes 73760 | tf_op jit(solution)/shard_map/ppermute | solution.py:282
  23.9 0.9 %collective-permute-done.6.refs_7_ = bf16[48,768]{1,0:T(8,128)(2,1)S(1)} collective-permute-done((bf16[48,768]{1,0:T(8,128)(2,1)S(1)}, bf16[48,768]{1,0:T(8,128)(2,1)S(1)}, u32[]{:S(2)}, u32[]{:S(2)}) %collective-permute-start.6) | collective-permute-done | bytes 73760 | tf_op jit(solution)/shard_map/ppermute | solution.py:282
  24.8 0.5 collective-permute-start.13
  25.4 0.7 %collective-permute-done.12.refs_13_ = bf16[48,768]{1,0:T(8,128)(2,1)S(1)} collective-permute-done((bf16[48,768]{1,0:T(8,128)(2,1)S(1)}, bf16[48,768]{1,0:T(8,128)(2,1)S(1)}, u32[]{:S(2)}, u32[]{:S(2)}) %collective-permute-start.12) | collective-permute-done | bytes 73760 | tf_op jit(solution)/shard_map/ppermute | solution.py:282
  26.1 0.2 collective-permute-done.13.refs_14_
  26.2 0.4 collective-permute-done.14.refs_15_
  26.7 9.0 %experts.1 = (bf16[384,768]{1,0:T(8,128)(2,1)S(1)}, bf16[384,768]{1,0:T(8,128)(2,1)}) custom-call(bf16[48,768]{1,0:T(8,128)(2,1)S(1)} %get-tuple-element.13.refs_0_, bf16[48,768]{1,0:T(8,128)(2,1)S(1)} %collective-permute-done.refs_1_, bf16[48,768]{1,0:T(8,128)(2,1)S(1)} %collective-permute-done.1.refs_2_, ...), custom_call_target="tpu_custom_call" | custom-call | flops 7247757312 | bytes 37748736 | tf_op jit(solution)/shard_map/experts/pallas_call | solution.py:296
  35.7 0.2 collective-permute-start.15
  35.9 2.1 %collective-permute-done.15 = bf16[384,768]{1,0:T(8,128)(2,1)S(1)} collective-permute-done((bf16[384,768]{1,0:T(8,128)(2,1)}, bf16[384,768]{1,0:T(8,128)(2,1)S(1)}, u32[]{:S(2)}, u32[]{:S(2)}) %collective-permute-start.15) | collective-permute-done | bytes 589856 | tf_op jit(solution)/shard_map/ppermute | solution.py:282
  37.9 0.1 add_convert_fusion.keep_ref
  38.1 1.0 %collective-permute-start.21 = (bf16[48,768]{1,0:T(8,128)(2,1)S(1)}, bf16[48,768]{1,0:T(8,128)(2,1)S(1)}, u32[]{:S(2)}, u32[]{:S(2)}) collective-permute-start(bf16[48,768]{1,0:T(8,128)(2,1)S(1)} %get-tuple-element.19), channel_id=1, source_target_pairs={{0,2},{1,3},{2,0},{3,1},{4,6},{5,7},{6,4},{7,5},{8,10},{9,11},{10,... | collective-permute-start | bytes 221192 | tf_op jit(solution)/shard_map/ppermute | solution.py:282
  39.1 1.1 %collective-permute-start.19 = (bf16[48,768]{1,0:T(8,128)(2,1)S(1)}, bf16[48,768]{1,0:T(8,128)(2,1)S(1)}, u32[]{:S(2)}, u32[]{:S(2)}) collective-permute-start(bf16[48,768]{1,0:T(8,128)(2,1)S(1)} %get-tuple-element.20), channel_id=1, source_target_pairs={{0,2},{1,3},{2,0},{3,1},{4,6},{5,7},{6,4},{7,5},{8,10},{9,11},{10,... | collective-permute-start | bytes 221192 | tf_op jit(solution)/shard_map/ppermute | solution.py:282
  40.2 0.9 %collective-permute-start.17 = (bf16[48,768]{1,0:T(8,128)(2,1)S(1)}, bf16[48,768]{1,0:T(8,128)(2,1)S(1)}, u32[]{:S(2)}, u32[]{:S(2)}) collective-permute-start(bf16[48,768]{1,0:T(8,128)(2,1)S(1)} %get-tuple-element.21), channel_id=1, source_target_pairs={{0,2},{1,3},{2,0},{3,1},{4,6},{5,7},{6,4},{7,5},{8,10},{9,11},{10,... | collective-permute-start | bytes 221192 | tf_op jit(solution)/shard_map/ppermute | solution.py:282
  41.1 1.1 %collective-permute-start.16 = (bf16[48,768]{1,0:T(8,128)(2,1)S(1)}, bf16[48,768]{1,0:T(8,128)(2,1)S(1)}, u32[]{:S(2)}, u32[]{:S(2)}) collective-permute-start(bf16[48,768]{1,0:T(8,128)(2,1)S(1)} %get-tuple-element.22), channel_id=1, source_target_pairs={{0,2},{1,3},{2,0},{3,1},{4,6},{5,7},{6,4},{7,5},{8,10},{9,11},{10,... | collective-permute-start | bytes 221192 | tf_op jit(solution)/shard_map/ppermute | solution.py:282
  42.2 1.1 %collective-permute-done.21.came_ref = bf16[48,768]{1,0:T(8,128)(2,1)S(1)} collective-permute-done((bf16[48,768]{1,0:T(8,128)(2,1)S(1)}, bf16[48,768]{1,0:T(8,128)(2,1)S(1)}, u32[]{:S(2)}, u32[]{:S(2)}) %collective-permute-start.21) | collective-permute-done | bytes 73760 | tf_op jit(solution)/shard_map/ppermute | solution.py:282
  43.3 0.2 collective-permute-start.22
  43.5 1.3 %collective-permute-done.19.came_ref = bf16[48,768]{1,0:T(8,128)(2,1)S(1)} collective-permute-done((bf16[48,768]{1,0:T(8,128)(2,1)S(1)}, bf16[48,768]{1,0:T(8,128)(2,1)S(1)}, u32[]{:S(2)}, u32[]{:S(2)}) %collective-permute-start.19) | collective-permute-done | bytes 73760 | tf_op jit(solution)/shard_map/ppermute | solution.py:282
  44.9 2.4 %collective-permute-start.20 = (bf16[48,768]{1,0:T(8,128)(2,1)S(1)}, bf16[48,768]{1,0:T(8,128)(2,1)S(1)}, u32[]{:S(2)}, u32[]{:S(2)}) collective-permute-start(bf16[48,768]{1,0:T(8,128)(2,1)S(1)} %add_block.6), channel_id=1, source_target_pairs={{0,8},{1,9},{2,10},{3,11},{4,12},{5,13},{6,14},{7,15},{8,0},{9,1},... | collective-permute-start | bytes 221192 | tf_op jit(solution)/shard_map/ppermute | solution.py:279
  47.3 2.5 %collective-permute-start.18 = (bf16[48,768]{1,0:T(8,128)(2,1)S(1)}, bf16[48,768]{1,0:T(8,128)(2,1)S(1)}, u32[]{:S(2)}, u32[]{:S(2)}) collective-permute-start(bf16[48,768]{1,0:T(8,128)(2,1)S(1)} %add_block.5), channel_id=1, source_target_pairs={{0,12},{1,13},{2,14},{3,15},{4,0},{5,1},{6,2},{7,3},{8,4},{9,5},{1... | collective-permute-start | bytes 221192 | tf_op jit(solution)/shard_map/ppermute | solution.py:279
  49.8 0.2 blend.1.blend_ref
  50.0 2.0 %collective-permute-done.20.m2_ref = bf16[48,768]{1,0:T(8,128)(2,1)S(1)} collective-permute-done((bf16[48,768]{1,0:T(8,128)(2,1)S(1)}, bf16[48,768]{1,0:T(8,128)(2,1)S(1)}, u32[]{:S(2)}, u32[]{:S(2)}) %collective-permute-start.20) | collective-permute-done | bytes 73760 | tf_op jit(solution)/shard_map/ppermute | solution.py:279
  52.1 0.9 %mix.1 = bf16[16,3072]{1,0:T(8,128)(2,1)} custom-call(bf16[16,3072]{1,0:T(8,128)(2,1)S(1)} %get-tuple-element.12.hid_ref, bf16[192,128]{1,0:T(8,128)(2,1)S(1)} %blend.1.blend_ref, bf16[48,768]{1,0:T(8,128)(2,1)S(1)} %add_block.4.m0_ref, bf16[48,768]{1,0:T(8,128)(2,1)S(1)} %collective-permute-done.18.m1_ref, ...), custom_call_target="tpu_custom_call" | custom-call | tf_op jit(solution)/shard_map/mix/pallas_call | solution.py:328
  (51 shorter events, 0.5 us)
Async XLA Ops:
  0.0 26.6 %slice-start.3 = ((s8[12582912]{0:T(1024)(128)(4,1)}), s8[4194304]{0:T(1024)(128)(4,1)S(1)}, s32[]{:S(2)}) async-start(s8[12582912]{0:T(1024)(128)(4,1)} %bitcast.6), calls=%async_computation.3 | async-start | bytes 8388608
  0.0 26.6 %slice-start.6 = ((s8[12582912]{0:T(1024)(128)(4,1)}), s8[4194304]{0:T(1024)(128)(4,1)S(1)}, s32[]{:S(2)}) async-start(s8[12582912]{0:T(1024)(128)(4,1)} %bitcast.8), calls=%async_computation.6 | async-start | bytes 8388608
  0.0 26.6 %slice-start.1 = ((s8[12582912]{0:T(1024)(128)(4,1)}), s8[4194304]{0:T(1024)(128)(4,1)S(1)}, s32[]{:S(2)}) async-start(s8[12582912]{0:T(1024)(128)(4,1)} %bitcast.4), calls=%async_computation.1 | async-start | bytes 8388608
  0.0 26.6 %slice-start.2 = ((s8[12582912]{0:T(1024)(128)(4,1)}), s8[4194304]{0:T(1024)(128)(4,1)S(1)}, s32[]{:S(2)}) async-start(s8[12582912]{0:T(1024)(128)(4,1)} %bitcast.4), calls=%async_computation.2 | async-start | bytes 8388608
  0.0 26.6 %slice-start.4 = ((s8[12582912]{0:T(1024)(128)(4,1)}), s8[4194304]{0:T(1024)(128)(4,1)S(1)}, s32[]{:S(2)}) async-start(s8[12582912]{0:T(1024)(128)(4,1)} %bitcast.6), calls=%async_computation.4 | async-start | bytes 8388608
  0.0 26.6 %slice-start.5 = ((s8[12582912]{0:T(1024)(128)(4,1)}), s8[4194304]{0:T(1024)(128)(4,1)S(1)}, s32[]{:S(2)}) async-start(s8[12582912]{0:T(1024)(128)(4,1)} %bitcast.6), calls=%async_computation.5 | async-start | bytes 8388608
  0.0 26.6 %slice-start.7 = ((s8[12582912]{0:T(1024)(128)(4,1)}), s8[4194304]{0:T(1024)(128)(4,1)S(1)}, s32[]{:S(2)}) async-start(s8[12582912]{0:T(1024)(128)(4,1)} %bitcast.8), calls=%async_computation.7 | async-start | bytes 8388608
  0.0 26.6 %slice-start.8 = ((s8[12582912]{0:T(1024)(128)(4,1)}), s8[4194304]{0:T(1024)(128)(4,1)S(1)}, s32[]{:S(2)}) async-start(s8[12582912]{0:T(1024)(128)(4,1)} %bitcast.8), calls=%async_computation.8 | async-start | bytes 8388608
  0.1 26.6 %copy-start = (bf16[192,192]{1,0:T(8,128)(2,1)S(1)}, bf16[192,192]{1,0:T(8,128)(2,1)}, u32[]{:S(2)}) copy-start(bf16[192,192]{1,0:T(8,128)(2,1)} %constant.22.clone.refs_16_.refs_17_) | copy-start | bytes 221188
  8.1 8.6 %collective-permute-start = (bf16[48,768]{1,0:T(8,128)(2,1)S(1)}, bf16[48,768]{1,0:T(8,128)(2,1)S(1)}, u32[]{:S(2)}, u32[]{:S(2)}) collective-permute-start(bf16[48,768]{1,0:T(8,128)(2,1)S(1)} %get-tuple-element.14), channel_id=1, source_target_pairs={{0,4},{1,5},{2,6},{3,7},{4,8},{5,9},{6,10},{7,11},{8,12},{9,13},{1... | collective-permute-start | bytes 221192 | tf_op jit(solution)/shard_map/ppermute | solution.py:279
  11.2 7.6 %collective-permute-start.1 = (bf16[48,768]{1,0:T(8,128)(2,1)S(1)}, bf16[48,768]{1,0:T(8,128)(2,1)S(1)}, u32[]{:S(2)}, u32[]{:S(2)}) collective-permute-start(bf16[48,768]{1,0:T(8,128)(2,1)S(1)} %get-tuple-element.15), channel_id=1, source_target_pairs={{0,8},{1,9},{2,10},{3,11},{4,12},{5,13},{6,14},{7,15},{8,0},{9,1},... | collective-permute-start | bytes 221192 | tf_op jit(solution)/shard_map/ppermute | solution.py:279
  13.8 6.7 %collective-permute-start.2 = (bf16[48,768]{1,0:T(8,128)(2,1)S(1)}, bf16[48,768]{1,0:T(8,128)(2,1)S(1)}, u32[]{:S(2)}, u32[]{:S(2)}) collective-permute-start(bf16[48,768]{1,0:T(8,128)(2,1)S(1)} %get-tuple-element.16), channel_id=1, source_target_pairs={{0,12},{1,13},{2,14},{3,15},{4,0},{5,1},{6,2},{7,3},{8,4},{9,5},{1... | collective-permute-start | bytes 221192 | tf_op jit(solution)/shard_map/ppermute | solution.py:279
  15.1 5.6 %collective-permute-start.3 = (bf16[48,768]{1,0:T(8,128)(2,1)S(1)}, bf16[48,768]{1,0:T(8,128)(2,1)S(1)}, u32[]{:S(2)}, u32[]{:S(2)}) collective-permute-start(bf16[48,768]{1,0:T(8,128)(2,1)S(1)} %get-tuple-element.13.refs_0_), channel_id=1, source_target_pairs={{0,2},{1,3},{2,0},{3,1},{4,6},{5,7},{6,4},{7,5},{8,10},{9,11},{10,... | collective-permute-start | bytes 221192 | tf_op jit(solution)/shard_map/ppermute | solution.py:282
  16.7 4.1 %collective-permute-start.7 = (bf16[48,768]{1,0:T(8,128)(2,1)S(1)}, bf16[48,768]{1,0:T(8,128)(2,1)S(1)}, u32[]{:S(2)}, u32[]{:S(2)}) collective-permute-start(bf16[48,768]{1,0:T(8,128)(2,1)S(1)} %get-tuple-element.13.refs_0_), channel_id=1, source_target_pairs={{0,1},{1,0},{2,3},{3,2},{4,5},{5,4},{6,7},{7,6},{8,9},{9,8},{10,11... | collective-permute-start | bytes 221192 | tf_op jit(solution)/shard_map/ppermute | solution.py:282
  16.7 4.8 %collective-permute-start.4 = (bf16[48,768]{1,0:T(8,128)(2,1)S(1)}, bf16[48,768]{1,0:T(8,128)(2,1)S(1)}, u32[]{:S(2)}, u32[]{:S(2)}) collective-permute-start(bf16[48,768]{1,0:T(8,128)(2,1)S(1)} %collective-permute-done.refs_1_), channel_id=1, source_target_pairs={{0,2},{1,3},{2,0},{3,1},{4,6},{5,7},{6,4},{7,5},{8,10},{9,11},{10,... | collective-permute-start | bytes 221192 | tf_op jit(solution)/shard_map/ppermute | solution.py:282
  18.7 5.1 %collective-permute-start.5 = (bf16[48,768]{1,0:T(8,128)(2,1)S(1)}, bf16[48,768]{1,0:T(8,128)(2,1)S(1)}, u32[]{:S(2)}, u32[]{:S(2)}) collective-permute-start(bf16[48,768]{1,0:T(8,128)(2,1)S(1)} %collective-permute-done.1.refs_2_), channel_id=1, source_target_pairs={{0,2},{1,3},{2,0},{3,1},{4,6},{5,7},{6,4},{7,5},{8,10},{9,11},{10,... | collective-permute-start | bytes 221192 | tf_op jit(solution)/shard_map/ppermute | solution.py:282
  20.4 4.4 %collective-permute-start.6 = (bf16[48,768]{1,0:T(8,128)(2,1)S(1)}, bf16[48,768]{1,0:T(8,128)(2,1)S(1)}, u32[]{:S(2)}, u32[]{:S(2)}) collective-permute-start(bf16[48,768]{1,0:T(8,128)(2,1)S(1)} %collective-permute-done.2.refs_3_), channel_id=1, source_target_pairs={{0,2},{1,3},{2,0},{3,1},{4,6},{5,7},{6,4},{7,5},{8,10},{9,11},{10,... | collective-permute-start | bytes 221192 | tf_op jit(solution)/shard_map/ppermute | solution.py:282
  20.8 4.0 %collective-permute-start.11 = (bf16[48,768]{1,0:T(8,128)(2,1)S(1)}, bf16[48,768]{1,0:T(8,128)(2,1)S(1)}, u32[]{:S(2)}, u32[]{:S(2)}) collective-permute-start(bf16[48,768]{1,0:T(8,128)(2,1)S(1)} %collective-permute-done.3.refs_4_), channel_id=1, source_target_pairs={{0,1},{1,0},{2,3},{3,2},{4,5},{5,4},{6,7},{7,6},{8,9},{9,8},{10,11... | collective-permute-start | bytes 221192 | tf_op jit(solution)/shard_map/ppermute | solution.py:282
  20.8 4.5 %collective-permute-start.10 = (bf16[48,768]{1,0:T(8,128)(2,1)S(1)}, bf16[48,768]{1,0:T(8,128)(2,1)S(1)}, u32[]{:S(2)}, u32[]{:S(2)}) collective-permute-start(bf16[48,768]{1,0:T(8,128)(2,1)S(1)} %collective-permute-done.2.refs_3_), channel_id=1, source_target_pairs={{0,1},{1,0},{2,3},{3,2},{4,5},{5,4},{6,7},{7,6},{8,9},{9,8},{10,11... | collective-permute-start | bytes 221192 | tf_op jit(solution)/shard_map/ppermute | solution.py:282
  21.4 4.0 %collective-permute-start.8 = (bf16[48,768]{1,0:T(8,128)(2,1)S(1)}, bf16[48,768]{1,0:T(8,128)(2,1)S(1)}, u32[]{:S(2)}, u32[]{:S(2)}) collective-permute-start(bf16[48,768]{1,0:T(8,128)(2,1)S(1)} %collective-permute-done.refs_1_), channel_id=1, source_target_pairs={{0,1},{1,0},{2,3},{3,2},{4,5},{5,4},{6,7},{7,6},{8,9},{9,8},{10,11... | collective-permute-start | bytes 221192 | tf_op jit(solution)/shard_map/ppermute | solution.py:282
  23.9 1.5 %collective-permute-start.9 = (bf16[48,768]{1,0:T(8,128)(2,1)S(1)}, bf16[48,768]{1,0:T(8,128)(2,1)S(1)}, u32[]{:S(2)}, u32[]{:S(2)}) collective-permute-start(bf16[48,768]{1,0:T(8,128)(2,1)S(1)} %collective-permute-done.1.refs_2_), channel_id=1, source_target_pairs={{0,1},{1,0},{2,3},{3,2},{4,5},{5,4},{6,7},{7,6},{8,9},{9,8},{10,11... | collective-permute-start | bytes 221192 | tf_op jit(solution)/shard_map/ppermute | solution.py:282
  24.8 1.3 %collective-permute-start.12 = (bf16[48,768]{1,0:T(8,128)(2,1)S(1)}, bf16[48,768]{1,0:T(8,128)(2,1)S(1)}, u32[]{:S(2)}, u32[]{:S(2)}) collective-permute-start(bf16[48,768]{1,0:T(8,128)(2,1)S(1)} %collective-permute-done.4.refs_5_), channel_id=1, source_target_pairs={{0,1},{1,0},{2,3},{3,2},{4,5},{5,4},{6,7},{7,6},{8,9},{9,8},{10,11... | collective-permute-start | bytes 221192 | tf_op jit(solution)/shard_map/ppermute | solution.py:282
  24.8 1.4 %collective-permute-start.13 = (bf16[48,768]{1,0:T(8,128)(2,1)S(1)}, bf16[48,768]{1,0:T(8,128)(2,1)S(1)}, u32[]{:S(2)}, u32[]{:S(2)}) collective-permute-start(bf16[48,768]{1,0:T(8,128)(2,1)S(1)} %collective-permute-done.5.refs_6_), channel_id=1, source_target_pairs={{0,1},{1,0},{2,3},{3,2},{4,5},{5,4},{6,7},{7,6},{8,9},{9,8},{10,11... | collective-permute-start | bytes 221192 | tf_op jit(solution)/shard_map/ppermute | solution.py:282
  25.3 1.3 %collective-permute-start.14 = (bf16[48,768]{1,0:T(8,128)(2,1)S(1)}, bf16[48,768]{1,0:T(8,128)(2,1)S(1)}, u32[]{:S(2)}, u32[]{:S(2)}) collective-permute-start(bf16[48,768]{1,0:T(8,128)(2,1)S(1)} %collective-permute-done.6.refs_7_), channel_id=1, source_target_pairs={{0,1},{1,0},{2,3},{3,2},{4,5},{5,4},{6,7},{7,6},{8,9},{9,8},{10,11... | collective-permute-start | bytes 221192 | tf_op jit(solution)/shard_map/ppermute | solution.py:282
  35.7 2.2 %collective-permute-start.15 = (bf16[384,768]{1,0:T(8,128)(2,1)}, bf16[384,768]{1,0:T(8,128)(2,1)S(1)}, u32[]{:S(2)}, u32[]{:S(2)}) collective-permute-start(bf16[384,768]{1,0:T(8,128)(2,1)} %get-tuple-element.18), channel_id=1, source_target_pairs={{0,1},{1,0},{2,3},{3,2},{4,5},{5,4},{6,7},{7,6},{8,9},{9,8},{10,11... | collective-permute-start | bytes 1769480 | tf_op jit(solution)/shard_map/ppermute | solution.py:282
  38.1 5.2 %collective-permute-start.21 = (bf16[48,768]{1,0:T(8,128)(2,1)S(1)}, bf16[48,768]{1,0:T(8,128)(2,1)S(1)}, u32[]{:S(2)}, u32[]{:S(2)}) collective-permute-start(bf16[48,768]{1,0:T(8,128)(2,1)S(1)} %get-tuple-element.19), channel_id=1, source_target_pairs={{0,2},{1,3},{2,0},{3,1},{4,6},{5,7},{6,4},{7,5},{8,10},{9,11},{10,... | collective-permute-start | bytes 221192 | tf_op jit(solution)/shard_map/ppermute | solution.py:282
  39.1 5.8 %collective-permute-start.19 = (bf16[48,768]{1,0:T(8,128)(2,1)S(1)}, bf16[48,768]{1,0:T(8,128)(2,1)S(1)}, u32[]{:S(2)}, u32[]{:S(2)}) collective-permute-start(bf16[48,768]{1,0:T(8,128)(2,1)S(1)} %get-tuple-element.20), channel_id=1, source_target_pairs={{0,2},{1,3},{2,0},{3,1},{4,6},{5,7},{6,4},{7,5},{8,10},{9,11},{10,... | collective-permute-start | bytes 221192 | tf_op jit(solution)/shard_map/ppermute | solution.py:282
  40.2 7.0 %collective-permute-start.17 = (bf16[48,768]{1,0:T(8,128)(2,1)S(1)}, bf16[48,768]{1,0:T(8,128)(2,1)S(1)}, u32[]{:S(2)}, u32[]{:S(2)}) collective-permute-start(bf16[48,768]{1,0:T(8,128)(2,1)S(1)} %get-tuple-element.21), channel_id=1, source_target_pairs={{0,2},{1,3},{2,0},{3,1},{4,6},{5,7},{6,4},{7,5},{8,10},{9,11},{10,... | collective-permute-start | bytes 221192 | tf_op jit(solution)/shard_map/ppermute | solution.py:282
  41.1 8.8 %collective-permute-start.16 = (bf16[48,768]{1,0:T(8,128)(2,1)S(1)}, bf16[48,768]{1,0:T(8,128)(2,1)S(1)}, u32[]{:S(2)}, u32[]{:S(2)}) collective-permute-start(bf16[48,768]{1,0:T(8,128)(2,1)S(1)} %get-tuple-element.22), channel_id=1, source_target_pairs={{0,2},{1,3},{2,0},{3,1},{4,6},{5,7},{6,4},{7,5},{8,10},{9,11},{10,... | collective-permute-start | bytes 221192 | tf_op jit(solution)/shard_map/ppermute | solution.py:282
  43.3 6.7 %collective-permute-start.22 = (bf16[48,768]{1,0:T(8,128)(2,1)S(1)}, bf16[48,768]{1,0:T(8,128)(2,1)S(1)}, u32[]{:S(2)}, u32[]{:S(2)}) collective-permute-start(bf16[48,768]{1,0:T(8,128)(2,1)S(1)} %add_block.7), channel_id=1, source_target_pairs={{0,4},{1,5},{2,6},{3,7},{4,8},{5,9},{6,10},{7,11},{8,12},{9,13},{1... | collective-permute-start | bytes 221192 | tf_op jit(solution)/shard_map/ppermute | solution.py:279
  44.9 7.1 %collective-permute-start.20 = (bf16[48,768]{1,0:T(8,128)(2,1)S(1)}, bf16[48,768]{1,0:T(8,128)(2,1)S(1)}, u32[]{:S(2)}, u32[]{:S(2)}) collective-permute-start(bf16[48,768]{1,0:T(8,128)(2,1)S(1)} %add_block.6), channel_id=1, source_target_pairs={{0,8},{1,9},{2,10},{3,11},{4,12},{5,13},{6,14},{7,15},{8,0},{9,1},... | collective-permute-start | bytes 221192 | tf_op jit(solution)/shard_map/ppermute | solution.py:279
  47.3 4.8 %collective-permute-start.18 = (bf16[48,768]{1,0:T(8,128)(2,1)S(1)}, bf16[48,768]{1,0:T(8,128)(2,1)S(1)}, u32[]{:S(2)}, u32[]{:S(2)}) collective-permute-start(bf16[48,768]{1,0:T(8,128)(2,1)S(1)} %add_block.5), channel_id=1, source_target_pairs={{0,12},{1,13},{2,14},{3,15},{4,0},{5,1},{6,2},{7,3},{8,4},{9,5},{1... | collective-permute-start | bytes 221192 | tf_op jit(solution)/shard_map/ppermute | solution.py:279
  (3 other events, 50.0 us)

commit v3 on v2

--- a/solution.py
+++ b/solution.py
@@ -54,13 +54,11 @@
     return (chunk == (lane >> 4)) & (slot[s : s + 1, :] == row - SLOTS * chunk)
 
 
-def attention_kernel(
-    plane_ref, *refs
-):
+def attention_kernel(plane_ref, *refs):
     operands, outs, scratch = refs[:9], refs[9:14], refs[14:]
     len_hbm, q_hbm, res_hbm, k_hbm, v_hbm, nk_hbm, nv_hbm, gain_hbm, ids_hbm = operands
     hid_ref, *block_refs = outs
-    len_ref, q_ref, res_ref, k_ref, v_ref, nk_ref, nv_ref, gain_ref, ids_ref, q_scr, o_scr, sems, small = scratch
+    len_ref, q_ref, res_ref, k_ref, v_ref, nk_ref, nv_ref, gain_ref, ids_ref, q_scr, o_scr, pick_scr, sems, small = scratch
     parts = sems.shape[1]
     step = ROWS // parts
 
@@ -70,55 +68,59 @@
         return copy
 
     early = [
-        fetch(q_hbm, q_ref, small.at[0]),
-        fetch(nk_hbm, nk_ref, small.at[1]),
-        fetch(nv_hbm, nv_ref, small.at[2]),
-        fetch(len_hbm, len_ref, small.at[3]),
+        fetch(ids_hbm, ids_ref, small.at[0]),
+        fetch(q_hbm, q_ref, small.at[1]),
+        fetch(nk_hbm, nk_ref, small.at[2]),
+        fetch(nv_hbm, nv_ref, small.at[3]),
+        fetch(len_hbm, len_ref, small.at[4]),
     ]
     copies = []
     for c in range(parts):
         own = pl.ds(c * step, step)
         copies.append((
-            fetch(k_hbm.at[own], k_ref.at[own], sems.at[0, c]),
-            fetch(v_hbm.at[own], v_ref.at[own], sems.at[1, c]),
+            fetch(k_hbm.at[own], k_ref.at[own, pl.ds(0, CACHE)], sems.at[0, c]),
+            fetch(v_hbm.at[own], v_ref.at[own, pl.ds(0, CACHE)], sems.at[1, c]),
         ))
-    late = [
-        fetch(res_hbm, res_ref, small.at[4]),
-        fetch(gain_hbm, gain_ref, small.at[5]),
-        fetch(ids_hbm, ids_ref, small.at[6]),
-    ]
-    for copy in early:
-        copy.wait()
+    late = [fetch(res_hbm, res_ref, small.at[5]), fetch(gain_hbm, gain_ref, small.at[6])]
+    early[0].wait()
+    slot, _, _, _ = slots_of(plane_ref[0], ids_ref)
+    for s in range(EXPERTS):
+        pick_scr[s * PACK : (s + 1) * PACK, :] = jnp.where(matching(slot, s), 1.0, 0.0).astype(BF16)
+    early[1].wait()
     for h in range(Q_HEADS):
         q_scr[pl.ds(h, ROWS, stride=Q_HEADS), :] = q_ref[:, h * HEAD : (h + 1) * HEAD].astype(F32)
+    for copy in early[2:]:
+        copy.wait()
+    nk, nv = nk_ref[...], nv_ref[...]
+    for t in range(ROWS):
+        k_ref[t, CACHE:, :] = nk
+        v_ref[t, CACHE:, :] = nv
     row, col = iota((Q_HEADS, KV_HEADS * HEAD), 0), iota((Q_HEADS, KV_HEADS * HEAD), 1)
     reads = sum((row >= GROUP * k).astype(I32) for k in range(1, KV_HEADS)) == (col >> 7)
     head_row = iota((Q_HEADS, HEAD), 0)
-    position, own_col = iota((Q_HEADS, CACHE), 1), iota((Q_HEADS, ROWS), 1)
+    position = iota((Q_HEADS, CACHE + ROWS), 1)
     scaling = 1.0 / math.sqrt(HEAD)
     contract = (((1,), (1,)), ((), ()))
-    nk, nv = nk_ref[...], nv_ref[...]
-    low = -1e30
-    for t in range(ROWS):
-        if t % step == 0:
-            for copy in copies[t // step]:
-                copy.wait()
-        q = q_scr[t * Q_HEADS : (t + 1) * Q_HEADS, :]
-        q = jnp.where(reads, jnp.concatenate([q] * KV_HEADS, axis=1), 0.0).astype(BF16)
-        s1 = lax.dot_general(q, k_ref[t], contract, preferred_element_type=F32) * scaling
-        s2 = lax.dot_general(q, nk, contract, preferred_element_type=F32) * scaling
-        s1 = jnp.where(position < len_ref[t], s1, low)
-        s2 = jnp.where(own_col == t, s2, low)
-        top = jnp.maximum(jnp.max(s1, axis=1, keepdims=True), jnp.max(s2, axis=1, keepdims=True))
-        e1, e2 = jnp.exp(s1 - top), jnp.exp(s2 - top)
-        total = jnp.sum(e1, axis=1, keepdims=True) + jnp.sum(e2, axis=1, keepdims=True)
-        p1, p2 = (e1 / total).astype(BF16), (e2 / total).astype(BF16)
-        o = jnp.dot(p1, v_ref[t], preferred_element_type=F32)
-        o = o + jnp.dot(p2, nv, preferred_element_type=F32)
-        picked = o[:, 0:HEAD]
-        for k in range(1, KV_HEADS):
-            picked = jnp.where(head_row >= GROUP * k, o[:, k * HEAD : (k + 1) * HEAD], picked)
-        o_scr[t * Q_HEADS : (t + 1) * Q_HEADS, :] = picked
+    for c in range(parts):
+        tokens = range(c * step, (c + 1) * step)
+        copies[c][0].wait()
+        scores = []
+        for t in tokens:
+            q = q_scr[t * Q_HEADS : (t + 1) * Q_HEADS, :]
+            q = jnp.where(reads, jnp.concatenate([q] * KV_HEADS, axis=1), 0.0).astype(BF16)
+            score = lax.dot_general(q, k_ref[t], contract, preferred_element_type=F32) * scaling
+            live = (position < len_ref[t]) | (position == CACHE + t)
+            scores.append(jnp.where(live, score, -1e30))
+        scores = jnp.concatenate(scores, axis=0)
+        weight = jnp.exp(scores - jnp.max(scores, axis=1, keepdims=True))
+        probs = (weight / jnp.sum(weight, axis=1, keepdims=True)).astype(BF16)
+        copies[c][1].wait()
+        for i, t in enumerate(tokens):
+            o = jnp.dot(probs[i * Q_HEADS : (i + 1) * Q_HEADS], v_ref[t], preferred_element_type=F32)
+            picked = o[:, 0:HEAD]
+            for k in range(1, KV_HEADS):
+                picked = jnp.where(head_row >= GROUP * k, o[:, k * HEAD : (k + 1) * HEAD], picked)
+            o_scr[t * Q_HEADS : (t + 1) * Q_HEADS, :] = picked
     for copy in late:
         copy.wait()
     squares = jnp.zeros((ROWS, HEAD), F32)
@@ -141,9 +143,8 @@
         ]
         chunks.append(jnp.concatenate(heads, axis=1))
     stacked = jnp.concatenate(chunks, axis=0)
-    slot, _, _, _ = slots_of(plane_ref[0], ids_ref)
     for s, out in enumerate(block_refs):
-        picker = jnp.where(matching(slot, s), 1.0, 0.0).astype(BF16)
+        picker = pick_scr[s * PACK : (s + 1) * PACK, :]
         out[...] = jnp.dot(picker, stacked, preferred_element_type=F32).astype(BF16)
 
 
@@ -223,11 +224,14 @@
         in_specs=[SMEM] + [HBM] * len(operands),
         out_specs=[VMEM] * (1 + EXPERTS),
         scratch_shapes=[pltpu.SMEM(operands[0].shape, I32)]
-        + [pltpu.VMEM(x.shape, x.dtype) for x in operands[1:]]
+        + [pltpu.VMEM(x.shape, x.dtype) for x in operands[1:3]]
+        + [pltpu.VMEM((ROWS, CACHE + ROWS, kv_width), BF16)] * 2
+        + [pltpu.VMEM(x.shape, x.dtype) for x in operands[5:]]
         + [
             pltpu.VMEM((ROWS * Q_HEADS, HEAD), F32),
             pltpu.VMEM((ROWS * Q_HEADS, HEAD), F32),
-            pltpu.SemaphoreType.DMA((2, 4)),
+            pltpu.VMEM((EXPERTS * PACK, LANES), BF16),
+            pltpu.SemaphoreType.DMA((2, 1)),
             pltpu.SemaphoreType.DMA((7,)),
         ],
         compiler_params=params(6),

time: 53.1 us -> 48.4 us (0.911)
  Pallas kernels: 18.2 us -> 13.5 us
    pallas_call x1, Pallas kernels: 8.02 us -> 3.33 us  [attention(): pl.pallas_call(attention_kernel, out_shape=[jax.ShapeDtypeStruct((ROWS, w...]
where the time goes in v3:
time: 48.4 us; the launch traced here: 48.3 us
  starting transfers between devices  22.1 us (46%)
  Pallas kernels  13.5 us (28%)
  waiting for transfers between devices  12.1 us (25%)
    ppermute x6, starting transfers between devices, shifted(): lax.ppermute(x, 'attn', [(i, (i + s * splits) % devices) for i in range(d...  12.1 us
    ppermute x17, starting transfers between devices, swapped(): return lax.ppermute(x, 'attn', [(i, i ^ bit) for i in range(devices)])  10.1 us
    ppermute x17, waiting for transfers between devices, swapped(): return lax.ppermute(x, 'attn', [(i, i ^ bit) for i in range(devices)])  9.17 us
    pallas_call x1, Pallas kernels, local(): pl.pallas_call(functools.partial(experts_kernel, splits), out_shape=[jax....  9.02 us
    pallas_call x1, Pallas kernels, attention(): pl.pallas_call(attention_kernel, out_shape=[jax.ShapeDtypeStruct((ROWS, w...  3.33 us
    ppermute x6, waiting for transfers between devices, shifted(): lax.ppermute(x, 'attn', [(i, (i + s * splits) % devices) for i in range(d...  2.96 us
  transfers between devices with their start and end apart: 23, of which 12 were waited for; matrix products, arithmetic and copies ran while one was open for 0% of the time, Pallas kernels for 1%

profile of v3, /device:TPU:0, one launch (start us, length us, event | category | flops | bytes accessed | tf_op | source)
XLA Modules:
  0.0 48.3 jit_solution(12248899480601250139)
XLA Ops:
  0.1 3.3 %attention.1 = (bf16[16,3072]{1,0:T(8,128)(2,1)S(1)}, bf16[48,768]{1,0:T(8,128)(2,1)S(1)}, bf16[48,768]{1,0:T(8,128)(2,1)S(1)}, bf16[48,768]{1,0:T(8,128)(2,1)S(1)}, bf16[48,768]{1,0:T(8,128)(2,1)S(1)}) custom-call(s32[1]{0:T(128)} %bitcast.plane_ref, s32[16]{0:T(128)} %refs_0_.1, bf16[16,3072]{1,0:T(8,128)(2,1)} %refs_1_.1, bf16[16,3072]{1,0:T(8,128)(2,1)} %refs_2_.1, ...), custom_call_target="tpu_custom_call" | custom-call | flops 40000000000 | bytes 4000000 | tf_op jit(solution)/shard_map/attention/pallas_call | solution.py:221
  3.4 3.1 %collective-permute-start = (bf16[48,768]{1,0:T(8,128)(2,1)S(1)}, bf16[48,768]{1,0:T(8,128)(2,1)S(1)}, u32[]{:S(2)}, u32[]{:S(2)}) collective-permute-start(bf16[48,768]{1,0:T(8,128)(2,1)S(1)} %get-tuple-element.14), channel_id=1, source_target_pairs={{0,4},{1,5},{2,6},{3,7},{4,8},{5,9},{6,10},{7,11},{8,12},{9,13},{1... | collective-permute-start | bytes 221192 | tf_op jit(solution)/shard_map/ppermute | solution.py:283
  6.5 2.6 %collective-permute-start.1 = (bf16[48,768]{1,0:T(8,128)(2,1)S(1)}, bf16[48,768]{1,0:T(8,128)(2,1)S(1)}, u32[]{:S(2)}, u32[]{:S(2)}) collective-permute-start(bf16[48,768]{1,0:T(8,128)(2,1)S(1)} %get-tuple-element.15), channel_id=1, source_target_pairs={{0,8},{1,9},{2,10},{3,11},{4,12},{5,13},{6,14},{7,15},{8,0},{9,1},... | collective-permute-start | bytes 221192 | tf_op jit(solution)/shard_map/ppermute | solution.py:283
  9.1 1.4 %collective-permute-start.2 = (bf16[48,768]{1,0:T(8,128)(2,1)S(1)}, bf16[48,768]{1,0:T(8,128)(2,1)S(1)}, u32[]{:S(2)}, u32[]{:S(2)}) collective-permute-start(bf16[48,768]{1,0:T(8,128)(2,1)S(1)} %get-tuple-element.16), channel_id=1, source_target_pairs={{0,12},{1,13},{2,14},{3,15},{4,0},{5,1},{6,2},{7,3},{8,4},{9,5},{1... | collective-permute-start | bytes 221192 | tf_op jit(solution)/shard_map/ppermute | solution.py:283
  10.4 1.5 %collective-permute-start.3 = (bf16[48,768]{1,0:T(8,128)(2,1)S(1)}, bf16[48,768]{1,0:T(8,128)(2,1)S(1)}, u32[]{:S(2)}, u32[]{:S(2)}) collective-permute-start(bf16[48,768]{1,0:T(8,128)(2,1)S(1)} %get-tuple-element.13.refs_0_), channel_id=1, source_target_pairs={{0,2},{1,3},{2,0},{3,1},{4,6},{5,7},{6,4},{7,5},{8,10},{9,11},{10,... | collective-permute-start | bytes 221192 | tf_op jit(solution)/shard_map/ppermute | solution.py:286
  12.0 1.1 %collective-permute-start.4 = (bf16[48,768]{1,0:T(8,128)(2,1)S(1)}, bf16[48,768]{1,0:T(8,128)(2,1)S(1)}, u32[]{:S(2)}, u32[]{:S(2)}) collective-permute-start(bf16[48,768]{1,0:T(8,128)(2,1)S(1)} %collective-permute-done.refs_1_), channel_id=1, source_target_pairs={{0,2},{1,3},{2,0},{3,1},{4,6},{5,7},{6,4},{7,5},{8,10},{9,11},{10,... | collective-permute-start | bytes 221192 | tf_op jit(solution)/shard_map/ppermute | solution.py:286
  13.1 0.9 %collective-permute-done.1.refs_2_ = bf16[48,768]{1,0:T(8,128)(2,1)S(1)} collective-permute-done((bf16[48,768]{1,0:T(8,128)(2,1)S(1)}, bf16[48,768]{1,0:T(8,128)(2,1)S(1)}, u32[]{:S(2)}, u32[]{:S(2)}) %collective-permute-start.1) | collective-permute-done | bytes 73760 | tf_op jit(solution)/shard_map/ppermute | solution.py:283
  14.0 1.7 %collective-permute-start.5 = (bf16[48,768]{1,0:T(8,128)(2,1)S(1)}, bf16[48,768]{1,0:T(8,128)(2,1)S(1)}, u32[]{:S(2)}, u32[]{:S(2)}) collective-permute-start(bf16[48,768]{1,0:T(8,128)(2,1)S(1)} %collective-permute-done.1.refs_2_), channel_id=1, source_target_pairs={{0,2},{1,3},{2,0},{3,1},{4,6},{5,7},{6,4},{7,5},{8,10},{9,11},{10,... | collective-permute-start | bytes 221192 | tf_op jit(solution)/shard_map/ppermute | solution.py:286
  15.8 0.3 collective-permute-start.6
  16.1 0.5 %collective-permute-start.10 = (bf16[48,768]{1,0:T(8,128)(2,1)S(1)}, bf16[48,768]{1,0:T(8,128)(2,1)S(1)}, u32[]{:S(2)}, u32[]{:S(2)}) collective-permute-start(bf16[48,768]{1,0:T(8,128)(2,1)S(1)} %collective-permute-done.2.refs_3_), channel_id=1, source_target_pairs={{0,1},{1,0},{2,3},{3,2},{4,5},{5,4},{6,7},{7,6},{8,9},{9,8},{10,11... | collective-permute-start | bytes 221192 | tf_op jit(solution)/shard_map/ppermute | solution.py:286
  16.6 0.1 collective-permute-done.4.refs_5_
  16.7 2.4 %collective-permute-done.5.refs_6_ = bf16[48,768]{1,0:T(8,128)(2,1)S(1)} collective-permute-done((bf16[48,768]{1,0:T(8,128)(2,1)S(1)}, bf16[48,768]{1,0:T(8,128)(2,1)S(1)}, u32[]{:S(2)}, u32[]{:S(2)}) %collective-permute-start.5) | collective-permute-done | bytes 73760 | tf_op jit(solution)/shard_map/ppermute | solution.py:286
  19.2 0.9 %collective-permute-done.6.refs_7_ = bf16[48,768]{1,0:T(8,128)(2,1)S(1)} collective-permute-done((bf16[48,768]{1,0:T(8,128)(2,1)S(1)}, bf16[48,768]{1,0:T(8,128)(2,1)S(1)}, u32[]{:S(2)}, u32[]{:S(2)}) %collective-permute-start.6) | collective-permute-done | bytes 73760 | tf_op jit(solution)/shard_map/ppermute | solution.py:286
  20.1 0.5 %collective-permute-start.13 = (bf16[48,768]{1,0:T(8,128)(2,1)S(1)}, bf16[48,768]{1,0:T(8,128)(2,1)S(1)}, u32[]{:S(2)}, u32[]{:S(2)}) collective-permute-start(bf16[48,768]{1,0:T(8,128)(2,1)S(1)} %collective-permute-done.5.refs_6_), channel_id=1, source_target_pairs={{0,1},{1,0},{2,3},{3,2},{4,5},{5,4},{6,7},{7,6},{8,9},{9,8},{10,11... | collective-permute-start | bytes 221192 | tf_op jit(solution)/shard_map/ppermute | solution.py:286
  20.7 0.7 %collective-permute-done.12.refs_13_ = bf16[48,768]{1,0:T(8,128)(2,1)S(1)} collective-permute-done((bf16[48,768]{1,0:T(8,128)(2,1)S(1)}, bf16[48,768]{1,0:T(8,128)(2,1)S(1)}, u32[]{:S(2)}, u32[]{:S(2)}) %collective-permute-start.12) | collective-permute-done | bytes 73760 | tf_op jit(solution)/shard_map/ppermute | solution.py:286
  21.4 0.2 collective-permute-done.13.refs_14_
  21.5 0.4 collective-permute-done.14.refs_15_
  22.0 9.0 %experts.1 = (bf16[384,768]{1,0:T(8,128)(2,1)S(1)}, bf16[384,768]{1,0:T(8,128)(2,1)}) custom-call(bf16[48,768]{1,0:T(8,128)(2,1)S(1)} %get-tuple-element.13.refs_0_, bf16[48,768]{1,0:T(8,128)(2,1)S(1)} %collective-permute-done.refs_1_, bf16[48,768]{1,0:T(8,128)(2,1)S(1)} %collective-permute-done.1.refs_2_, ...), custom_call_target="tpu_custom_call" | custom-call | flops 7247757312 | bytes 37748736 | tf_op jit(solution)/shard_map/experts/pallas_call | solution.py:300
  31.0 0.1 collective-permute-start.15
  31.2 2.1 %collective-permute-done.15 = bf16[384,768]{1,0:T(8,128)(2,1)S(1)} collective-permute-done((bf16[384,768]{1,0:T(8,128)(2,1)}, bf16[384,768]{1,0:T(8,128)(2,1)S(1)}, u32[]{:S(2)}, u32[]{:S(2)}) %collective-permute-start.15) | collective-permute-done | bytes 589856 | tf_op jit(solution)/shard_map/ppermute | solution.py:286
  33.4 1.0 %collective-permute-start.21 = (bf16[48,768]{1,0:T(8,128)(2,1)S(1)}, bf16[48,768]{1,0:T(8,128)(2,1)S(1)}, u32[]{:S(2)}, u32[]{:S(2)}) collective-permute-start(bf16[48,768]{1,0:T(8,128)(2,1)S(1)} %get-tuple-element.19), channel_id=1, source_target_pairs={{0,2},{1,3},{2,0},{3,1},{4,6},{5,7},{6,4},{7,5},{8,10},{9,11},{10,... | collective-permute-start | bytes 221192 | tf_op jit(solution)/shard_map/ppermute | solution.py:286
  34.4 1.1 %collective-permute-start.19 = (bf16[48,768]{1,0:T(8,128)(2,1)S(1)}, bf16[48,768]{1,0:T(8,128)(2,1)S(1)}, u32[]{:S(2)}, u32[]{:S(2)}) collective-permute-start(bf16[48,768]{1,0:T(8,128)(2,1)S(1)} %get-tuple-element.20), channel_id=1, source_target_pairs={{0,2},{1,3},{2,0},{3,1},{4,6},{5,7},{6,4},{7,5},{8,10},{9,11},{10,... | collective-permute-start | bytes 221192 | tf_op jit(solution)/shard_map/ppermute | solution.py:286
  35.5 1.0 %collective-permute-start.17 = (bf16[48,768]{1,0:T(8,128)(2,1)S(1)}, bf16[48,768]{1,0:T(8,128)(2,1)S(1)}, u32[]{:S(2)}, u32[]{:S(2)}) collective-permute-start(bf16[48,768]{1,0:T(8,128)(2,1)S(1)} %get-tuple-element.21), channel_id=1, source_target_pairs={{0,2},{1,3},{2,0},{3,1},{4,6},{5,7},{6,4},{7,5},{8,10},{9,11},{10,... | collective-permute-start | bytes 221192 | tf_op jit(solution)/shard_map/ppermute | solution.py:286
  36.5 1.1 %collective-permute-start.16 = (bf16[48,768]{1,0:T(8,128)(2,1)S(1)}, bf16[48,768]{1,0:T(8,128)(2,1)S(1)}, u32[]{:S(2)}, u32[]{:S(2)}) collective-permute-start(bf16[48,768]{1,0:T(8,128)(2,1)S(1)} %get-tuple-element.22), channel_id=1, source_target_pairs={{0,2},{1,3},{2,0},{3,1},{4,6},{5,7},{6,4},{7,5},{8,10},{9,11},{10,... | collective-permute-start | bytes 221192 | tf_op jit(solution)/shard_map/ppermute | solution.py:286
  37.5 1.1 %collective-permute-done.21.came_ref = bf16[48,768]{1,0:T(8,128)(2,1)S(1)} collective-permute-done((bf16[48,768]{1,0:T(8,128)(2,1)S(1)}, bf16[48,768]{1,0:T(8,128)(2,1)S(1)}, u32[]{:S(2)}, u32[]{:S(2)}) %collective-permute-start.21) | collective-permute-done | bytes 73760 | tf_op jit(solution)/shard_map/ppermute | solution.py:286
  38.6 0.2 collective-permute-start.22
  38.9 1.3 %collective-permute-done.19.came_ref = bf16[48,768]{1,0:T(8,128)(2,1)S(1)} collective-permute-done((bf16[48,768]{1,0:T(8,128)(2,1)S(1)}, bf16[48,768]{1,0:T(8,128)(2,1)S(1)}, u32[]{:S(2)}, u32[]{:S(2)}) %collective-permute-start.19) | collective-permute-done | bytes 73760 | tf_op jit(solution)/shard_map/ppermute | solution.py:286
  40.2 2.4 %collective-permute-start.20 = (bf16[48,768]{1,0:T(8,128)(2,1)S(1)}, bf16[48,768]{1,0:T(8,128)(2,1)S(1)}, u32[]{:S(2)}, u32[]{:S(2)}) collective-permute-start(bf16[48,768]{1,0:T(8,128)(2,1)S(1)} %add_block.6), channel_id=1, source_target_pairs={{0,8},{1,9},{2,10},{3,11},{4,12},{5,13},{6,14},{7,15},{8,0},{9,1},... | collective-permute-start | bytes 221192 | tf_op jit(solution)/shard_map/ppermute | solution.py:283
  42.6 2.5 %collective-permute-start.18 = (bf16[48,768]{1,0:T(8,128)(2,1)S(1)}, bf16[48,768]{1,0:T(8,128)(2,1)S(1)}, u32[]{:S(2)}, u32[]{:S(2)}) collective-permute-start(bf16[48,768]{1,0:T(8,128)(2,1)S(1)} %add_block.5), channel_id=1, source_target_pairs={{0,12},{1,13},{2,14},{3,15},{4,0},{5,1},{6,2},{7,3},{8,4},{9,5},{1... | collective-permute-start | bytes 221192 | tf_op jit(solution)/shard_map/ppermute | solution.py:283
  45.1 0.2 blend.1.blend_ref
  45.3 2.0 %collective-permute-done.20.m2_ref = bf16[48,768]{1,0:T(8,128)(2,1)S(1)} collective-permute-done((bf16[48,768]{1,0:T(8,128)(2,1)S(1)}, bf16[48,768]{1,0:T(8,128)(2,1)S(1)}, u32[]{:S(2)}, u32[]{:S(2)}) %collective-permute-start.20) | collective-permute-done | bytes 73760 | tf_op jit(solution)/shard_map/ppermute | solution.py:283
  47.4 0.9 %mix.1 = bf16[16,3072]{1,0:T(8,128)(2,1)} custom-call(bf16[16,3072]{1,0:T(8,128)(2,1)S(1)} %get-tuple-element.12.hid_ref, bf16[192,128]{1,0:T(8,128)(2,1)S(1)} %blend.1.blend_ref, bf16[48,768]{1,0:T(8,128)(2,1)S(1)} %add_block.4.m0_ref, bf16[48,768]{1,0:T(8,128)(2,1)S(1)} %collective-permute-done.18.m1_ref, ...), custom_call_target="tpu_custom_call" | custom-call | tf_op jit(solution)/shard_map/mix/pallas_call | solution.py:332
  (51 shorter events, 0.5 us)
Async XLA Ops:
  0.0 21.9 %slice-start.3 = ((s8[12582912]{0:T(1024)(128)(4,1)}), s8[4194304]{0:T(1024)(128)(4,1)S(1)}, s32[]{:S(2)}) async-start(s8[12582912]{0:T(1024)(128)(4,1)} %bitcast.6), calls=%async_computation.3 | async-start | bytes 8388608
  0.0 21.9 %slice-start.6 = ((s8[12582912]{0:T(1024)(128)(4,1)}), s8[4194304]{0:T(1024)(128)(4,1)S(1)}, s32[]{:S(2)}) async-start(s8[12582912]{0:T(1024)(128)(4,1)} %bitcast.8), calls=%async_computation.6 | async-start | bytes 8388608
  0.0 21.9 %slice-start.1 = ((s8[12582912]{0:T(1024)(128)(4,1)}), s8[4194304]{0:T(1024)(128)(4,1)S(1)}, s32[]{:S(2)}) async-start(s8[12582912]{0:T(1024)(128)(4,1)} %bitcast.4), calls=%async_computation.1 | async-start | bytes 8388608
  0.0 21.9 %slice-start.2 = ((s8[12582912]{0:T(1024)(128)(4,1)}), s8[4194304]{0:T(1024)(128)(4,1)S(1)}, s32[]{:S(2)}) async-start(s8[12582912]{0:T(1024)(128)(4,1)} %bitcast.4), calls=%async_computation.2 | async-start | bytes 8388608
  0.0 21.9 %slice-start.4 = ((s8[12582912]{0:T(1024)(128)(4,1)}), s8[4194304]{0:T(1024)(128)(4,1)S(1)}, s32[]{:S(2)}) async-start(s8[12582912]{0:T(1024)(128)(4,1)} %bitcast.6), calls=%async_computation.4 | async-start | bytes 8388608
  0.0 21.9 %slice-start.5 = ((s8[12582912]{0:T(1024)(128)(4,1)}), s8[4194304]{0:T(1024)(128)(4,1)S(1)}, s32[]{:S(2)}) async-start(s8[12582912]{0:T(1024)(128)(4,1)} %bitcast.6), calls=%async_computation.5 | async-start | bytes 8388608
  0.0 21.9 %slice-start.7 = ((s8[12582912]{0:T(1024)(128)(4,1)}), s8[4194304]{0:T(1024)(128)(4,1)S(1)}, s32[]{:S(2)}) async-start(s8[12582912]{0:T(1024)(128)(4,1)} %bitcast.8), calls=%async_computation.7 | async-start | bytes 8388608
  0.0 21.9 %slice-start.8 = ((s8[12582912]{0:T(1024)(128)(4,1)}), s8[4194304]{0:T(1024)(128)(4,1)S(1)}, s32[]{:S(2)}) async-start(s8[12582912]{0:T(1024)(128)(4,1)} %bitcast.8), calls=%async_computation.8 | async-start | bytes 8388608
  0.1 21.9 %copy-start = (bf16[192,192]{1,0:T(8,128)(2,1)S(1)}, bf16[192,192]{1,0:T(8,128)(2,1)}, u32[]{:S(2)}) copy-start(bf16[192,192]{1,0:T(8,128)(2,1)} %constant.22.clone.refs_16_.refs_17_) | copy-start | bytes 221188
  3.4 8.6 %collective-permute-start = (bf16[48,768]{1,0:T(8,128)(2,1)S(1)}, bf16[48,768]{1,0:T(8,128)(2,1)S(1)}, u32[]{:S(2)}, u32[]{:S(2)}) collective-permute-start(bf16[48,768]{1,0:T(8,128)(2,1)S(1)} %get-tuple-element.14), channel_id=1, source_target_pairs={{0,4},{1,5},{2,6},{3,7},{4,8},{5,9},{6,10},{7,11},{8,12},{9,13},{1... | collective-permute-start | bytes 221192 | tf_op jit(solution)/shard_map/ppermute | solution.py:283
  6.5 7.5 %collective-permute-start.1 = (bf16[48,768]{1,0:T(8,128)(2,1)S(1)}, bf16[48,768]{1,0:T(8,128)(2,1)S(1)}, u32[]{:S(2)}, u32[]{:S(2)}) collective-permute-start(bf16[48,768]{1,0:T(8,128)(2,1)S(1)} %get-tuple-element.15), channel_id=1, source_target_pairs={{0,8},{1,9},{2,10},{3,11},{4,12},{5,13},{6,14},{7,15},{8,0},{9,1},... | collective-permute-start | bytes 221192 | tf_op jit(solution)/shard_map/ppermute | solution.py:283
  9.1 6.7 %collective-permute-start.2 = (bf16[48,768]{1,0:T(8,128)(2,1)S(1)}, bf16[48,768]{1,0:T(8,128)(2,1)S(1)}, u32[]{:S(2)}, u32[]{:S(2)}) collective-permute-start(bf16[48,768]{1,0:T(8,128)(2,1)S(1)} %get-tuple-element.16), channel_id=1, source_target_pairs={{0,12},{1,13},{2,14},{3,15},{4,0},{5,1},{6,2},{7,3},{8,4},{9,5},{1... | collective-permute-start | bytes 221192 | tf_op jit(solution)/shard_map/ppermute | solution.py:283
  10.4 5.6 %collective-permute-start.3 = (bf16[48,768]{1,0:T(8,128)(2,1)S(1)}, bf16[48,768]{1,0:T(8,128)(2,1)S(1)}, u32[]{:S(2)}, u32[]{:S(2)}) collective-permute-start(bf16[48,768]{1,0:T(8,128)(2,1)S(1)} %get-tuple-element.13.refs_0_), channel_id=1, source_target_pairs={{0,2},{1,3},{2,0},{3,1},{4,6},{5,7},{6,4},{7,5},{8,10},{9,11},{10,... | collective-permute-start | bytes 221192 | tf_op jit(solution)/shard_map/ppermute | solution.py:286
  12.0 4.1 %collective-permute-start.7 = (bf16[48,768]{1,0:T(8,128)(2,1)S(1)}, bf16[48,768]{1,0:T(8,128)(2,1)S(1)}, u32[]{:S(2)}, u32[]{:S(2)}) collective-permute-start(bf16[48,768]{1,0:T(8,128)(2,1)S(1)} %get-tuple-element.13.refs_0_), channel_id=1, source_target_pairs={{0,1},{1,0},{2,3},{3,2},{4,5},{5,4},{6,7},{7,6},{8,9},{9,8},{10,11... | collective-permute-start | bytes 221192 | tf_op jit(solution)/shard_map/ppermute | solution.py:286
  12.0 4.8 %collective-permute-start.4 = (bf16[48,768]{1,0:T(8,128)(2,1)S(1)}, bf16[48,768]{1,0:T(8,128)(2,1)S(1)}, u32[]{:S(2)}, u32[]{:S(2)}) collective-permute-start(bf16[48,768]{1,0:T(8,128)(2,1)S(1)} %collective-permute-done.refs_1_), channel_id=1, source_target_pairs={{0,2},{1,3},{2,0},{3,1},{4,6},{5,7},{6,4},{7,5},{8,10},{9,11},{10,... | collective-permute-start | bytes 221192 | tf_op jit(solution)/shard_map/ppermute | solution.py:286
  14.0 5.1 %collective-permute-start.5 = (bf16[48,768]{1,0:T(8,128)(2,1)S(1)}, bf16[48,768]{1,0:T(8,128)(2,1)S(1)}, u32[]{:S(2)}, u32[]{:S(2)}) collective-permute-start(bf16[48,768]{1,0:T(8,128)(2,1)S(1)} %collective-permute-done.1.refs_2_), channel_id=1, source_target_pairs={{0,2},{1,3},{2,0},{3,1},{4,6},{5,7},{6,4},{7,5},{8,10},{9,11},{10,... | collective-permute-start | bytes 221192 | tf_op jit(solution)/shard_map/ppermute | solution.py:286
  15.8 4.4 %collective-permute-start.6 = (bf16[48,768]{1,0:T(8,128)(2,1)S(1)}, bf16[48,768]{1,0:T(8,128)(2,1)S(1)}, u32[]{:S(2)}, u32[]{:S(2)}) collective-permute-start(bf16[48,768]{1,0:T(8,128)(2,1)S(1)} %collective-permute-done.2.refs_3_), channel_id=1, source_target_pairs={{0,2},{1,3},{2,0},{3,1},{4,6},{5,7},{6,4},{7,5},{8,10},{9,11},{10,... | collective-permute-start | bytes 221192 | tf_op jit(solution)/shard_map/ppermute | solution.py:286
  16.1 4.0 %collective-permute-start.11 = (bf16[48,768]{1,0:T(8,128)(2,1)S(1)}, bf16[48,768]{1,0:T(8,128)(2,1)S(1)}, u32[]{:S(2)}, u32[]{:S(2)}) collective-permute-start(bf16[48,768]{1,0:T(8,128)(2,1)S(1)} %collective-permute-done.3.refs_4_), channel_id=1, source_target_pairs={{0,1},{1,0},{2,3},{3,2},{4,5},{5,4},{6,7},{7,6},{8,9},{9,8},{10,11... | collective-permute-start | bytes 221192 | tf_op jit(solution)/shard_map/ppermute | solution.py:286
  16.1 4.5 %collective-permute-start.10 = (bf16[48,768]{1,0:T(8,128)(2,1)S(1)}, bf16[48,768]{1,0:T(8,128)(2,1)S(1)}, u32[]{:S(2)}, u32[]{:S(2)}) collective-permute-start(bf16[48,768]{1,0:T(8,128)(2,1)S(1)} %collective-permute-done.2.refs_3_), channel_id=1, source_target_pairs={{0,1},{1,0},{2,3},{3,2},{4,5},{5,4},{6,7},{7,6},{8,9},{9,8},{10,11... | collective-permute-start | bytes 221192 | tf_op jit(solution)/shard_map/ppermute | solution.py:286
  16.7 4.0 %collective-permute-start.8 = (bf16[48,768]{1,0:T(8,128)(2,1)S(1)}, bf16[48,768]{1,0:T(8,128)(2,1)S(1)}, u32[]{:S(2)}, u32[]{:S(2)}) collective-permute-start(bf16[48,768]{1,0:T(8,128)(2,1)S(1)} %collective-permute-done.refs_1_), channel_id=1, source_target_pairs={{0,1},{1,0},{2,3},{3,2},{4,5},{5,4},{6,7},{7,6},{8,9},{9,8},{10,11... | collective-permute-start | bytes 221192 | tf_op jit(solution)/shard_map/ppermute | solution.py:286
  19.2 1.5 %collective-permute-start.9 = (bf16[48,768]{1,0:T(8,128)(2,1)S(1)}, bf16[48,768]{1,0:T(8,128)(2,1)S(1)}, u32[]{:S(2)}, u32[]{:S(2)}) collective-permute-start(bf16[48,768]{1,0:T(8,128)(2,1)S(1)} %collective-permute-done.1.refs_2_), channel_id=1, source_target_pairs={{0,1},{1,0},{2,3},{3,2},{4,5},{5,4},{6,7},{7,6},{8,9},{9,8},{10,11... | collective-permute-start | bytes 221192 | tf_op jit(solution)/shard_map/ppermute | solution.py:286
  20.1 1.3 %collective-permute-start.12 = (bf16[48,768]{1,0:T(8,128)(2,1)S(1)}, bf16[48,768]{1,0:T(8,128)(2,1)S(1)}, u32[]{:S(2)}, u32[]{:S(2)}) collective-permute-start(bf16[48,768]{1,0:T(8,128)(2,1)S(1)} %collective-permute-done.4.refs_5_), channel_id=1, source_target_pairs={{0,1},{1,0},{2,3},{3,2},{4,5},{5,4},{6,7},{7,6},{8,9},{9,8},{10,11... | collective-permute-start | bytes 221192 | tf_op jit(solution)/shard_map/ppermute | solution.py:286
  20.1 1.4 %collective-permute-start.13 = (bf16[48,768]{1,0:T(8,128)(2,1)S(1)}, bf16[48,768]{1,0:T(8,128)(2,1)S(1)}, u32[]{:S(2)}, u32[]{:S(2)}) collective-permute-start(bf16[48,768]{1,0:T(8,128)(2,1)S(1)} %collective-permute-done.5.refs_6_), channel_id=1, source_target_pairs={{0,1},{1,0},{2,3},{3,2},{4,5},{5,4},{6,7},{7,6},{8,9},{9,8},{10,11... | collective-permute-start | bytes 221192 | tf_op jit(solution)/shard_map/ppermute | solution.py:286
  20.6 1.3 %collective-permute-start.14 = (bf16[48,768]{1,0:T(8,128)(2,1)S(1)}, bf16[48,768]{1,0:T(8,128)(2,1)S(1)}, u32[]{:S(2)}, u32[]{:S(2)}) collective-permute-start(bf16[48,768]{1,0:T(8,128)(2,1)S(1)} %collective-permute-done.6.refs_7_), channel_id=1, source_target_pairs={{0,1},{1,0},{2,3},{3,2},{4,5},{5,4},{6,7},{7,6},{8,9},{9,8},{10,11... | collective-permute-start | bytes 221192 | tf_op jit(solution)/shard_map/ppermute | solution.py:286
  31.0 2.2 %collective-permute-start.15 = (bf16[384,768]{1,0:T(8,128)(2,1)}, bf16[384,768]{1,0:T(8,128)(2,1)S(1)}, u32[]{:S(2)}, u32[]{:S(2)}) collective-permute-start(bf16[384,768]{1,0:T(8,128)(2,1)} %get-tuple-element.18), channel_id=1, source_target_pairs={{0,1},{1,0},{2,3},{3,2},{4,5},{5,4},{6,7},{7,6},{8,9},{9,8},{10,11... | collective-permute-start | bytes 1769480 | tf_op jit(solution)/shard_map/ppermute | solution.py:286
  33.4 5.2 %collective-permute-start.21 = (bf16[48,768]{1,0:T(8,128)(2,1)S(1)}, bf16[48,768]{1,0:T(8,128)(2,1)S(1)}, u32[]{:S(2)}, u32[]{:S(2)}) collective-permute-start(bf16[48,768]{1,0:T(8,128)(2,1)S(1)} %get-tuple-element.19), channel_id=1, source_target_pairs={{0,2},{1,3},{2,0},{3,1},{4,6},{5,7},{6,4},{7,5},{8,10},{9,11},{10,... | collective-permute-start | bytes 221192 | tf_op jit(solution)/shard_map/ppermute | solution.py:286
  34.4 5.8 %collective-permute-start.19 = (bf16[48,768]{1,0:T(8,128)(2,1)S(1)}, bf16[48,768]{1,0:T(8,128)(2,1)S(1)}, u32[]{:S(2)}, u32[]{:S(2)}) collective-permute-start(bf16[48,768]{1,0:T(8,128)(2,1)S(1)} %get-tuple-element.20), channel_id=1, source_target_pairs={{0,2},{1,3},{2,0},{3,1},{4,6},{5,7},{6,4},{7,5},{8,10},{9,11},{10,... | collective-permute-start | bytes 221192 | tf_op jit(solution)/shard_map/ppermute | solution.py:286
  35.5 7.0 %collective-permute-start.17 = (bf16[48,768]{1,0:T(8,128)(2,1)S(1)}, bf16[48,768]{1,0:T(8,128)(2,1)S(1)}, u32[]{:S(2)}, u32[]{:S(2)}) collective-permute-start(bf16[48,768]{1,0:T(8,128)(2,1)S(1)} %get-tuple-element.21), channel_id=1, source_target_pairs={{0,2},{1,3},{2,0},{3,1},{4,6},{5,7},{6,4},{7,5},{8,10},{9,11},{10,... | collective-permute-start | bytes 221192 | tf_op jit(solution)/shard_map/ppermute | solution.py:286
  36.5 8.8 %collective-permute-start.16 = (bf16[48,768]{1,0:T(8,128)(2,1)S(1)}, bf16[48,768]{1,0:T(8,128)(2,1)S(1)}, u32[]{:S(2)}, u32[]{:S(2)}) collective-permute-start(bf16[48,768]{1,0:T(8,128)(2,1)S(1)} %get-tuple-element.22), channel_id=1, source_target_pairs={{0,2},{1,3},{2,0},{3,1},{4,6},{5,7},{6,4},{7,5},{8,10},{9,11},{10,... | collective-permute-start | bytes 221192 | tf_op jit(solution)/shard_map/ppermute | solution.py:286
  38.6 6.7 %collective-permute-start.22 = (bf16[48,768]{1,0:T(8,128)(2,1)S(1)}, bf16[48,768]{1,0:T(8,128)(2,1)S(1)}, u32[]{:S(2)}, u32[]{:S(2)}) collective-permute-start(bf16[48,768]{1,0:T(8,128)(2,1)S(1)} %add_block.7), channel_id=1, source_target_pairs={{0,4},{1,5},{2,6},{3,7},{4,8},{5,9},{6,10},{7,11},{8,12},{9,13},{1... | collective-permute-start | bytes 221192 | tf_op jit(solution)/shard_map/ppermute | solution.py:283
  40.2 7.1 %collective-permute-start.20 = (bf16[48,768]{1,0:T(8,128)(2,1)S(1)}, bf16[48,768]{1,0:T(8,128)(2,1)S(1)}, u32[]{:S(2)}, u32[]{:S(2)}) collective-permute-start(bf16[48,768]{1,0:T(8,128)(2,1)S(1)} %add_block.6), channel_id=1, source_target_pairs={{0,8},{1,9},{2,10},{3,11},{4,12},{5,13},{6,14},{7,15},{8,0},{9,1},... | collective-permute-start | bytes 221192 | tf_op jit(solution)/shard_map/ppermute | solution.py:283
  42.6 4.8 %collective-permute-start.18 = (bf16[48,768]{1,0:T(8,128)(2,1)S(1)}, bf16[48,768]{1,0:T(8,128)(2,1)S(1)}, u32[]{:S(2)}, u32[]{:S(2)}) collective-permute-start(bf16[48,768]{1,0:T(8,128)(2,1)S(1)} %add_block.5), channel_id=1, source_target_pairs={{0,12},{1,13},{2,14},{3,15},{4,0},{5,1},{6,2},{7,3},{8,4},{9,5},{1... | collective-permute-start | bytes 221192 | tf_op jit(solution)/shard_map/ppermute | solution.py:283
  (3 other events, 45.3 us)

commit v4 on v3

--- a/solution.py
+++ b/solution.py
@@ -24,6 +24,7 @@
 PACK = FEAT * SLOTS
 GROUP = Q_HEADS // KV_HEADS
 LANES = FEAT * ROWS
+SHIFTS = (0, 1, 3, 2)
 MIB = 2**20
 BF16, F32, I32 = jnp.bfloat16, jnp.float32, jnp.int32
 
@@ -160,19 +161,22 @@
         out_ref[rows, LANES : 2 * LANES] = jnp.where(match, rest[s : s + 1, :], 0.0).astype(BF16)
 
 
+def slab_kernel(order_ref, *refs):
+    parts = dict(zip(SHIFTS, refs[:EXPERTS]))
+    packed = jnp.concatenate([parts[s][...] for s in range(EXPERTS)], axis=0)
+    refs[EXPERTS][...] = jnp.dot(order_ref[...], packed, preferred_element_type=F32).astype(BF16)
+
+
 def experts_kernel(slabs, *refs):
-    blocks = refs[: slabs * EXPERTS]
-    order_ref, back_ref, gate_ref, up_ref, down_ref = refs[slabs * EXPERTS : slabs * EXPERTS + 5]
-    outs = refs[slabs * EXPERTS + 5 : -3]
-    x_ref, a_ref, y_ref = refs[-3:]
+    joined = refs[:slabs]
+    gate_ref, up_ref, down_ref = refs[slabs : slabs + 3]
+    outs = refs[slabs + 3 : slabs + 5]
+    x_ref, a_ref = refs[slabs + 5 :]
     rows = EXPERTS * SLOTS
-    part = y_ref.shape[2]
-    order = order_ref[...]
+    part = joined[0].shape[1]
     for q in range(slabs):
-        packed = jnp.concatenate([b[...] for b in blocks[q * EXPERTS : (q + 1) * EXPERTS]], axis=0)
-        x = jnp.dot(order, packed, preferred_element_type=F32).astype(BF16)
         for f in range(FEAT):
-            x_ref[q * rows : (q + 1) * rows, f * part : (f + 1) * part] = x[f * rows : (f + 1) * rows]
+            x_ref[q * rows : (q + 1) * rows, f * part : (f + 1) * part] = joined[q][f * rows : (f + 1) * rows, :]
     x = x_ref[...]
     units = gate_ref.shape[1]
     tile = min(512, units)
@@ -184,14 +188,19 @@
     a = a_ref[...]
     for f in range(FEAT):
         span = slice(f * part, (f + 1) * part)
-        y_ref[f] = jnp.dot(a, down_ref[:, span], preferred_element_type=F32).astype(BF16)
-    back = back_ref[...]
-    for q in range(slabs):
-        stacked = jnp.concatenate([y_ref[f, q * rows : (q + 1) * rows, :] for f in range(FEAT)], axis=0)
-        packed = jnp.dot(back, stacked, preferred_element_type=F32).astype(BF16)
-        half = q // (slabs // 2)
-        at = (q % (slabs // 2)) * EXPERTS * PACK
-        outs[half][at : at + EXPERTS * PACK, :] = packed
+        y = jnp.dot(a, down_ref[:, span], preferred_element_type=F32).astype(BF16)
+        for q in range(slabs):
+            half = q // (slabs // 2)
+            at = (q % (slabs // 2)) * EXPERTS * PACK + f * rows
+            outs[half][at : at + rows, :] = y[q * rows : (q + 1) * rows]
+
+
+def add_pack_kernel(back_ref, keep_ref, came_ref, out_ref):
+    slab = EXPERTS * PACK
+    for q in range(2):
+        rows = slice(q * slab, (q + 1) * slab)
+        total = (keep_ref[rows, :].astype(F32) + came_ref[rows, :].astype(F32)).astype(BF16)
+        out_ref[rows, :] = jnp.dot(back_ref[...], total, preferred_element_type=F32).astype(BF16)
 
 
 def mix_kernel(hid_ref, blend_ref, m0_ref, m1_ref, m2_ref, m3_ref, out_ref):
@@ -285,43 +294,53 @@
     def swapped(x, bit):
         return lax.ppermute(x, "attn", [(i, i ^ bit) for i in range(devices)])
 
-    got = [blocks[0]] + [shifted(blocks[s], s) for s in range(1, EXPERTS)]
-    bit = splits // 2
-    while bit >= 1:
-        got = got + [swapped(b, bit) for b in got]
-        bit //= 2
-    total = splits * EXPERTS * SLOTS
     to = np.arange(EXPERTS * PACK)
     f, s, j = to // (EXPERTS * SLOTS), to // SLOTS % EXPERTS, to % SLOTS
     order = np.zeros((EXPERTS * PACK, EXPERTS * PACK), np.float32)
     order[to, s * PACK + f * SLOTS + j] = 1.0
+    back = jnp.asarray(order.T, BF16)
+    order = jnp.asarray(order, BF16)
+    slab = jax.ShapeDtypeStruct((EXPERTS * PACK, part), BF16)
+
+    def joined(group):
+        return pl.pallas_call(
+            slab_kernel, out_shape=slab, in_specs=[VMEM] * (1 + EXPERTS), out_specs=VMEM,
+            compiler_params=params(4), name="slab",
+        )(order, *group)
+
+    got = [blocks[0]] + [shifted(blocks[s], s) for s in SHIFTS[1:]]
+    bit = splits // 2
+    while bit >= 2:
+        got = got + [swapped(b, bit) for b in got]
+        bit //= 2
+    slabs = [joined(got[i : i + EXPERTS]) for i in range(0, len(got), EXPERTS)]
+    slabs = slabs + [swapped(b, 1) for b in slabs]
+    total = splits * EXPERTS * SLOTS
     weights = [pltpu.with_memory_space_constraint(w, pltpu.VMEM) for w in (gate_weight, up_weight, down_weight)]
     units = gate_weight.shape[1]
     keep, send = pl.pallas_call(
         functools.partial(experts_kernel, splits),
         out_shape=[jax.ShapeDtypeStruct((splits // 2 * EXPERTS * PACK, part), BF16)] * 2,
-        in_specs=[VMEM] * (splits * EXPERTS + 5),
+        in_specs=[VMEM] * (splits + 3),
         out_specs=[VMEM] * 2,
-        scratch_shapes=[
-            pltpu.VMEM((total, width), BF16),
-            pltpu.VMEM((total, units), BF16),
-            pltpu.VMEM((FEAT, total, part), BF16),
-        ],
+        scratch_shapes=[pltpu.VMEM((total, width), BF16), pltpu.VMEM((total, units), BF16)],
         compiler_params=params(16 if total <= 192 else 36),
         cost_estimate=pl.CostEstimate(
             flops=6 * total * width * units, bytes_accessed=6 * width * units, transcendentals=0
         ),
         name="experts",
-    )(*got, jnp.asarray(order, BF16), jnp.asarray(order.T, BF16), *weights)
-
-    def plus(a, b):
-        return (a.astype(F32) + b.astype(F32)).astype(BF16)
-
-    keep = plus(keep, swapped(send, 1))
+    )(*slabs, *weights)
+
+    came = swapped(send, 1)
     rows, bit = keep.shape[0], 2
     while rows > EXPERTS * PACK * 2:
-        keep = plus(keep[: rows // 2], swapped(keep[rows // 2 :], bit))
+        both = (keep.astype(F32) + came.astype(F32)).astype(BF16)
+        keep, came = both[: rows // 2], swapped(both[rows // 2 :], bit)
         rows, bit = rows // 2, bit * 2
+    keep = pl.pallas_call(
+        add_pack_kernel, out_shape=jax.ShapeDtypeStruct((rows, part), BF16), in_specs=[VMEM] * 3,
+        out_specs=VMEM, compiler_params=params(6), name="add_pack",
+    )(back, keep, came)
     summed = [None] * EXPERTS
     came = {}
     for s in (2, 1, 3, 0):

time: 48.4 us -> 47.4 us (0.979)
  starting transfers between devices: 22.1 us -> 20.2 us
  waiting for transfers between devices: 12.1 us -> 13.1 us
    ppermute x6, waiting for transfers between devices: 2.96 us -> 5.17 us  [shifted(): lax.ppermute(x, 'attn', [(i, (i + s * splits) % devices) for i in range(d...]
    ppermute x6, starting transfers between devices: 12.1 us -> 10.5 us  [shifted(): lax.ppermute(x, 'attn', [(i, (i + s * splits) % devices) for i in range(d...]
    ppermute x17 -> x11, waiting for transfers between devices: 9.17 us -> 7.98 us  [swapped(): return lax.ppermute(x, 'attn', [(i, i ^ bit) for i in range(devices)])]
    pallas_call x0 -> x3, Pallas kernels: none -> 0.79 us  [the longest x2 0.46 us: joined(): pl.pallas_call(slab_kernel, out_shape=slab, in_specs=[VMEM] * (1 + EXPERT...]
    pallas_call x1, Pallas kernels: 9.02 us -> 8.32 us  [local(): pl.pallas_call(functools.partial(experts_kernel, splits), out_shape=[jax....]
    ppermute x17 -> x11, starting transfers between devices: 10.1 us -> 9.71 us  [swapped(): return lax.ppermute(x, 'attn', [(i, i ^ bit) for i in range(devices)])]
  transfers between devices with their start and end apart: 23 -> 17, of which waited for: 12 -> 10; matrix products, arithmetic and copies ran while one was open for 0% -> 0% of each run, Pallas kernels for 1% -> 2%
where the time goes in v4:
time: 47.4 us; the launch traced here: 47.2 us
  starting transfers between devices  20.2 us (43%)
  Pallas kernels  13.6 us (29%)
  waiting for transfers between devices  13.1 us (28%)
    ppermute x6, starting transfers between devices, shifted(): lax.ppermute(x, 'attn', [(i, (i + s * splits) % devices) for i in range(d...  10.5 us
    ppermute x11, starting transfers between devices, swapped(): return lax.ppermute(x, 'attn', [(i, i ^ bit) for i in range(devices)])  9.71 us
    pallas_call x1, Pallas kernels, local(): pl.pallas_call(functools.partial(experts_kernel, splits), out_shape=[jax....  8.32 us
    ppermute x11, waiting for transfers between devices, swapped(): return lax.ppermute(x, 'attn', [(i, i ^ bit) for i in range(devices)])  7.98 us
    ppermute x6, waiting for transfers between devices, shifted(): lax.ppermute(x, 'attn', [(i, (i + s * splits) % devices) for i in range(d...  5.17 us
    pallas_call x1, Pallas kernels, attention(): pl.pallas_call(attention_kernel, out_shape=[jax.ShapeDtypeStruct((ROWS, w...  3.35 us
  transfers between devices with their start and end apart: 17, of which 10 were waited for; matrix products, arithmetic and copies ran while one was open for 0% of the time, Pallas kernels for 2%

profile of v4, /device:TPU:0, one launch (start us, length us, event | category | flops | bytes accessed | tf_op | source)
XLA Modules:
  0.0 47.2 jit_solution(14175468011370033259)
XLA Ops:
  0.0 3.4 %attention.1 = (bf16[16,3072]{1,0:T(8,128)(2,1)S(1)}, bf16[48,768]{1,0:T(8,128)(2,1)S(1)}, bf16[48,768]{1,0:T(8,128)(2,1)S(1)}, bf16[48,768]{1,0:T(8,128)(2,1)S(1)}, bf16[48,768]{1,0:T(8,128)(2,1)S(1)}) custom-call(s32[1]{0:T(128)} %bitcast.plane_ref, s32[16]{0:T(128)} %refs_0_.1, bf16[16,3072]{1,0:T(8,128)(2,1)} %refs_1_.1, bf16[16,3072]{1,0:T(8,128)(2,1)} %refs_2_.1, ...), custom_call_target="tpu_custom_call" | custom-call | flops 40000000000 | bytes 4000000 | tf_op jit(solution)/shard_map/attention/pallas_call | solution.py:230
  3.4 3.1 %collective-permute-start = (bf16[48,768]{1,0:T(8,128)(2,1)S(1)}, bf16[48,768]{1,0:T(8,128)(2,1)S(1)}, u32[]{:S(2)}, u32[]{:S(2)}) collective-permute-start(bf16[48,768]{1,0:T(8,128)(2,1)S(1)} %get-tuple-element.14), channel_id=1, source_target_pairs={{0,4},{1,5},{2,6},{3,7},{4,8},{5,9},{6,10},{7,11},{8,12},{9,13},{1... | collective-permute-start | bytes 221192 | tf_op jit(solution)/shard_map/ppermute | solution.py:292
  6.5 2.1 %collective-permute-start.1 = (bf16[48,768]{1,0:T(8,128)(2,1)S(1)}, bf16[48,768]{1,0:T(8,128)(2,1)S(1)}, u32[]{:S(2)}, u32[]{:S(2)}) collective-permute-start(bf16[48,768]{1,0:T(8,128)(2,1)S(1)} %get-tuple-element.15), channel_id=1, source_target_pairs={{0,12},{1,13},{2,14},{3,15},{4,0},{5,1},{6,2},{7,3},{8,4},{9,5},{1... | collective-permute-start | bytes 221192 | tf_op jit(solution)/shard_map/ppermute | solution.py:292
  8.6 1.0 %collective-permute-start.2 = (bf16[48,768]{1,0:T(8,128)(2,1)S(1)}, bf16[48,768]{1,0:T(8,128)(2,1)S(1)}, u32[]{:S(2)}, u32[]{:S(2)}) collective-permute-start(bf16[48,768]{1,0:T(8,128)(2,1)S(1)} %get-tuple-element.16), channel_id=1, source_target_pairs={{0,8},{1,9},{2,10},{3,11},{4,12},{5,13},{6,14},{7,15},{8,0},{9,1},... | collective-permute-start | bytes 221192 | tf_op jit(solution)/shard_map/ppermute | solution.py:292
  9.5 1.5 %collective-permute-start.3 = (bf16[48,768]{1,0:T(8,128)(2,1)S(1)}, bf16[48,768]{1,0:T(8,128)(2,1)S(1)}, u32[]{:S(2)}, u32[]{:S(2)}) collective-permute-start(bf16[48,768]{1,0:T(8,128)(2,1)S(1)} %get-tuple-element.13.refs_0_), channel_id=1, source_target_pairs={{0,2},{1,3},{2,0},{3,1},{4,6},{5,7},{6,4},{7,5},{8,10},{9,11},{10,... | collective-permute-start | bytes 221192 | tf_op jit(solution)/shard_map/ppermute | solution.py:295
  11.1 2.0 %collective-permute-start.4 = (bf16[48,768]{1,0:T(8,128)(2,1)S(1)}, bf16[48,768]{1,0:T(8,128)(2,1)S(1)}, u32[]{:S(2)}, u32[]{:S(2)}) collective-permute-start(bf16[48,768]{1,0:T(8,128)(2,1)S(1)} %collective-permute-done.refs_1_), channel_id=1, source_target_pairs={{0,2},{1,3},{2,0},{3,1},{4,6},{5,7},{6,4},{7,5},{8,10},{9,11},{10,... | collective-permute-start | bytes 221192 | tf_op jit(solution)/shard_map/ppermute | solution.py:295
  13.1 0.3 collective-permute-start.5
  13.3 2.2 %collective-permute-done.2.refs_3_ = bf16[48,768]{1,0:T(8,128)(2,1)S(1)} collective-permute-done((bf16[48,768]{1,0:T(8,128)(2,1)S(1)}, bf16[48,768]{1,0:T(8,128)(2,1)S(1)}, u32[]{:S(2)}, u32[]{:S(2)}) %collective-permute-start.2) | collective-permute-done | bytes 73760 | tf_op jit(solution)/shard_map/ppermute | solution.py:292
  15.5 1.5 %collective-permute-start.6 = (bf16[48,768]{1,0:T(8,128)(2,1)S(1)}, bf16[48,768]{1,0:T(8,128)(2,1)S(1)}, u32[]{:S(2)}, u32[]{:S(2)}) collective-permute-start(bf16[48,768]{1,0:T(8,128)(2,1)S(1)} %collective-permute-done.2.refs_3_), channel_id=1, source_target_pairs={{0,2},{1,3},{2,0},{3,1},{4,6},{5,7},{6,4},{7,5},{8,10},{9,11},{10,... | collective-permute-start | bytes 221192 | tf_op jit(solution)/shard_map/ppermute | solution.py:295
  17.0 0.2 slab.2.refs_0_
  17.3 0.1 collective-permute-start.7
  17.4 2.4 %collective-permute-done.6.refs_3_ = bf16[48,768]{1,0:T(8,128)(2,1)S(1)} collective-permute-done((bf16[48,768]{1,0:T(8,128)(2,1)S(1)}, bf16[48,768]{1,0:T(8,128)(2,1)S(1)}, u32[]{:S(2)}, u32[]{:S(2)}) %collective-permute-start.6) | collective-permute-done | bytes 73760 | tf_op jit(solution)/shard_map/ppermute | solution.py:295
  19.8 0.2 slab.3.refs_1_
  20.2 1.6 %collective-permute-done.8.refs_3_ = bf16[192,768]{1,0:T(8,128)(2,1)S(1)} collective-permute-done((bf16[192,768]{1,0:T(8,128)(2,1)S(1)}, bf16[192,768]{1,0:T(8,128)(2,1)S(1)}, u32[]{:S(2)}, u32[]{:S(2)}) %collective-permute-start.8) | collective-permute-done | bytes 294944 | tf_op jit(solution)/shard_map/ppermute | solution.py:295
  21.8 8.3 %experts.1 = (bf16[384,768]{1,0:T(8,128)(2,1)S(1)}, bf16[384,768]{1,0:T(8,128)(2,1)}) custom-call(bf16[192,768]{1,0:T(8,128)(2,1)S(1)} %slab.2.refs_0_, bf16[192,768]{1,0:T(8,128)(2,1)S(1)} %slab.3.refs_1_, bf16[192,768]{1,0:T(8,128)(2,1)S(1)} %collective-permute-done.7.refs_2_, bf16[192,768]{1,0:T(8,128)(2,1)S(1)} %collective-permute-done.8.refs_3_, ...), custom_call_target="tpu_custom_call" | custom-call | flops 7247757312 | bytes 37748736 | tf_op jit(solution)/shard_map/experts/pallas_call | solution.py:321
  30.1 0.1 collective-permute-start.9
  30.2 2.1 %collective-permute-done.9.came_ref = bf16[384,768]{1,0:T(8,128)(2,1)S(1)} collective-permute-done((bf16[384,768]{1,0:T(8,128)(2,1)}, bf16[384,768]{1,0:T(8,128)(2,1)S(1)}, u32[]{:S(2)}, u32[]{:S(2)}) %collective-permute-start.9) | collective-permute-done | bytes 589856 | tf_op jit(solution)/shard_map/ppermute | solution.py:295
  32.3 0.3 add_pack.1.keep_ref
  32.7 1.6 %collective-permute-start.15 = (bf16[48,768]{1,0:T(8,128)(2,1)S(1)}, bf16[48,768]{1,0:T(8,128)(2,1)S(1)}, u32[]{:S(2)}, u32[]{:S(2)}) collective-permute-start(bf16[48,768]{1,0:T(8,128)(2,1)S(1)} %get-tuple-element.19), channel_id=1, source_target_pairs={{0,2},{1,3},{2,0},{3,1},{4,6},{5,7},{6,4},{7,5},{8,10},{9,11},{10,... | collective-permute-start | bytes 221192 | tf_op jit(solution)/shard_map/ppermute | solution.py:295
  34.3 0.5 %collective-permute-start.13 = (bf16[48,768]{1,0:T(8,128)(2,1)S(1)}, bf16[48,768]{1,0:T(8,128)(2,1)S(1)}, u32[]{:S(2)}, u32[]{:S(2)}) collective-permute-start(bf16[48,768]{1,0:T(8,128)(2,1)S(1)} %get-tuple-element.20), channel_id=1, source_target_pairs={{0,2},{1,3},{2,0},{3,1},{4,6},{5,7},{6,4},{7,5},{8,10},{9,11},{10,... | collective-permute-start | bytes 221192 | tf_op jit(solution)/shard_map/ppermute | solution.py:295
  34.8 1.5 %collective-permute-start.11 = (bf16[48,768]{1,0:T(8,128)(2,1)S(1)}, bf16[48,768]{1,0:T(8,128)(2,1)S(1)}, u32[]{:S(2)}, u32[]{:S(2)}) collective-permute-start(bf16[48,768]{1,0:T(8,128)(2,1)S(1)} %get-tuple-element.21), channel_id=1, source_target_pairs={{0,2},{1,3},{2,0},{3,1},{4,6},{5,7},{6,4},{7,5},{8,10},{9,11},{10,... | collective-permute-start | bytes 221192 | tf_op jit(solution)/shard_map/ppermute | solution.py:295
  36.3 0.5 %collective-permute-start.10 = (bf16[48,768]{1,0:T(8,128)(2,1)S(1)}, bf16[48,768]{1,0:T(8,128)(2,1)S(1)}, u32[]{:S(2)}, u32[]{:S(2)}) collective-permute-start(bf16[48,768]{1,0:T(8,128)(2,1)S(1)} %get-tuple-element.22), channel_id=1, source_target_pairs={{0,2},{1,3},{2,0},{3,1},{4,6},{5,7},{6,4},{7,5},{8,10},{9,11},{10,... | collective-permute-start | bytes 221192 | tf_op jit(solution)/shard_map/ppermute | solution.py:295
  36.8 0.7 %collective-permute-done.15.came_ref = bf16[48,768]{1,0:T(8,128)(2,1)S(1)} collective-permute-done((bf16[48,768]{1,0:T(8,128)(2,1)S(1)}, bf16[48,768]{1,0:T(8,128)(2,1)S(1)}, u32[]{:S(2)}, u32[]{:S(2)}) %collective-permute-start.15) | collective-permute-done | bytes 73760 | tf_op jit(solution)/shard_map/ppermute | solution.py:295
  37.6 1.5 %collective-permute-start.16 = (bf16[48,768]{1,0:T(8,128)(2,1)S(1)}, bf16[48,768]{1,0:T(8,128)(2,1)S(1)}, u32[]{:S(2)}, u32[]{:S(2)}) collective-permute-start(bf16[48,768]{1,0:T(8,128)(2,1)S(1)} %add_block.7), channel_id=1, source_target_pairs={{0,4},{1,5},{2,6},{3,7},{4,8},{5,9},{6,10},{7,11},{8,12},{9,13},{1... | collective-permute-start | bytes 221192 | tf_op jit(solution)/shard_map/ppermute | solution.py:292
  39.0 0.4 collective-permute-done.13.came_ref
  39.5 0.8 %collective-permute-start.14 = (bf16[48,768]{1,0:T(8,128)(2,1)S(1)}, bf16[48,768]{1,0:T(8,128)(2,1)S(1)}, u32[]{:S(2)}, u32[]{:S(2)}) collective-permute-start(bf16[48,768]{1,0:T(8,128)(2,1)S(1)} %add_block.6), channel_id=1, source_target_pairs={{0,8},{1,9},{2,10},{3,11},{4,12},{5,13},{6,14},{7,15},{8,0},{9,1},... | collective-permute-start | bytes 221192 | tf_op jit(solution)/shard_map/ppermute | solution.py:292
  40.3 0.7 %collective-permute-done.11.came_ref = bf16[48,768]{1,0:T(8,128)(2,1)S(1)} collective-permute-done((bf16[48,768]{1,0:T(8,128)(2,1)S(1)}, bf16[48,768]{1,0:T(8,128)(2,1)S(1)}, u32[]{:S(2)}, u32[]{:S(2)}) %collective-permute-start.11) | collective-permute-done | bytes 73760 | tf_op jit(solution)/shard_map/ppermute | solution.py:295
  41.0 2.1 %collective-permute-start.12 = (bf16[48,768]{1,0:T(8,128)(2,1)S(1)}, bf16[48,768]{1,0:T(8,128)(2,1)S(1)}, u32[]{:S(2)}, u32[]{:S(2)}) collective-permute-start(bf16[48,768]{1,0:T(8,128)(2,1)S(1)} %add_block.5), channel_id=1, source_target_pairs={{0,12},{1,13},{2,14},{3,15},{4,0},{5,1},{6,2},{7,3},{8,4},{9,5},{1... | collective-permute-start | bytes 221192 | tf_op jit(solution)/shard_map/ppermute | solution.py:292
  43.1 0.2 blend.1.blend_ref
  43.4 1.1 %collective-permute-done.16.m3_ref = bf16[48,768]{1,0:T(8,128)(2,1)S(1)} collective-permute-done((bf16[48,768]{1,0:T(8,128)(2,1)S(1)}, bf16[48,768]{1,0:T(8,128)(2,1)S(1)}, u32[]{:S(2)}, u32[]{:S(2)}) %collective-permute-start.16) | collective-permute-done | bytes 73760 | tf_op jit(solution)/shard_map/ppermute | solution.py:292
  44.5 1.9 %collective-permute-done.14.m2_ref = bf16[48,768]{1,0:T(8,128)(2,1)S(1)} collective-permute-done((bf16[48,768]{1,0:T(8,128)(2,1)S(1)}, bf16[48,768]{1,0:T(8,128)(2,1)S(1)}, u32[]{:S(2)}, u32[]{:S(2)}) %collective-permute-start.14) | collective-permute-done | bytes 73760 | tf_op jit(solution)/shard_map/ppermute | solution.py:292
  46.4 0.9 %mix.1 = bf16[16,3072]{1,0:T(8,128)(2,1)} custom-call(bf16[16,3072]{1,0:T(8,128)(2,1)S(1)} %get-tuple-element.12.hid_ref, bf16[192,128]{1,0:T(8,128)(2,1)S(1)} %blend.1.blend_ref, bf16[48,768]{1,0:T(8,128)(2,1)S(1)} %add_block.4.m0_ref, bf16[48,768]{1,0:T(8,128)(2,1)S(1)} %collective-permute-done.12.m1_ref, ...), custom_call_target="tpu_custom_call" | custom-call | tf_op jit(solution)/shard_map/mix/pallas_call | solution.py:351
  (26 shorter events, 0.3 us)
Async XLA Ops:
  0.0 17.0 %copy-start.3 = (bf16[192,192]{1,0:T(8,128)(2,1)S(1)}, bf16[192,192]{1,0:T(8,128)(2,1)}, u32[]{:S(2)}) copy-start(bf16[192,192]{1,0:T(8,128)(2,1)} %constant.22.clone.order_ref.back_ref) | copy-start | bytes 221188
  0.0 21.8 %copy-start = (bf16[3072,2048]{1,0:T(8,128)(2,1)S(1)}, bf16[3072,2048]{1,0:T(8,128)(2,1)}, u32[]{:S(2)}) copy-start(bf16[3072,2048]{1,0:T(8,128)(2,1)} %refs_4_.3) | copy-start | bytes 37748740
  0.0 21.8 %copy-start.1 = (bf16[3072,2048]{1,0:T(8,128)(2,1)S(1)}, bf16[3072,2048]{1,0:T(8,128)(2,1)}, u32[]{:S(2)}) copy-start(bf16[3072,2048]{1,0:T(8,128)(2,1)} %refs_5_.3) | copy-start | bytes 37748740
  0.0 21.8 %copy-start.2 = (bf16[2048,3072]{1,0:T(8,128)(2,1)S(1)}, bf16[2048,3072]{1,0:T(8,128)(2,1)}, u32[]{:S(2)}) copy-start(bf16[2048,3072]{1,0:T(8,128)(2,1)} %refs_6_.3) | copy-start | bytes 37748740
  3.4 7.7 %collective-permute-start = (bf16[48,768]{1,0:T(8,128)(2,1)S(1)}, bf16[48,768]{1,0:T(8,128)(2,1)S(1)}, u32[]{:S(2)}, u32[]{:S(2)}) collective-permute-start(bf16[48,768]{1,0:T(8,128)(2,1)S(1)} %get-tuple-element.14), channel_id=1, source_target_pairs={{0,4},{1,5},{2,6},{3,7},{4,8},{5,9},{6,10},{7,11},{8,12},{9,13},{1... | collective-permute-start | bytes 221192 | tf_op jit(solution)/shard_map/ppermute | solution.py:292
  6.5 6.6 %collective-permute-start.1 = (bf16[48,768]{1,0:T(8,128)(2,1)S(1)}, bf16[48,768]{1,0:T(8,128)(2,1)S(1)}, u32[]{:S(2)}, u32[]{:S(2)}) collective-permute-start(bf16[48,768]{1,0:T(8,128)(2,1)S(1)} %get-tuple-element.15), channel_id=1, source_target_pairs={{0,12},{1,13},{2,14},{3,15},{4,0},{5,1},{6,2},{7,3},{8,4},{9,5},{1... | collective-permute-start | bytes 221192 | tf_op jit(solution)/shard_map/ppermute | solution.py:292
  8.6 6.9 %collective-permute-start.2 = (bf16[48,768]{1,0:T(8,128)(2,1)S(1)}, bf16[48,768]{1,0:T(8,128)(2,1)S(1)}, u32[]{:S(2)}, u32[]{:S(2)}) collective-permute-start(bf16[48,768]{1,0:T(8,128)(2,1)S(1)} %get-tuple-element.16), channel_id=1, source_target_pairs={{0,8},{1,9},{2,10},{3,11},{4,12},{5,13},{6,14},{7,15},{8,0},{9,1},... | collective-permute-start | bytes 221192 | tf_op jit(solution)/shard_map/ppermute | solution.py:292
  9.5 7.8 %collective-permute-start.3 = (bf16[48,768]{1,0:T(8,128)(2,1)S(1)}, bf16[48,768]{1,0:T(8,128)(2,1)S(1)}, u32[]{:S(2)}, u32[]{:S(2)}) collective-permute-start(bf16[48,768]{1,0:T(8,128)(2,1)S(1)} %get-tuple-element.13.refs_0_), channel_id=1, source_target_pairs={{0,2},{1,3},{2,0},{3,1},{4,6},{5,7},{6,4},{7,5},{8,10},{9,11},{10,... | collective-permute-start | bytes 221192 | tf_op jit(solution)/shard_map/ppermute | solution.py:295
  11.1 6.3 %collective-permute-start.4 = (bf16[48,768]{1,0:T(8,128)(2,1)S(1)}, bf16[48,768]{1,0:T(8,128)(2,1)S(1)}, u32[]{:S(2)}, u32[]{:S(2)}) collective-permute-start(bf16[48,768]{1,0:T(8,128)(2,1)S(1)} %collective-permute-done.refs_1_), channel_id=1, source_target_pairs={{0,2},{1,3},{2,0},{3,1},{4,6},{5,7},{6,4},{7,5},{8,10},{9,11},{10,... | collective-permute-start | bytes 221192 | tf_op jit(solution)/shard_map/ppermute | solution.py:295
  13.1 4.4 %collective-permute-start.5 = (bf16[48,768]{1,0:T(8,128)(2,1)S(1)}, bf16[48,768]{1,0:T(8,128)(2,1)S(1)}, u32[]{:S(2)}, u32[]{:S(2)}) collective-permute-start(bf16[48,768]{1,0:T(8,128)(2,1)S(1)} %collective-permute-done.1.refs_2_), channel_id=1, source_target_pairs={{0,2},{1,3},{2,0},{3,1},{4,6},{5,7},{6,4},{7,5},{8,10},{9,11},{10,... | collective-permute-start | bytes 221192 | tf_op jit(solution)/shard_map/ppermute | solution.py:295
  15.5 4.4 %collective-permute-start.6 = (bf16[48,768]{1,0:T(8,128)(2,1)S(1)}, bf16[48,768]{1,0:T(8,128)(2,1)S(1)}, u32[]{:S(2)}, u32[]{:S(2)}) collective-permute-start(bf16[48,768]{1,0:T(8,128)(2,1)S(1)} %collective-permute-done.2.refs_3_), channel_id=1, source_target_pairs={{0,2},{1,3},{2,0},{3,1},{4,6},{5,7},{6,4},{7,5},{8,10},{9,11},{10,... | collective-permute-start | bytes 221192 | tf_op jit(solution)/shard_map/ppermute | solution.py:295
  17.3 2.9 %collective-permute-start.7 = (bf16[192,768]{1,0:T(8,128)(2,1)S(1)}, bf16[192,768]{1,0:T(8,128)(2,1)S(1)}, u32[]{:S(2)}, u32[]{:S(2)}) collective-permute-start(bf16[192,768]{1,0:T(8,128)(2,1)S(1)} %slab.2.refs_0_), channel_id=1, source_target_pairs={{0,1},{1,0},{2,3},{3,2},{4,5},{5,4},{6,7},{7,6},{8,9},{9,8},{10,11... | collective-permute-start | bytes 884744 | tf_op jit(solution)/shard_map/ppermute | solution.py:295
  20.1 23.0 %copy-start.4 = (s32[16,2]{0,1:T(2,128)S(1)}, s32[16,2]{0,1:T(2,128)}, u32[]{:S(2)}) copy-start(s32[16,2]{0,1:T(2,128)} %param.23) | copy-start | bytes 388
  20.1 23.0 %copy-start.5 = (s32[16,2]{0,1:T(2,128)S(1)}, s32[16,2]{0,1:T(2,128)}, u32[]{:S(2)}) copy-start(s32[16,2]{0,1:T(2,128)} %param.24) | copy-start | bytes 388
  20.1 1.6 %collective-permute-start.8 = (bf16[192,768]{1,0:T(8,128)(2,1)S(1)}, bf16[192,768]{1,0:T(8,128)(2,1)S(1)}, u32[]{:S(2)}, u32[]{:S(2)}) collective-permute-start(bf16[192,768]{1,0:T(8,128)(2,1)S(1)} %slab.3.refs_1_), channel_id=1, source_target_pairs={{0,1},{1,0},{2,3},{3,2},{4,5},{5,4},{6,7},{7,6},{8,9},{9,8},{10,11... | collective-permute-start | bytes 884744 | tf_op jit(solution)/shard_map/ppermute | solution.py:295
  30.1 2.2 %collective-permute-start.9 = (bf16[384,768]{1,0:T(8,128)(2,1)}, bf16[384,768]{1,0:T(8,128)(2,1)S(1)}, u32[]{:S(2)}, u32[]{:S(2)}) collective-permute-start(bf16[384,768]{1,0:T(8,128)(2,1)} %get-tuple-element.18), channel_id=1, source_target_pairs={{0,1},{1,0},{2,3},{3,2},{4,5},{5,4},{6,7},{7,6},{8,9},{9,8},{10,11... | collective-permute-start | bytes 1769480 | tf_op jit(solution)/shard_map/ppermute | solution.py:295
  32.7 4.9 %collective-permute-start.15 = (bf16[48,768]{1,0:T(8,128)(2,1)S(1)}, bf16[48,768]{1,0:T(8,128)(2,1)S(1)}, u32[]{:S(2)}, u32[]{:S(2)}) collective-permute-start(bf16[48,768]{1,0:T(8,128)(2,1)S(1)} %get-tuple-element.19), channel_id=1, source_target_pairs={{0,2},{1,3},{2,0},{3,1},{4,6},{5,7},{6,4},{7,5},{8,10},{9,11},{10,... | collective-permute-start | bytes 221192 | tf_op jit(solution)/shard_map/ppermute | solution.py:295
  34.3 5.2 %collective-permute-start.13 = (bf16[48,768]{1,0:T(8,128)(2,1)S(1)}, bf16[48,768]{1,0:T(8,128)(2,1)S(1)}, u32[]{:S(2)}, u32[]{:S(2)}) collective-permute-start(bf16[48,768]{1,0:T(8,128)(2,1)S(1)} %get-tuple-element.20), channel_id=1, source_target_pairs={{0,2},{1,3},{2,0},{3,1},{4,6},{5,7},{6,4},{7,5},{8,10},{9,11},{10,... | collective-permute-start | bytes 221192 | tf_op jit(solution)/shard_map/ppermute | solution.py:295
  34.8 6.2 %collective-permute-start.11 = (bf16[48,768]{1,0:T(8,128)(2,1)S(1)}, bf16[48,768]{1,0:T(8,128)(2,1)S(1)}, u32[]{:S(2)}, u32[]{:S(2)}) collective-permute-start(bf16[48,768]{1,0:T(8,128)(2,1)S(1)} %get-tuple-element.21), channel_id=1, source_target_pairs={{0,2},{1,3},{2,0},{3,1},{4,6},{5,7},{6,4},{7,5},{8,10},{9,11},{10,... | collective-permute-start | bytes 221192 | tf_op jit(solution)/shard_map/ppermute | solution.py:295
  36.3 7.0 %collective-permute-start.10 = (bf16[48,768]{1,0:T(8,128)(2,1)S(1)}, bf16[48,768]{1,0:T(8,128)(2,1)S(1)}, u32[]{:S(2)}, u32[]{:S(2)}) collective-permute-start(bf16[48,768]{1,0:T(8,128)(2,1)S(1)} %get-tuple-element.22), channel_id=1, source_target_pairs={{0,2},{1,3},{2,0},{3,1},{4,6},{5,7},{6,4},{7,5},{8,10},{9,11},{10,... | collective-permute-start | bytes 221192 | tf_op jit(solution)/shard_map/ppermute | solution.py:295
  37.6 6.9 %collective-permute-start.16 = (bf16[48,768]{1,0:T(8,128)(2,1)S(1)}, bf16[48,768]{1,0:T(8,128)(2,1)S(1)}, u32[]{:S(2)}, u32[]{:S(2)}) collective-permute-start(bf16[48,768]{1,0:T(8,128)(2,1)S(1)} %add_block.7), channel_id=1, source_target_pairs={{0,4},{1,5},{2,6},{3,7},{4,8},{5,9},{6,10},{7,11},{8,12},{9,13},{1... | collective-permute-start | bytes 221192 | tf_op jit(solution)/shard_map/ppermute | solution.py:292
  39.5 6.9 %collective-permute-start.14 = (bf16[48,768]{1,0:T(8,128)(2,1)S(1)}, bf16[48,768]{1,0:T(8,128)(2,1)S(1)}, u32[]{:S(2)}, u32[]{:S(2)}) collective-permute-start(bf16[48,768]{1,0:T(8,128)(2,1)S(1)} %add_block.6), channel_id=1, source_target_pairs={{0,8},{1,9},{2,10},{3,11},{4,12},{5,13},{6,14},{7,15},{8,0},{9,1},... | collective-permute-start | bytes 221192 | tf_op jit(solution)/shard_map/ppermute | solution.py:292
  41.0 5.3 %collective-permute-start.12 = (bf16[48,768]{1,0:T(8,128)(2,1)S(1)}, bf16[48,768]{1,0:T(8,128)(2,1)S(1)}, u32[]{:S(2)}, u32[]{:S(2)}) collective-permute-start(bf16[48,768]{1,0:T(8,128)(2,1)S(1)} %add_block.5), channel_id=1, source_target_pairs={{0,12},{1,13},{2,14},{3,15},{4,0},{5,1},{6,2},{7,3},{8,4},{9,5},{1... | collective-permute-start | bytes 221192 | tf_op jit(solution)/shard_map/ppermute | solution.py:292

commit v5 on v4

--- a/solution.py
+++ b/solution.py
@@ -149,7 +149,7 @@
         out[...] = jnp.dot(picker, stacked, preferred_element_type=F32).astype(BF16)
 
 
-def blend_kernel(plane_ref, ids_ref, gate_ref, out_ref):
+def blend_kernel(plane_ref, ids_ref, gate_ref, out_ref, wide_ref):
     slot, spread, first, second = slots_of(plane_ref[0], ids_ref)
     gate = jnp.where(first, gate_ref[0:1, :], 0) + jnp.where(second, gate_ref[1:2, :], 0)
     high = jnp.dot((gate >> 6).astype(F32).astype(BF16), spread, preferred_element_type=F32)
@@ -157,8 +157,9 @@
     for s in range(EXPERTS):
         match = matching(slot, s)
         rows = slice(s * PACK, (s + 1) * PACK)
-        out_ref[rows, 0:LANES] = jnp.where(match, high[s : s + 1, :], 0.0).astype(BF16)
-        out_ref[rows, LANES : 2 * LANES] = jnp.where(match, rest[s : s + 1, :], 0.0).astype(BF16)
+        both = [jnp.where(match, high[s : s + 1, :], 0.0), jnp.where(match, rest[s : s + 1, :], 0.0)]
+        wide_ref[rows, :] = jnp.concatenate(both, axis=1)
+    out_ref[...] = wide_ref[...].T.astype(BF16)
 
 
 def slab_kernel(order_ref, *refs):
@@ -195,18 +196,16 @@
             outs[half][at : at + rows, :] = y[q * rows : (q + 1) * rows]
 
 
-def add_pack_kernel(back_ref, keep_ref, came_ref, out_ref):
-    slab = EXPERTS * PACK
-    for q in range(2):
-        rows = slice(q * slab, (q + 1) * slab)
-        total = (keep_ref[rows, :].astype(F32) + came_ref[rows, :].astype(F32)).astype(BF16)
-        out_ref[rows, :] = jnp.dot(back_ref[...], total, preferred_element_type=F32).astype(BF16)
+def add_pack_kernel(at, back_ref, keep_ref, came_ref, out_ref):
+    rows = slice(at, at + EXPERTS * PACK)
+    total = (keep_ref[rows, :].astype(F32) + came_ref[rows, :].astype(F32)).astype(BF16)
+    out_ref[...] = jnp.dot(back_ref[...], total, preferred_element_type=F32).astype(BF16)
 
 
 def mix_kernel(hid_ref, blend_ref, m0_ref, m1_ref, m2_ref, m3_ref, out_ref):
     part = m0_ref.shape[1]
     packed = jnp.concatenate([m0_ref[...], m1_ref[...], m2_ref[...], m3_ref[...]], axis=0)
-    mixed = lax.dot_general(blend_ref[...], packed, (((0,), (0,)), ((), ())), preferred_element_type=F32)
+    mixed = jnp.dot(blend_ref[...], packed, preferred_element_type=F32)
     mixed = mixed[:LANES] * (1.0 / 64.0) + mixed[LANES:] * (1.0 / 4096.0)
     for f in range(FEAT):
         span = slice(f * part, (f + 1) * part)
@@ -281,7 +280,8 @@
     )
     blend = pl.pallas_call(
         blend_kernel,
-        out_shape=jax.ShapeDtypeStruct((EXPERTS * PACK, 2 * LANES), BF16),
+        out_shape=jax.ShapeDtypeStruct((2 * LANES, EXPERTS * PACK), BF16),
+        scratch_shapes=[pltpu.VMEM((EXPERTS * PACK, 2 * LANES), F32)],
         in_specs=[SMEM, VMEM, VMEM],
         out_specs=VMEM,
         compiler_params=params(4),
@@ -337,16 +337,16 @@
         both = (keep.astype(F32) + came.astype(F32)).astype(BF16)
         keep, came = both[: rows // 2], swapped(both[rows // 2 :], bit)
         rows, bit = rows // 2, bit * 2
-    keep = pl.pallas_call(
-        add_pack_kernel, out_shape=jax.ShapeDtypeStruct((rows, part), BF16), in_specs=[VMEM] * 3,
-        out_specs=VMEM, compiler_params=params(6), name="add_pack",
-    )(back, keep, came)
-    summed = [None] * EXPERTS
-    came = {}
-    for s in (2, 1, 3, 0):
-        came[s] = swapped(keep[rows // 2 + s * PACK : rows // 2 + (s + 1) * PACK], bit)
-    for s in (2, 1, 3, 0):
-        summed[s] = add_block(keep, came[s], s * PACK)
+
+    def add_pack(at):
+        return pl.pallas_call(
+            functools.partial(add_pack_kernel, at), out_shape=slab, in_specs=[VMEM] * 3, out_specs=VMEM,
+            compiler_params=params(6), name="add_pack",
+        )(back, keep, came)
+
+    leaving, staying = add_pack(EXPERTS * PACK), add_pack(0)
+    arrived = {s: swapped(leaving[s * PACK : (s + 1) * PACK], bit) for s in (2, 1, 3, 0)}
+    summed = [add_block(staying, arrived[s], s * PACK) for s in range(EXPERTS)]
     mine = [summed[0]] + [shifted(summed[s], -s) for s in range(1, EXPERTS)]
     return pl.pallas_call(
         mix_kernel,

time: 47.4 us -> 47.3 us (level)
  no operation moved by 1% of the time
where the time goes in v5:
time: 47.3 us; the launch traced here: 47.1 us
  starting transfers between devices  20.2 us (43%)
  Pallas kernels  13.9 us (29%)
  waiting for transfers between devices  12.8 us (27%)
    ppermute x6, starting transfers between devices, shifted(): lax.ppermute(x, 'attn', [(i, (i + s * splits) % devices) for i in range(d...  10.5 us
    ppermute x11, starting transfers between devices, swapped(): return lax.ppermute(x, 'attn', [(i, i ^ bit) for i in range(devices)])  9.71 us
    pallas_call x1, Pallas kernels, local(): pl.pallas_call(functools.partial(experts_kernel, splits), out_shape=[jax....  8.32 us
    ppermute x11, waiting for transfers between devices, swapped(): return lax.ppermute(x, 'attn', [(i, i ^ bit) for i in range(devices)])  7.72 us
    ppermute x6, waiting for transfers between devices, shifted(): lax.ppermute(x, 'attn', [(i, (i + s * splits) % devices) for i in range(d...  5.09 us
    pallas_call x1, Pallas kernels, attention(): pl.pallas_call(attention_kernel, out_shape=[jax.ShapeDtypeStruct((ROWS, w...  3.35 us
  transfers between devices with their start and end apart: 17, of which 10 were waited for; matrix products, arithmetic and copies ran while one was open for 0% of the time, Pallas kernels for 2%

profile of v5, /device:TPU:0, one launch (start us, length us, event | category | flops | bytes accessed | tf_op | source)
XLA Modules:
  0.0 47.1 jit_solution(1517662175750458124)
XLA Ops:
  0.0 3.4 %attention.1 = (bf16[16,3072]{1,0:T(8,128)(2,1)S(1)}, bf16[48,768]{1,0:T(8,128)(2,1)S(1)}, bf16[48,768]{1,0:T(8,128)(2,1)S(1)}, bf16[48,768]{1,0:T(8,128)(2,1)S(1)}, bf16[48,768]{1,0:T(8,128)(2,1)S(1)}) custom-call(s32[1]{0:T(128)} %bitcast.plane_ref, s32[16]{0:T(128)} %refs_0_.1, bf16[16,3072]{1,0:T(8,128)(2,1)} %refs_1_.1, bf16[16,3072]{1,0:T(8,128)(2,1)} %refs_2_.1, ...), custom_call_target="tpu_custom_call" | custom-call | flops 40000000000 | bytes 4000000 | tf_op jit(solution)/shard_map/attention/pallas_call | solution.py:229
  3.4 3.1 %collective-permute-start = (bf16[48,768]{1,0:T(8,128)(2,1)S(1)}, bf16[48,768]{1,0:T(8,128)(2,1)S(1)}, u32[]{:S(2)}, u32[]{:S(2)}) collective-permute-start(bf16[48,768]{1,0:T(8,128)(2,1)S(1)} %get-tuple-element.14), channel_id=1, source_target_pairs={{0,4},{1,5},{2,6},{3,7},{4,8},{5,9},{6,10},{7,11},{8,12},{9,13},{1... | collective-permute-start | bytes 221192 | tf_op jit(solution)/shard_map/ppermute | solution.py:292
  6.5 2.1 %collective-permute-start.1 = (bf16[48,768]{1,0:T(8,128)(2,1)S(1)}, bf16[48,768]{1,0:T(8,128)(2,1)S(1)}, u32[]{:S(2)}, u32[]{:S(2)}) collective-permute-start(bf16[48,768]{1,0:T(8,128)(2,1)S(1)} %get-tuple-element.15), channel_id=1, source_target_pairs={{0,12},{1,13},{2,14},{3,15},{4,0},{5,1},{6,2},{7,3},{8,4},{9,5},{1... | collective-permute-start | bytes 221192 | tf_op jit(solution)/shard_map/ppermute | solution.py:292
  8.6 1.0 %collective-permute-start.2 = (bf16[48,768]{1,0:T(8,128)(2,1)S(1)}, bf16[48,768]{1,0:T(8,128)(2,1)S(1)}, u32[]{:S(2)}, u32[]{:S(2)}) collective-permute-start(bf16[48,768]{1,0:T(8,128)(2,1)S(1)} %get-tuple-element.16), channel_id=1, source_target_pairs={{0,8},{1,9},{2,10},{3,11},{4,12},{5,13},{6,14},{7,15},{8,0},{9,1},... | collective-permute-start | bytes 221192 | tf_op jit(solution)/shard_map/ppermute | solution.py:292
  9.5 1.5 %collective-permute-start.3 = (bf16[48,768]{1,0:T(8,128)(2,1)S(1)}, bf16[48,768]{1,0:T(8,128)(2,1)S(1)}, u32[]{:S(2)}, u32[]{:S(2)}) collective-permute-start(bf16[48,768]{1,0:T(8,128)(2,1)S(1)} %get-tuple-element.13.refs_0_), channel_id=1, source_target_pairs={{0,2},{1,3},{2,0},{3,1},{4,6},{5,7},{6,4},{7,5},{8,10},{9,11},{10,... | collective-permute-start | bytes 221192 | tf_op jit(solution)/shard_map/ppermute | solution.py:295
  11.1 2.0 %collective-permute-start.4 = (bf16[48,768]{1,0:T(8,128)(2,1)S(1)}, bf16[48,768]{1,0:T(8,128)(2,1)S(1)}, u32[]{:S(2)}, u32[]{:S(2)}) collective-permute-start(bf16[48,768]{1,0:T(8,128)(2,1)S(1)} %collective-permute-done.refs_1_), channel_id=1, source_target_pairs={{0,2},{1,3},{2,0},{3,1},{4,6},{5,7},{6,4},{7,5},{8,10},{9,11},{10,... | collective-permute-start | bytes 221192 | tf_op jit(solution)/shard_map/ppermute | solution.py:295
  13.1 0.3 collective-permute-start.5
  13.3 2.2 %collective-permute-done.2.refs_3_ = bf16[48,768]{1,0:T(8,128)(2,1)S(1)} collective-permute-done((bf16[48,768]{1,0:T(8,128)(2,1)S(1)}, bf16[48,768]{1,0:T(8,128)(2,1)S(1)}, u32[]{:S(2)}, u32[]{:S(2)}) %collective-permute-start.2) | collective-permute-done | bytes 73760 | tf_op jit(solution)/shard_map/ppermute | solution.py:292
  15.5 1.5 %collective-permute-start.6 = (bf16[48,768]{1,0:T(8,128)(2,1)S(1)}, bf16[48,768]{1,0:T(8,128)(2,1)S(1)}, u32[]{:S(2)}, u32[]{:S(2)}) collective-permute-start(bf16[48,768]{1,0:T(8,128)(2,1)S(1)} %collective-permute-done.2.refs_3_), channel_id=1, source_target_pairs={{0,2},{1,3},{2,0},{3,1},{4,6},{5,7},{6,4},{7,5},{8,10},{9,11},{10,... | collective-permute-start | bytes 221192 | tf_op jit(solution)/shard_map/ppermute | solution.py:295
  17.0 0.2 slab.2.refs_0_
  17.4 2.4 %collective-permute-done.6.refs_3_ = bf16[48,768]{1,0:T(8,128)(2,1)S(1)} collective-permute-done((bf16[48,768]{1,0:T(8,128)(2,1)S(1)}, bf16[48,768]{1,0:T(8,128)(2,1)S(1)}, u32[]{:S(2)}, u32[]{:S(2)}) %collective-permute-start.6) | collective-permute-done | bytes 73760 | tf_op jit(solution)/shard_map/ppermute | solution.py:295
  19.8 0.2 slab.3.refs_1_
  20.2 1.6 %collective-permute-done.8.refs_3_ = bf16[192,768]{1,0:T(8,128)(2,1)S(1)} collective-permute-done((bf16[192,768]{1,0:T(8,128)(2,1)S(1)}, bf16[192,768]{1,0:T(8,128)(2,1)S(1)}, u32[]{:S(2)}, u32[]{:S(2)}) %collective-permute-start.8) | collective-permute-done | bytes 294944 | tf_op jit(solution)/shard_map/ppermute | solution.py:295
  21.8 8.3 %experts.1 = (bf16[384,768]{1,0:T(8,128)(2,1)S(1)}, bf16[384,768]{1,0:T(8,128)(2,1)}) custom-call(bf16[192,768]{1,0:T(8,128)(2,1)S(1)} %slab.2.refs_0_, bf16[192,768]{1,0:T(8,128)(2,1)S(1)} %slab.3.refs_1_, bf16[192,768]{1,0:T(8,128)(2,1)S(1)} %collective-permute-done.7.refs_2_, bf16[192,768]{1,0:T(8,128)(2,1)S(1)} %collective-permute-done.8.refs_3_, ...), custom_call_target="tpu_custom_call" | custom-call | flops 7247757312 | bytes 37748736 | tf_op jit(solution)/shard_map/experts/pallas_call | solution.py:321
  30.1 0.1 collective-permute-start.9
  30.2 2.1 %collective-permute-done.9.came_ref = bf16[384,768]{1,0:T(8,128)(2,1)S(1)} collective-permute-done((bf16[384,768]{1,0:T(8,128)(2,1)}, bf16[384,768]{1,0:T(8,128)(2,1)S(1)}, u32[]{:S(2)}, u32[]{:S(2)}) %collective-permute-start.9) | collective-permute-done | bytes 589856 | tf_op jit(solution)/shard_map/ppermute | solution.py:295
  32.3 0.3 add_pack.3
  32.6 1.6 %collective-permute-start.15 = (bf16[48,768]{1,0:T(8,128)(2,1)S(1)}, bf16[48,768]{1,0:T(8,128)(2,1)S(1)}, u32[]{:S(2)}, u32[]{:S(2)}) collective-permute-start(bf16[48,768]{1,0:T(8,128)(2,1)S(1)} %get-tuple-element.19), channel_id=1, source_target_pairs={{0,2},{1,3},{2,0},{3,1},{4,6},{5,7},{6,4},{7,5},{8,10},{9,11},{10,... | collective-permute-start | bytes 221192 | tf_op jit(solution)/shard_map/ppermute | solution.py:295
  34.2 0.5 %collective-permute-start.13 = (bf16[48,768]{1,0:T(8,128)(2,1)S(1)}, bf16[48,768]{1,0:T(8,128)(2,1)S(1)}, u32[]{:S(2)}, u32[]{:S(2)}) collective-permute-start(bf16[48,768]{1,0:T(8,128)(2,1)S(1)} %get-tuple-element.20), channel_id=1, source_target_pairs={{0,2},{1,3},{2,0},{3,1},{4,6},{5,7},{6,4},{7,5},{8,10},{9,11},{10,... | collective-permute-start | bytes 221192 | tf_op jit(solution)/shard_map/ppermute | solution.py:295
  34.7 1.5 %collective-permute-start.11 = (bf16[48,768]{1,0:T(8,128)(2,1)S(1)}, bf16[48,768]{1,0:T(8,128)(2,1)S(1)}, u32[]{:S(2)}, u32[]{:S(2)}) collective-permute-start(bf16[48,768]{1,0:T(8,128)(2,1)S(1)} %get-tuple-element.21), channel_id=1, source_target_pairs={{0,2},{1,3},{2,0},{3,1},{4,6},{5,7},{6,4},{7,5},{8,10},{9,11},{10,... | collective-permute-start | bytes 221192 | tf_op jit(solution)/shard_map/ppermute | solution.py:295
  36.2 0.5 %collective-permute-start.10 = (bf16[48,768]{1,0:T(8,128)(2,1)S(1)}, bf16[48,768]{1,0:T(8,128)(2,1)S(1)}, u32[]{:S(2)}, u32[]{:S(2)}) collective-permute-start(bf16[48,768]{1,0:T(8,128)(2,1)S(1)} %get-tuple-element.22), channel_id=1, source_target_pairs={{0,2},{1,3},{2,0},{3,1},{4,6},{5,7},{6,4},{7,5},{8,10},{9,11},{10,... | collective-permute-start | bytes 221192 | tf_op jit(solution)/shard_map/ppermute | solution.py:295
  36.7 0.3 add_pack.2.keep_ref
  37.0 0.5 %collective-permute-done.15.came_ref = bf16[48,768]{1,0:T(8,128)(2,1)S(1)} collective-permute-done((bf16[48,768]{1,0:T(8,128)(2,1)S(1)}, bf16[48,768]{1,0:T(8,128)(2,1)S(1)}, u32[]{:S(2)}, u32[]{:S(2)}) %collective-permute-start.15) | collective-permute-done | bytes 73760 | tf_op jit(solution)/shard_map/ppermute | solution.py:295
  37.5 1.4 %collective-permute-start.16 = (bf16[48,768]{1,0:T(8,128)(2,1)S(1)}, bf16[48,768]{1,0:T(8,128)(2,1)S(1)}, u32[]{:S(2)}, u32[]{:S(2)}) collective-permute-start(bf16[48,768]{1,0:T(8,128)(2,1)S(1)} %add_block.7), channel_id=1, source_target_pairs={{0,4},{1,5},{2,6},{3,7},{4,8},{5,9},{6,10},{7,11},{8,12},{9,13},{1... | collective-permute-start | bytes 221192 | tf_op jit(solution)/shard_map/ppermute | solution.py:292
  39.0 0.4 collective-permute-done.13.came_ref
  39.4 0.9 %collective-permute-start.14 = (bf16[48,768]{1,0:T(8,128)(2,1)S(1)}, bf16[48,768]{1,0:T(8,128)(2,1)S(1)}, u32[]{:S(2)}, u32[]{:S(2)}) collective-permute-start(bf16[48,768]{1,0:T(8,128)(2,1)S(1)} %add_block.6), channel_id=1, source_target_pairs={{0,8},{1,9},{2,10},{3,11},{4,12},{5,13},{6,14},{7,15},{8,0},{9,1},... | collective-permute-start | bytes 221192 | tf_op jit(solution)/shard_map/ppermute | solution.py:292
  40.2 0.7 %collective-permute-done.11.came_ref = bf16[48,768]{1,0:T(8,128)(2,1)S(1)} collective-permute-done((bf16[48,768]{1,0:T(8,128)(2,1)S(1)}, bf16[48,768]{1,0:T(8,128)(2,1)S(1)}, u32[]{:S(2)}, u32[]{:S(2)}) %collective-permute-start.11) | collective-permute-done | bytes 73760 | tf_op jit(solution)/shard_map/ppermute | solution.py:295
  41.0 2.1 %collective-permute-start.12 = (bf16[48,768]{1,0:T(8,128)(2,1)S(1)}, bf16[48,768]{1,0:T(8,128)(2,1)S(1)}, u32[]{:S(2)}, u32[]{:S(2)}) collective-permute-start(bf16[48,768]{1,0:T(8,128)(2,1)S(1)} %add_block.5), channel_id=1, source_target_pairs={{0,12},{1,13},{2,14},{3,15},{4,0},{5,1},{6,2},{7,3},{8,4},{9,5},{1... | collective-permute-start | bytes 221192 | tf_op jit(solution)/shard_map/ppermute | solution.py:292
  43.0 0.3 blend.1.blend_ref
  43.4 1.0 %collective-permute-done.16.m3_ref = bf16[48,768]{1,0:T(8,128)(2,1)S(1)} collective-permute-done((bf16[48,768]{1,0:T(8,128)(2,1)S(1)}, bf16[48,768]{1,0:T(8,128)(2,1)S(1)}, u32[]{:S(2)}, u32[]{:S(2)}) %collective-permute-start.16) | collective-permute-done | bytes 73760 | tf_op jit(solution)/shard_map/ppermute | solution.py:292
  44.4 1.9 %collective-permute-done.14.m2_ref = bf16[48,768]{1,0:T(8,128)(2,1)S(1)} collective-permute-done((bf16[48,768]{1,0:T(8,128)(2,1)S(1)}, bf16[48,768]{1,0:T(8,128)(2,1)S(1)}, u32[]{:S(2)}, u32[]{:S(2)}) %collective-permute-start.14) | collective-permute-done | bytes 73760 | tf_op jit(solution)/shard_map/ppermute | solution.py:292
  46.3 0.9 %mix.1 = bf16[16,3072]{1,0:T(8,128)(2,1)} custom-call(bf16[16,3072]{1,0:T(8,128)(2,1)S(1)} %get-tuple-element.12.hid_ref, bf16[128,192]{1,0:T(8,128)(2,1)S(1)} %blend.1.blend_ref, bf16[48,768]{1,0:T(8,128)(2,1)S(1)} %add_block.4.m0_ref, bf16[48,768]{1,0:T(8,128)(2,1)S(1)} %collective-permute-done.12.m1_ref, ...), custom_call_target="tpu_custom_call" | custom-call | tf_op jit(solution)/shard_map/mix/pallas_call | solution.py:351
  (27 shorter events, 0.4 us)
Async XLA Ops:
  0.0 17.0 %copy-start.3 = (bf16[192,192]{1,0:T(8,128)(2,1)S(1)}, bf16[192,192]{1,0:T(8,128)(2,1)}, u32[]{:S(2)}) copy-start(bf16[192,192]{1,0:T(8,128)(2,1)} %constant.22.clone.order_ref.back_ref) | copy-start | bytes 221188
  0.0 21.8 %copy-start = (bf16[3072,2048]{1,0:T(8,128)(2,1)S(1)}, bf16[3072,2048]{1,0:T(8,128)(2,1)}, u32[]{:S(2)}) copy-start(bf16[3072,2048]{1,0:T(8,128)(2,1)} %refs_4_.3) | copy-start | bytes 37748740
  0.0 21.8 %copy-start.1 = (bf16[3072,2048]{1,0:T(8,128)(2,1)S(1)}, bf16[3072,2048]{1,0:T(8,128)(2,1)}, u32[]{:S(2)}) copy-start(bf16[3072,2048]{1,0:T(8,128)(2,1)} %refs_5_.3) | copy-start | bytes 37748740
  0.0 21.8 %copy-start.2 = (bf16[2048,3072]{1,0:T(8,128)(2,1)S(1)}, bf16[2048,3072]{1,0:T(8,128)(2,1)}, u32[]{:S(2)}) copy-start(bf16[2048,3072]{1,0:T(8,128)(2,1)} %refs_6_.3) | copy-start | bytes 37748740
  3.4 7.7 %collective-permute-start = (bf16[48,768]{1,0:T(8,128)(2,1)S(1)}, bf16[48,768]{1,0:T(8,128)(2,1)S(1)}, u32[]{:S(2)}, u32[]{:S(2)}) collective-permute-start(bf16[48,768]{1,0:T(8,128)(2,1)S(1)} %get-tuple-element.14), channel_id=1, source_target_pairs={{0,4},{1,5},{2,6},{3,7},{4,8},{5,9},{6,10},{7,11},{8,12},{9,13},{1... | collective-permute-start | bytes 221192 | tf_op jit(solution)/shard_map/ppermute | solution.py:292
  6.5 6.6 %collective-permute-start.1 = (bf16[48,768]{1,0:T(8,128)(2,1)S(1)}, bf16[48,768]{1,0:T(8,128)(2,1)S(1)}, u32[]{:S(2)}, u32[]{:S(2)}) collective-permute-start(bf16[48,768]{1,0:T(8,128)(2,1)S(1)} %get-tuple-element.15), channel_id=1, source_target_pairs={{0,12},{1,13},{2,14},{3,15},{4,0},{5,1},{6,2},{7,3},{8,4},{9,5},{1... | collective-permute-start | bytes 221192 | tf_op jit(solution)/shard_map/ppermute | solution.py:292
  8.6 6.9 %collective-permute-start.2 = (bf16[48,768]{1,0:T(8,128)(2,1)S(1)}, bf16[48,768]{1,0:T(8,128)(2,1)S(1)}, u32[]{:S(2)}, u32[]{:S(2)}) collective-permute-start(bf16[48,768]{1,0:T(8,128)(2,1)S(1)} %get-tuple-element.16), channel_id=1, source_target_pairs={{0,8},{1,9},{2,10},{3,11},{4,12},{5,13},{6,14},{7,15},{8,0},{9,1},... | collective-permute-start | bytes 221192 | tf_op jit(solution)/shard_map/ppermute | solution.py:292
  9.5 7.8 %collective-permute-start.3 = (bf16[48,768]{1,0:T(8,128)(2,1)S(1)}, bf16[48,768]{1,0:T(8,128)(2,1)S(1)}, u32[]{:S(2)}, u32[]{:S(2)}) collective-permute-start(bf16[48,768]{1,0:T(8,128)(2,1)S(1)} %get-tuple-element.13.refs_0_), channel_id=1, source_target_pairs={{0,2},{1,3},{2,0},{3,1},{4,6},{5,7},{6,4},{7,5},{8,10},{9,11},{10,... | collective-permute-start | bytes 221192 | tf_op jit(solution)/shard_map/ppermute | solution.py:295
  11.1 6.3 %collective-permute-start.4 = (bf16[48,768]{1,0:T(8,128)(2,1)S(1)}, bf16[48,768]{1,0:T(8,128)(2,1)S(1)}, u32[]{:S(2)}, u32[]{:S(2)}) collective-permute-start(bf16[48,768]{1,0:T(8,128)(2,1)S(1)} %collective-permute-done.refs_1_), channel_id=1, source_target_pairs={{0,2},{1,3},{2,0},{3,1},{4,6},{5,7},{6,4},{7,5},{8,10},{9,11},{10,... | collective-permute-start | bytes 221192 | tf_op jit(solution)/shard_map/ppermute | solution.py:295
  13.1 4.4 %collective-permute-start.5 = (bf16[48,768]{1,0:T(8,128)(2,1)S(1)}, bf16[48,768]{1,0:T(8,128)(2,1)S(1)}, u32[]{:S(2)}, u32[]{:S(2)}) collective-permute-start(bf16[48,768]{1,0:T(8,128)(2,1)S(1)} %collective-permute-done.1.refs_2_), channel_id=1, source_target_pairs={{0,2},{1,3},{2,0},{3,1},{4,6},{5,7},{6,4},{7,5},{8,10},{9,11},{10,... | collective-permute-start | bytes 221192 | tf_op jit(solution)/shard_map/ppermute | solution.py:295
  15.5 4.4 %collective-permute-start.6 = (bf16[48,768]{1,0:T(8,128)(2,1)S(1)}, bf16[48,768]{1,0:T(8,128)(2,1)S(1)}, u32[]{:S(2)}, u32[]{:S(2)}) collective-permute-start(bf16[48,768]{1,0:T(8,128)(2,1)S(1)} %collective-permute-done.2.refs_3_), channel_id=1, source_target_pairs={{0,2},{1,3},{2,0},{3,1},{4,6},{5,7},{6,4},{7,5},{8,10},{9,11},{10,... | collective-permute-start | bytes 221192 | tf_op jit(solution)/shard_map/ppermute | solution.py:295
  17.3 2.9 %collective-permute-start.7 = (bf16[192,768]{1,0:T(8,128)(2,1)S(1)}, bf16[192,768]{1,0:T(8,128)(2,1)S(1)}, u32[]{:S(2)}, u32[]{:S(2)}) collective-permute-start(bf16[192,768]{1,0:T(8,128)(2,1)S(1)} %slab.2.refs_0_), channel_id=1, source_target_pairs={{0,1},{1,0},{2,3},{3,2},{4,5},{5,4},{6,7},{7,6},{8,9},{9,8},{10,11... | collective-permute-start | bytes 884744 | tf_op jit(solution)/shard_map/ppermute | solution.py:295
  20.1 23.0 %copy-start.4 = (s32[16,2]{0,1:T(2,128)S(1)}, s32[16,2]{0,1:T(2,128)}, u32[]{:S(2)}) copy-start(s32[16,2]{0,1:T(2,128)} %param.23) | copy-start | bytes 388
  20.1 23.0 %copy-start.5 = (s32[16,2]{0,1:T(2,128)S(1)}, s32[16,2]{0,1:T(2,128)}, u32[]{:S(2)}) copy-start(s32[16,2]{0,1:T(2,128)} %param.24) | copy-start | bytes 388
  20.1 1.6 %collective-permute-start.8 = (bf16[192,768]{1,0:T(8,128)(2,1)S(1)}, bf16[192,768]{1,0:T(8,128)(2,1)S(1)}, u32[]{:S(2)}, u32[]{:S(2)}) collective-permute-start(bf16[192,768]{1,0:T(8,128)(2,1)S(1)} %slab.3.refs_1_), channel_id=1, source_target_pairs={{0,1},{1,0},{2,3},{3,2},{4,5},{5,4},{6,7},{7,6},{8,9},{9,8},{10,11... | collective-permute-start | bytes 884744 | tf_op jit(solution)/shard_map/ppermute | solution.py:295
  30.1 2.2 %collective-permute-start.9 = (bf16[384,768]{1,0:T(8,128)(2,1)}, bf16[384,768]{1,0:T(8,128)(2,1)S(1)}, u32[]{:S(2)}, u32[]{:S(2)}) collective-permute-start(bf16[384,768]{1,0:T(8,128)(2,1)} %get-tuple-element.18), channel_id=1, source_target_pairs={{0,1},{1,0},{2,3},{3,2},{4,5},{5,4},{6,7},{7,6},{8,9},{9,8},{10,11... | collective-permute-start | bytes 1769480 | tf_op jit(solution)/shard_map/ppermute | solution.py:295
  32.6 4.9 %collective-permute-start.15 = (bf16[48,768]{1,0:T(8,128)(2,1)S(1)}, bf16[48,768]{1,0:T(8,128)(2,1)S(1)}, u32[]{:S(2)}, u32[]{:S(2)}) collective-permute-start(bf16[48,768]{1,0:T(8,128)(2,1)S(1)} %get-tuple-element.19), channel_id=1, source_target_pairs={{0,2},{1,3},{2,0},{3,1},{4,6},{5,7},{6,4},{7,5},{8,10},{9,11},{10,... | collective-permute-start | bytes 221192 | tf_op jit(solution)/shard_map/ppermute | solution.py:295
  34.2 5.2 %collective-permute-start.13 = (bf16[48,768]{1,0:T(8,128)(2,1)S(1)}, bf16[48,768]{1,0:T(8,128)(2,1)S(1)}, u32[]{:S(2)}, u32[]{:S(2)}) collective-permute-start(bf16[48,768]{1,0:T(8,128)(2,1)S(1)} %get-tuple-element.20), channel_id=1, source_target_pairs={{0,2},{1,3},{2,0},{3,1},{4,6},{5,7},{6,4},{7,5},{8,10},{9,11},{10,... | collective-permute-start | bytes 221192 | tf_op jit(solution)/shard_map/ppermute | solution.py:295
  34.7 6.2 %collective-permute-start.11 = (bf16[48,768]{1,0:T(8,128)(2,1)S(1)}, bf16[48,768]{1,0:T(8,128)(2,1)S(1)}, u32[]{:S(2)}, u32[]{:S(2)}) collective-permute-start(bf16[48,768]{1,0:T(8,128)(2,1)S(1)} %get-tuple-element.21), channel_id=1, source_target_pairs={{0,2},{1,3},{2,0},{3,1},{4,6},{5,7},{6,4},{7,5},{8,10},{9,11},{10,... | collective-permute-start | bytes 221192 | tf_op jit(solution)/shard_map/ppermute | solution.py:295
  36.2 7.1 %collective-permute-start.10 = (bf16[48,768]{1,0:T(8,128)(2,1)S(1)}, bf16[48,768]{1,0:T(8,128)(2,1)S(1)}, u32[]{:S(2)}, u32[]{:S(2)}) collective-permute-start(bf16[48,768]{1,0:T(8,128)(2,1)S(1)} %get-tuple-element.22), channel_id=1, source_target_pairs={{0,2},{1,3},{2,0},{3,1},{4,6},{5,7},{6,4},{7,5},{8,10},{9,11},{10,... | collective-permute-start | bytes 221192 | tf_op jit(solution)/shard_map/ppermute | solution.py:295
  37.5 6.9 %collective-permute-start.16 = (bf16[48,768]{1,0:T(8,128)(2,1)S(1)}, bf16[48,768]{1,0:T(8,128)(2,1)S(1)}, u32[]{:S(2)}, u32[]{:S(2)}) collective-permute-start(bf16[48,768]{1,0:T(8,128)(2,1)S(1)} %add_block.7), channel_id=1, source_target_pairs={{0,4},{1,5},{2,6},{3,7},{4,8},{5,9},{6,10},{7,11},{8,12},{9,13},{1... | collective-permute-start | bytes 221192 | tf_op jit(solution)/shard_map/ppermute | solution.py:292
  39.4 6.9 %collective-permute-start.14 = (bf16[48,768]{1,0:T(8,128)(2,1)S(1)}, bf16[48,768]{1,0:T(8,128)(2,1)S(1)}, u32[]{:S(2)}, u32[]{:S(2)}) collective-permute-start(bf16[48,768]{1,0:T(8,128)(2,1)S(1)} %add_block.6), channel_id=1, source_target_pairs={{0,8},{1,9},{2,10},{3,11},{4,12},{5,13},{6,14},{7,15},{8,0},{9,1},... | collective-permute-start | bytes 221192 | tf_op jit(solution)/shard_map/ppermute | solution.py:292
  41.0 5.3 %collective-permute-start.12 = (bf16[48,768]{1,0:T(8,128)(2,1)S(1)}, bf16[48,768]{1,0:T(8,128)(2,1)S(1)}, u32[]{:S(2)}, u32[]{:S(2)}) collective-permute-start(bf16[48,768]{1,0:T(8,128)(2,1)S(1)} %add_block.5), channel_id=1, source_target_pairs={{0,12},{1,13},{2,14},{3,15},{4,0},{5,1},{6,2},{7,3},{8,4},{9,5},{1... | collective-permute-start | bytes 221192 | tf_op jit(solution)/shard_map/ppermute | solution.py:292
